TPU v7x, 256 devices: a whole 4x4x8 slice. The times are simulated.
256 devices in a mesh: dp: 64 (over z, y, core), seq: 4 (over x).
Axes of the slice: x: 4, y: 4, z: 8, core: 2. Of those that a mesh axis runs over, the one named last changes fastest.
Arguments:
- resid_in: bfloat16 [64, 2048, 512], P('dp', 'seq'), may hold values from -16 to 16
- conv_weight: bfloat16 [2, 1024, 1024], replicated, may hold values from -0.1875 to 0.1875
- out_weight: bfloat16 [2, 512, 1024], replicated, may hold values from -0.25 to 0.25
- resid_cot: bfloat16 [64, 2048, 512], P('dp', 'seq'), may hold values from -6 to 6
- skip_cot: bfloat16 [64, 2048, 512], P('dp', 'seq'), may hold values from -6 to 6
Outputs:
- conv_grad: float32 [2, 1024, 1024], P(None, 'dp')
- out_grad: float32 [2, 512, 1024], P(None, 'dp')
- resid_grad: bfloat16 [64, 2048, 512], P('dp', 'seq')
- skip_sum: bfloat16 [64, 2048, 512], P('dp', 'seq')
All inputs are finite; a program needn't handle non-finite values.
Results may differ from a plain program's by a relative error of at most 0.014.
Values may be sent and summed in bfloat16 or wider, within the bound.
No kernel may reach another device: no remote copies, remote signals or barrier semaphores. Data moves between devices by JAX's collectives and lax.ppermute only.
A program may use at most 128 MiB of HBM per device.

v0:
```python
import functools

import jax
import jax.numpy as jnp
from jax import lax
from jax.experimental import pallas as pl
from jax.experimental.pallas import tpu as pltpu
from jax.sharding import Mesh, PartitionSpec as P

F32, BF16 = jnp.float32, jnp.bfloat16
Z, Y, CORES, X = 8, 4, 2, 4
D0, D1 = 128, 256
ROWS, CH = 512, 512
HALO = D0 + D1
TILE = 256
VMEM_LIMIT = 56 * 1024 * 1024

FIRST, SECOND = (1, 0, 3, 2), (3, 2, 1, 0)
BIT_A, BIT_B = (0, 1, 1, 0), (0, 0, 1, 1)
Z_PAIRS = ((1, 0, 3, 2, 5, 4, 7, 6), (7, 2, 1, 4, 3, 6, 5, 0), (3, 6, 5, 0, 7, 2, 1, 4))
Z_ORDER = (0, 3, 7, 4, 1, 6, 2, 5)


def ring_place(i, half):
    a, b = BIT_A[i], BIT_B[i]
    return 2 * a + b if half == 0 else 2 * b + a


def dot(a, b):
    return jnp.dot(a, b, preferred_element_type=F32)


def dot_cols(a, b):
    return lax.dot_general(a, b, (((1,), (1,)), ((), ())), preferred_element_type=F32)


def dot_rows(a, b):
    return lax.dot_general(a, b, (((0,), (0,)), ((), ())), preferred_element_type=F32)


def gates(pre):
    return jnp.tanh(pre[:, :CH]), 0.5 * jnp.tanh(0.5 * pre[:, CH:]) + 0.5


def forward_kernel(
    ext, cw, ow, rc, sc,
    early, flow, pre1, stream1, gated0, gated1, slope_f, slope_g, skip,
    skip_acc,
):
    for r in range(0, ROWS + D1, TILE):
        now = ext[D0 + r : D0 + r + TILE, :]
        pre = dot(ext[r : r + TILE, :], cw[0, :CH, :]) + dot(now, cw[0, CH:, :])
        f, g = gates(pre)
        gated = (f * g).astype(BF16)
        stream1[r : r + TILE, :] = (now.astype(F32) + dot(gated, ow[0, :, :CH])).astype(BF16)
        if r >= D1:
            at = slice(r - D1, r - D1 + TILE)
            gated0[at, :] = gated
            slope_f[at, :] = (1.0 - f * f) * g
            slope_g[at, :] = f * g * (1.0 - g)
            skip_acc[at, :] = dot(gated, ow[0, :, CH:])
    for r in range(0, ROWS, TILE):
        at = slice(r, r + TILE)
        pre = dot(stream1[at, :], cw[1, :CH, :]) + dot(stream1[r + D1 : r + D1 + TILE, :], cw[1, CH:, :])
        f, g = gates(pre)
        gated = (f * g).astype(BF16)
        gated1[at, :] = gated
        skip[at, :] = (skip_acc[at, :] + dot(gated, ow[1, :, CH:])).astype(BF16)
        gc = dot_cols(rc[at, :], ow[1, :, :CH]) + dot_cols(sc[at, :], ow[1, :, CH:])
        pre1[at, :CH] = (gc * ((1.0 - f * f) * g)).astype(BF16)
        pre1[at, CH:] = (gc * (f * g * (1.0 - g))).astype(BF16)
        pc = pre1[at, :]
        flow[at, :] = rc[at, :].astype(F32) + dot_cols(pc, cw[1, CH:, :])
        ahead = dot_cols(pc, cw[1, :CH, :])
        if r < D1:
            early[at, :] = ahead.astype(BF16)
        else:
            flow[r - D1 : r - D1 + TILE, :] += ahead


def backward_kernel(flow1, returned, slope_f, slope_g, sc, ow, cw, proj, pre0, flow, early):
    for r in range(0, ROWS, TILE):
        at = slice(r, r + TILE)
        fl = flow1[at, :]
        if r + TILE > ROWS - D1:
            fl = fl + returned[r - (ROWS - D1) : r - (ROWS - D1) + TILE, :].astype(F32)
        flow_b = fl.astype(BF16)
        proj[at, :] = flow_b
        gc = dot_cols(flow_b, ow[0, :, :CH]) + dot_cols(sc[at, :], ow[0, :, CH:])
        pre0[at, :CH] = (gc * slope_f[at, :]).astype(BF16)
        pre0[at, CH:] = (gc * slope_g[at, :]).astype(BF16)
        pc = pre0[at, :]
        flow[at, :] = fl + dot_cols(pc, cw[0, CH:, :])
        ahead = dot_cols(pc, cw[0, :CH, :])
        if r == 0:
            early[...] = ahead[:D0, :].astype(BF16)
            flow[: TILE - D0, :] += ahead[D0:, :]
        else:
            flow[r - D0 : r - D0 + TILE, :] += ahead


def gradient_kernel(layer, core, stream, gated, pre, left, right, mine, other):
    delay = D0 if layer == 0 else D1
    odd = jnp.full((16, 128), core[0], jnp.int32) == 1
    odd_8 = jnp.full((8, 128), core[0], jnp.int32) == 1

    def place(half, y, block):
        return (half, block, ring_place(y, 0)) if layer == 1 else (half, ring_place(y, half), block)

    for n in range(4):
        half = n // 2
        cot = pre[:, n * 256 : (n + 1) * 256]
        for m in range(4):
            start = 0 if m < 2 else delay
            lhs = stream[start : start + ROWS, (m % 2) * 256 : (m % 2) * 256 + 256]
            g = dot_rows(lhs, cot)
            for dz in range(2):
                unit, t = divmod(Z_ORDER.index(m * 2 + dz), 2)
                for y in range(Y):
                    row = dz * 128 + y * 32
                    for b in range(2):
                        at = place(half, y, 2 * (n % 2) + b) + (unit, slice(t * 16, t * 16 + 16))
                        even = g[row : row + 16, b * 128 : b * 128 + 128]
                        uneven = g[row + 16 : row + 32, b * 128 : b * 128 + 128]
                        mine[at] = jnp.where(odd, uneven, even).astype(BF16)
                        other[at] = jnp.where(odd, even, uneven).astype(BF16)
        side = left if n < 2 else right
        g = dot_rows(gated[...], side[:, (n % 2) * 256 : (n % 2) * 256 + 256])
        for unit in range(4):
            for y in range(Y):
                for b in range(2):
                    at = place(half, y, 2 * (n % 2) + b) + (unit, slice(32, 48))
                    mine_parts, other_parts = [], []
                    for t in range(2):
                        row = Z_ORDER[unit * 2 + t] * 64 + y * 16
                        even = g[row : row + 8, b * 128 : b * 128 + 128]
                        uneven = g[row + 8 : row + 16, b * 128 : b * 128 + 128]
                        mine_parts.append(jnp.where(odd_8, uneven, even))
                        other_parts.append(jnp.where(odd_8, even, uneven))
                    mine[at] = jnp.concatenate(mine_parts, axis=0).astype(BF16)
                    other[at] = jnp.concatenate(other_parts, axis=0).astype(BF16)


def kernel_call(kernel, shapes, args, flops, moved, scratch=(), smem=0):
    vmem = pl.BlockSpec(memory_space=pltpu.VMEM)
    return pl.pallas_call(
        kernel,
        out_shape=[jax.ShapeDtypeStruct(s, t) for s, t in shapes],
        in_specs=[pl.BlockSpec(memory_space=pltpu.SMEM)] * smem + [vmem] * (len(args) - smem),
        out_specs=[vmem] * len(shapes),
        scratch_shapes=scratch,
        compiler_params=pltpu.CompilerParams(vmem_limit_bytes=VMEM_LIMIT),
        cost_estimate=pl.CostEstimate(flops=flops, bytes_accessed=moved, transcendentals=0),
    )(*args)


def table(values, i):
    return jnp.asarray(values, jnp.int32)[i]


def halve(parts, axis, pairs, bit):
    kept = lax.dynamic_index_in_dim(parts, bit, 0, False)
    sent = lax.dynamic_index_in_dim(parts, 1 - bit, 0, False)
    got = lax.ppermute(sent, axis, list(enumerate(pairs)))
    return (kept.astype(F32) + got.astype(F32)).astype(BF16)


def core_sum(mine, other):
    got = lax.ppermute(other, "c", [(0, 1), (1, 0)])
    return (mine.astype(F32) + got.astype(F32)).astype(BF16)


def ring_first(s, axis, bit_a, bit_b):
    rest = s.shape[2:]
    one = halve(s[0].reshape((2, 2) + rest), axis, FIRST, bit_a)
    two = halve(s[1].reshape((2, 2) + rest), axis, SECOND, bit_b)
    one = halve(one, axis, SECOND, bit_b)
    two = halve(two, axis, FIRST, bit_a)
    return one, two


def ring_last(one, two, axis, bit_a, bit_b):
    s = jnp.stack([one, two], axis=1)
    s = s.reshape((2, 2) + s.shape[1:])
    s = halve(s, axis, FIRST, bit_a)
    return halve(s, axis, SECOND, bit_b)


def along(value, steps):
    initial, last = (max(0, -steps), min(X, X - steps))
    return lax.ppermute(value, "x", [(s, s + steps) for s in range(initial, last)])


def on_device(resid_in, conv_weight, out_weight, resid_cot, skip_cot):
    x0, rc, sc = resid_in[0], resid_cot[0], skip_cot[0]
    core = lax.axis_index("c").astype(jnp.int32)[None]
    xi, yi, zi = (lax.axis_index(a) for a in ("x", "y", "z"))
    xa, xb, ya, yb = table(BIT_A, xi), table(BIT_B, xi), table(BIT_A, yi), table(BIT_B, yi)
    ext = jnp.concatenate([along(x0[ROWS - HALO :], 1), x0])
    early1, flow1, pre1, stream1, gated0, gated1, slope_f, slope_g, skip = kernel_call(
        forward_kernel,
        [((D1, CH), BF16), ((ROWS, CH), F32), ((ROWS, 2 * CH), BF16), ((ROWS + D1, CH), BF16)]
        + [((ROWS, CH), BF16)] * 2
        + [((ROWS, CH), F32)] * 2
        + [((ROWS, CH), BF16)],
        (ext, conv_weight, out_weight, rc, sc),
        6 * 10**9,
        10**7,
        [pltpu.VMEM((ROWS, CH), F32)],
    )
    returned1 = along(early1, -1)
    pieces = (2, 4, 4, 4, 48, 128)
    shapes = [(pieces, BF16)] * 2
    mine1, other1 = kernel_call(
        functools.partial(gradient_kernel, 1), shapes, (core, stream1, gated1, pre1, rc, sc), 16 * 10**8, 6 * 10**6, smem=1
    )
    proj0, pre0, flow0, early0 = kernel_call(
        backward_kernel,
        [((ROWS, CH), BF16), ((ROWS, 2 * CH), BF16), ((ROWS, CH), F32), ((D0, CH), BF16)],
        (flow1, returned1, slope_f, slope_g, sc, out_weight, conv_weight),
        16 * 10**8,
        6 * 10**6,
    )
    returned0 = along(early0, -1)
    mine0, other0 = kernel_call(
        functools.partial(gradient_kernel, 0),
        shapes,
        (core, ext[D1:], gated0, pre0, proj0, sc),
        16 * 10**8,
        6 * 10**6,
        smem=1,
    )
    resid = jnp.concatenate([flow0[: ROWS - D0], flow0[ROWS - D0 :] + returned0.astype(F32)]).astype(BF16)

    s1 = core_sum(mine1, other1)
    s0 = core_sum(mine0, other0)
    one1, two1 = ring_first(s1, "x", xa, xb)
    one0, two0 = ring_first(s0, "y", ya, yb)
    s1 = ring_last(one1, two1, "y", ya, yb)
    s0 = ring_last(one0, two0, "x", xa, xb)
    s = jnp.stack([s1, s0]).transpose(2, 0, 1, 3, 4)
    place = table([Z_ORDER.index(i) for i in range(Z)], zi)
    s = halve(s.reshape((2, 2) + s.shape[1:]), "z", Z_PAIRS[0], place // 4)
    s = halve(s, "z", Z_PAIRS[1], (place // 2) % 2)
    conv, out = s[:, :, :32].reshape(2, 2, 2, 16, 128), s[:, :, 32:].reshape(2, 2, 2, 8, 128)
    s = halve(jnp.concatenate([conv, out], axis=3).transpose(2, 0, 1, 3, 4), "z", Z_PAIRS[2], place % 2)
    parts = [s] + [lax.ppermute(s, "x", [(i, (i + k) % X) for i in range(X)]) for k in range(1, X)]
    whole = jnp.stack(parts)
    layer_rows = []
    for slot, layer in ((0, 1), (1, 0)):
        halves = []
        for half in range(2):
            source = [[ring_place(i, half if layer == 1 else 0) for i in range(X)].index(b) for b in range(X)]
            picks = lax.rem(xi - jnp.asarray(source) + X, X)
            halves.append(whole[picks, slot, half].transpose(1, 0, 2).reshape(24, 512))
        layer_rows.append(jnp.concatenate(halves, axis=1).astype(F32))
    conv_grad = jnp.stack([layer_rows[1][:16], layer_rows[0][:16]])
    out_grad = jnp.stack([layer_rows[1][16:], layer_rows[0][16:]])
    return conv_grad, out_grad, resid[None], skip[None]


def solution(mesh):
    fine = Mesh(mesh.devices.reshape(Z, Y, CORES, X), ("z", "y", "c", "x"))
    dp = ("z", "y", "c")
    return jax.shard_map(
        on_device,
        mesh=fine,
        in_specs=(P(dp, "x", None), P(), P(), P(dp, "x", None), P(dp, "x", None)),
        out_specs=(P(None, dp, None), P(None, dp, None), P(dp, "x", None), P(dp, "x", None)),
        check_vma=False,
    )
```

profile of v0, /device:TPU:8, one launch (start us, length us, event | category | flops | bytes accessed | tf_op | source)
XLA Modules:
  0.0 146.9 jit_solution(841572718847902674)
XLA Ops:
  1.7 3.4 %collective-permute-start = (bf16[384,512]{1,0:T(8,128)(2,1)S(1)}, bf16[384,512]{1,0:T(8,128)(2,1)S(1)}, u32[]{:S(2)}, u32[]{:S(2)}) collective-permute-start(bf16[384,512]{1,0:T(8,128)(2,1)S(1)} %slice_bitcast_fusion), channel_id=1, source_target_pairs={{0,1},{1,2},{2,3},{4,5},{5,6},{6,7},{8,9},{9,10},{10,11},{12,13},{... | collective-permute-start | bytes 1179656 | tf_op jit(solution)/shard_map/ppermute | solution.py:191
  5.1 8.3 %collective-permute-done = bf16[384,512]{1,0:T(8,128)(2,1)S(1)} collective-permute-done((bf16[384,512]{1,0:T(8,128)(2,1)S(1)}, bf16[384,512]{1,0:T(8,128)(2,1)S(1)}, u32[]{:S(2)}, u32[]{:S(2)}) %collective-permute-start) | collective-permute-done | bytes 393248 | tf_op jit(solution)/shard_map/ppermute | solution.py:191
  13.4 2.0 %pad_maximum_fusion.ext = bf16[896,512]{1,0:T(8,128)(2,1)} fusion(bf16[384,512]{1,0:T(8,128)(2,1)S(1)} %collective-permute-done, bf16[512,512]{1,0:T(8,128)(2,1)} %bitcast.163), kind=kLoop, calls=%fused_computation.7 | loop fusion | flops 1835008 | bytes 1835008 | tf_op jit(solution)/shard_map/concatenate | solution.py:199
  15.5 11.0 %shard_map.165 = (bf16[256,512]{1,0:T(8,128)(2,1)}, f32[512,512]{1,0:T(8,128)}, bf16[512,1024]{1,0:T(8,128)(2,1)}, bf16[768,512]{1,0:T(8,128)(2,1)}, bf16[512,51...) custom-call(bf16[896,512]{1,0:T(8,128)(2,1)} %pad_maximum_fusion.ext, ...), custom_call_target="tpu_custom_call" | custom-call | flops 6000000000 | bytes 10000000 | tf_op jit(solution)/shard_map/pallas_call | solution.py:146
  26.5 5.5 %shard_map.166 = (bf16[2,4,4,4,48,128]{5,4,3,2,1,0:T(8,128)(2,1)}, bf16[2,4,4,4,48,128]{5,4,3,2,1,0:T(8,128)(2,1)}) custom-call(s32[1]{0:T(128)} %bitcast.core, bf16[768,512]{1,0:T(8,128)(2,1)} %get-tuple-element.21.stream, bf16[512,512]{1,0:T(8,128)(2,1)} %get-tuple-element.22.gated, bf16[512,1024]{1,0:T(8,128)(2,1)} %get-tuple-element.23.pre, ...), custom_call_target="tpu_custom_call" | custom-call | flops 1600000000 | bytes 6000000 | tf_op jit(solution)/shard_map/pallas_call | solution.py:146
  34.2 9.1 %collective-permute-done.8.returned = bf16[256,512]{1,0:T(8,128)(2,1)S(1)} collective-permute-done((bf16[256,512]{1,0:T(8,128)(2,1)S(1)}, bf16[256,512]{1,0:T(8,128)(2,1)S(1)}, u32[]{:S(2)}, u32[]{:S(2)}) %collective-permute-start.8) | collective-permute-done | bytes 262176 | tf_op jit(solution)/shard_map/ppermute | solution.py:191
  44.0 7.1 %shard_map.167 = (bf16[512,512]{1,0:T(8,128)(2,1)}, bf16[512,1024]{1,0:T(8,128)(2,1)}, f32[512,512]{1,0:T(8,128)}, bf16[128,512]{1,0:T(8,128)(2,1)}) custom-call(f32[512,512]{1,0:T(8,128)} %get-tuple-element.27.flow1, bf16[256,512]{1,0:T(8,128)(2,1)} %copy-done.4, f32[512,512]{1,0:T(8,128)} %get-tuple-element.29.slope_f, ...), custom_call_target="tpu_custom_call" | custom-call | flops 1600000000 | bytes 6000000 | tf_op jit(solution)/shard_map/pallas_call | solution.py:146
  51.1 5.5 %shard_map.168 = (bf16[2,4,4,4,48,128]{5,4,3,2,1,0:T(8,128)(2,1)}, bf16[2,4,4,4,48,128]{5,4,3,2,1,0:T(8,128)(2,1)}) custom-call(s32[1]{0:T(128)} %bitcast.core, bf16[640,512]{1,0:T(8,128)(2,1)} %fusion.4.stream, bf16[512,512]{1,0:T(8,128)(2,1)} %get-tuple-element.26.gated, bf16[512,1024]{1,0:T(8,128)(2,1)} %get-tuple-element.31.pre, ...), custom_call_target="tpu_custom_call" | custom-call | flops 1600000000 | bytes 6000000 | tf_op jit(solution)/shard_map/pallas_call | solution.py:146
  75.8 2.2 %collective-permute-start.4 = (bf16[2,4,4,48,128]{4,3,2,1,0:T(8,128)(2,1)S(1)}, bf16[2,4,4,48,128]{4,3,2,1,0:T(8,128)(2,1)S(1)}, u32[]{:S(2)}, u32[]{:S(2)}) collective-permute-start(bf16[2,4,4,48,128]{4,3,2,1,0:T(8,128)(2,1)S(1)} %dynamic-slice_bitcast_fusion.2), channel_id=1, source_target_pairs={{0,3},{1,2},{2,1},{3,0},{4,7},{5,6},{6,5},{7,4},{8,11},{9,10},{10,... | collective-permute-start | bytes 1179656 | tf_op jit(solution)/shard_map/ppermute | solution.py:164
  80.7 2.5 %collective-permute-start.12 = (bf16[2,4,4,48,128]{4,3,2,1,0:T(8,128)(2,1)S(1)}, bf16[2,4,4,48,128]{4,3,2,1,0:T(8,128)(2,1)S(1)}, u32[]{:S(2)}, u32[]{:S(2)}) collective-permute-start(bf16[2,4,4,48,128]{4,3,2,1,0:T(8,128)(2,1)S(1)} %dynamic-slice_bitcast_fusion), channel_id=1, source_target_pairs={{0,24},{8,16},{16,8},{24,0},{1,25},{9,17},{17,9},{25,1},{2,26},{10... | collective-permute-start | bytes 1179656 | tf_op jit(solution)/shard_map/ppermute | solution.py:164
  83.2 2.4 %collective-permute-done.2 = bf16[2,4,4,48,128]{4,3,2,1,0:T(8,128)(2,1)S(1)} collective-permute-done((bf16[2,4,4,48,128]{4,3,2,1,0:T(8,128)(2,1)S(1)}, bf16[2,4,4,48,128]{4,3,2,1,0:T(8,128)(2,1)S(1)}, u32[]{:S(2)}, u32[]{:S(2)}) %collective-permute-start.2) | collective-permute-done | bytes 393248 | tf_op jit(solution)/shard_map/ppermute | solution.py:164
  85.7 2.2 %collective-permute-start.3 = (bf16[4,4,48,128]{3,2,1,0:T(8,128)(2,1)S(1)}, bf16[4,4,48,128]{3,2,1,0:T(8,128)(2,1)S(1)}, u32[]{:S(2)}, u32[]{:S(2)}) collective-permute-start(bf16[4,4,48,128]{3,2,1,0:T(8,128)(2,1)S(1)} %dynamic-slice_bitcast_fusion.7), channel_id=1, source_target_pairs={{0,3},{1,2},{2,1},{3,0},{4,7},{5,6},{6,5},{7,4},{8,11},{9,10},{10,... | collective-permute-start | bytes 589832 | tf_op jit(solution)/shard_map/ppermute | solution.py:164
  89.2 4.3 %collective-permute-done.3 = bf16[4,4,48,128]{3,2,1,0:T(8,128)(2,1)S(1)} collective-permute-done((bf16[4,4,48,128]{3,2,1,0:T(8,128)(2,1)S(1)}, bf16[4,4,48,128]{3,2,1,0:T(8,128)(2,1)S(1)}, u32[]{:S(2)}, u32[]{:S(2)}) %collective-permute-start.3) | collective-permute-done | bytes 196640 | tf_op jit(solution)/shard_map/ppermute | solution.py:164
  95.5 2.5 %collective-permute-start.11 = (bf16[4,4,48,128]{3,2,1,0:T(8,128)(2,1)S(1)}, bf16[4,4,48,128]{3,2,1,0:T(8,128)(2,1)S(1)}, u32[]{:S(2)}, u32[]{:S(2)}) collective-permute-start(bf16[4,4,48,128]{3,2,1,0:T(8,128)(2,1)S(1)} %dynamic-slice_bitcast_fusion.5), channel_id=1, source_target_pairs={{0,24},{8,16},{16,8},{24,0},{1,25},{9,17},{17,9},{25,1},{2,26},{10... | collective-permute-start | bytes 589832 | tf_op jit(solution)/shard_map/ppermute | solution.py:164
  99.6 2.1 %collective-permute-done.11 = bf16[4,4,48,128]{3,2,1,0:T(8,128)(2,1)S(1)} collective-permute-done((bf16[4,4,48,128]{3,2,1,0:T(8,128)(2,1)S(1)}, bf16[4,4,48,128]{3,2,1,0:T(8,128)(2,1)S(1)}, u32[]{:S(2)}, u32[]{:S(2)}) %collective-permute-start.11) | collective-permute-done | bytes 196640 | tf_op jit(solution)/shard_map/ppermute | solution.py:164
  101.7 3.1 %collective-permute-done.13 = bf16[4,4,48,128]{3,2,1,0:T(8,128)(2,1)S(1)} collective-permute-done((bf16[4,4,48,128]{3,2,1,0:T(8,128)(2,1)S(1)}, bf16[4,4,48,128]{3,2,1,0:T(8,128)(2,1)S(1)}, u32[]{:S(2)}, u32[]{:S(2)}) %collective-permute-start.13) | collective-permute-done | bytes 196640 | tf_op jit(solution)/shard_map/ppermute | solution.py:164
  107.2 3.5 %collective-permute-done.14 = bf16[2,2,4,48,128]{4,3,1,2,0:T(8,128)(2,1)S(1)} collective-permute-done((bf16[2,2,4,48,128]{4,3,1,2,0:T(8,128)(2,1)S(1)}, bf16[2,2,4,48,128]{4,3,1,2,0:T(8,128)(2,1)S(1)}, u32[]{:S(2)}, u32[]{:S(2)}) %collective-permute-start.14) | collective-permute-done | bytes 196640 | tf_op jit(solution)/shard_map/ppermute | solution.py:164
  110.8 2.2 %collective-permute-start.15 = (bf16[2,4,48,128]{3,2,0,1:T(8,128)(2,1)S(1)}, bf16[2,4,48,128]{3,2,0,1:T(8,128)(2,1)S(1)}, u32[]{:S(2)}, u32[]{:S(2)}) collective-permute-start(bf16[2,4,48,128]{3,2,0,1:T(8,128)(2,1)S(1)} %dynamic-slice_bitcast_fusion.9), channel_id=1, source_target_pairs={{0,3},{1,2},{2,1},{3,0},{4,7},{5,6},{6,5},{7,4},{8,11},{9,10},{10,... | collective-permute-start | bytes 294920 | tf_op jit(solution)/shard_map/ppermute | solution.py:164
  113.0 3.7 %collective-permute-done.15 = bf16[2,4,48,128]{3,2,0,1:T(8,128)(2,1)S(1)} collective-permute-done((bf16[2,4,48,128]{3,2,0,1:T(8,128)(2,1)S(1)}, bf16[2,4,48,128]{3,2,0,1:T(8,128)(2,1)S(1)}, u32[]{:S(2)}, u32[]{:S(2)}) %collective-permute-start.15) | collective-permute-done | bytes 98336 | tf_op jit(solution)/shard_map/ppermute | solution.py:164
  121.5 6.0 %collective-permute-start.17 = (bf16[2,2,48,128]{3,2,1,0:T(8,128)(2,1)S(1)}, bf16[2,2,48,128]{3,2,1,0:T(8,128)(2,1)S(1)}, u32[]{:S(2)}, u32[]{:S(2)}) collective-permute-start(bf16[2,2,48,128]{3,2,1,0:T(8,128)(2,1)S(1)} %dynamic-slice_bitcast_fusion.11), channel_id=1, source_target_pairs={{0,224},{32,64},{64,32},{96,128},{128,96},{160,192},{192,160},{224... | collective-permute-start | bytes 147464 | tf_op jit(solution)/shard_map/ppermute | solution.py:164
  129.6 2.1 %collective-permute-start.18 = (bf16[2,2,24,128]{3,2,1,0:T(8,128)(2,1)S(1)}, bf16[2,2,24,128]{3,2,1,0:T(8,128)(2,1)S(1)}, u32[]{:S(2)}, u32[]{:S(2)}) collective-permute-start(bf16[2,2,24,128]{3,2,1,0:T(8,128)(2,1)S(1)} %fusion.29), channel_id=1, source_target_pairs={{0,96},{32,192},{64,160},{96,0},{128,224},{160,64},{192,32},{224,1... | collective-permute-start | bytes 73736 | tf_op jit(solution)/shard_map/ppermute | solution.py:164
  131.7 3.9 %collective-permute-done.18 = bf16[2,2,24,128]{3,2,1,0:T(8,128)(2,1)S(1)} collective-permute-done((bf16[2,2,24,128]{3,2,1,0:T(8,128)(2,1)S(1)}, bf16[2,2,24,128]{3,2,1,0:T(8,128)(2,1)S(1)}, u32[]{:S(2)}, u32[]{:S(2)}) %collective-permute-start.18) | collective-permute-done | bytes 24608 | tf_op jit(solution)/shard_map/ppermute | solution.py:164
  135.6 2.2 %collective-permute-start.21 = (bf16[2,2,24,128]{3,2,1,0:T(8,128)(2,1)S(1)}, bf16[2,2,24,128]{3,2,1,0:T(8,128)(2,1)S(1)}, u32[]{:S(2)}, u32[]{:S(2)}) collective-permute-start(bf16[2,2,24,128]{3,2,1,0:T(8,128)(2,1)S(1)} %fusion.27), channel_id=1, source_target_pairs={{0,3},{1,0},{2,1},{3,2},{4,7},{5,4},{6,5},{7,6},{8,11},{9,8},{10,9... | collective-permute-start | bytes 73736 | tf_op jit(solution)/shard_map/ppermute | solution.py:247
  139.6 3.6 %collective-permute-done.20 = bf16[2,2,24,128]{3,2,1,0:T(8,128)(2,1)S(1)} collective-permute-done((bf16[2,2,24,128]{3,2,1,0:T(8,128)(2,1)S(1)}, bf16[2,2,24,128]{3,2,1,0:T(8,128)(2,1)S(1)}, u32[]{:S(2)}, u32[]{:S(2)}) %collective-permute-start.20) | collective-permute-done | bytes 24608 | tf_op jit(solution)/shard_map/ppermute | solution.py:247
  (115 shorter events, 30.4 us)
Async XLA Ops:
  1.7 11.8 %collective-permute-start = (bf16[384,512]{1,0:T(8,128)(2,1)S(1)}, bf16[384,512]{1,0:T(8,128)(2,1)S(1)}, u32[]{:S(2)}, u32[]{:S(2)}) collective-permute-start(bf16[384,512]{1,0:T(8,128)(2,1)S(1)} %slice_bitcast_fusion), channel_id=1, source_target_pairs={{0,1},{1,2},{2,3},{4,5},{5,6},{6,7},{8,9},{9,10},{10,11},{12,13},{... | collective-permute-start | bytes 1179656 | tf_op jit(solution)/shard_map/ppermute | solution.py:191
  32.0 41.2 %collective-permute-start.1 = (bf16[2,4,4,4,48,128]{5,4,3,2,1,0:T(8,128)(2,1)}, bf16[2,4,4,4,48,128]{5,4,3,2,1,0:T(8,128)(2,1)S(1)}, u32[]{:S(2)}, u32[]{:S(2)}) collective-permute-start(bf16[2,4,4,4,48,128]{5,4,3,2,1,0:T(8,128)(2,1)} %get-tuple-element.25), channel_id=1, source_target_pairs={{0,4},{4,0},{1,5},{5,1},{2,6},{6,2},{3,7},{7,3},{8,12},{12,8},{9,1... | collective-permute-start | bytes 4718600 | tf_op jit(solution)/shard_map/ppermute | solution.py:169
  32.0 11.3 %collective-permute-start.8 = (bf16[256,512]{1,0:T(8,128)(2,1)S(1)}, bf16[256,512]{1,0:T(8,128)(2,1)S(1)}, u32[]{:S(2)}, u32[]{:S(2)}) collective-permute-start(bf16[256,512]{1,0:T(8,128)(2,1)S(1)} %copy-done.8), channel_id=1, source_target_pairs={{1,0},{2,1},{3,2},{5,4},{6,5},{7,6},{9,8},{10,9},{11,10},{13,12},{... | collective-permute-start | bytes 786440 | tf_op jit(solution)/shard_map/ppermute | solution.py:191
  51.1 22.0 %copy-start.1 = (bf16[2,4,4,4,48,128]{5,4,3,2,1,0:T(8,128)(2,1)S(1)}, bf16[2,4,4,4,48,128]{5,4,3,2,1,0:T(8,128)(2,1)}, u32[]{:S(2)}) copy-start(bf16[2,4,4,4,48,128]{5,4,3,2,1,0:T(8,128)(2,1)} %get-tuple-element.24) | copy-start | bytes 4718596
  56.7 21.3 %collective-permute-start.9 = (bf16[2,4,4,4,48,128]{5,4,3,2,1,0:T(8,128)(2,1)}, bf16[2,4,4,4,48,128]{5,4,3,2,1,0:T(8,128)(2,1)}, u32[]{:S(2)}, u32[]{:S(2)}) collective-permute-start(bf16[2,4,4,4,48,128]{5,4,3,2,1,0:T(8,128)(2,1)} %get-tuple-element.34), channel_id=1, source_target_pairs={{0,4},{4,0},{1,5},{5,1},{2,6},{6,2},{3,7},{7,3},{8,12},{12,8},{9,1... | collective-permute-start | bytes 4718600 | tf_op jit(solution)/shard_map/ppermute | solution.py:169
  73.9 11.6 %collective-permute-start.2 = (bf16[2,4,4,48,128]{4,3,2,1,0:T(8,128)(2,1)S(1)}, bf16[2,4,4,48,128]{4,3,2,1,0:T(8,128)(2,1)S(1)}, u32[]{:S(2)}, u32[]{:S(2)}) collective-permute-start(bf16[2,4,4,48,128]{4,3,2,1,0:T(8,128)(2,1)S(1)} %dynamic-slice_bitcast_fusion.3), channel_id=1, source_target_pairs={{0,1},{1,0},{2,3},{3,2},{4,5},{5,4},{6,7},{7,6},{8,9},{9,8},{10,11... | collective-permute-start | bytes 1179656 | tf_op jit(solution)/shard_map/ppermute | solution.py:164
  75.8 12.5 %collective-permute-start.4 = (bf16[2,4,4,48,128]{4,3,2,1,0:T(8,128)(2,1)S(1)}, bf16[2,4,4,48,128]{4,3,2,1,0:T(8,128)(2,1)S(1)}, u32[]{:S(2)}, u32[]{:S(2)}) collective-permute-start(bf16[2,4,4,48,128]{4,3,2,1,0:T(8,128)(2,1)S(1)} %dynamic-slice_bitcast_fusion.2), channel_id=1, source_target_pairs={{0,3},{1,2},{2,1},{3,0},{4,7},{5,6},{6,5},{7,4},{8,11},{9,10},{10,... | collective-permute-start | bytes 1179656 | tf_op jit(solution)/shard_map/ppermute | solution.py:164
  80.1 15.3 %collective-permute-start.10 = (bf16[2,4,4,48,128]{4,3,2,1,0:T(8,128)(2,1)S(1)}, bf16[2,4,4,48,128]{4,3,2,1,0:T(8,128)(2,1)S(1)}, u32[]{:S(2)}, u32[]{:S(2)}) collective-permute-start(bf16[2,4,4,48,128]{4,3,2,1,0:T(8,128)(2,1)S(1)} %dynamic-slice_bitcast_fusion.1), channel_id=1, source_target_pairs={{0,8},{8,0},{16,24},{24,16},{1,9},{9,1},{17,25},{25,17},{2,10},{10... | collective-permute-start | bytes 1179656 | tf_op jit(solution)/shard_map/ppermute | solution.py:164
  80.7 17.4 %collective-permute-start.12 = (bf16[2,4,4,48,128]{4,3,2,1,0:T(8,128)(2,1)S(1)}, bf16[2,4,4,48,128]{4,3,2,1,0:T(8,128)(2,1)S(1)}, u32[]{:S(2)}, u32[]{:S(2)}) collective-permute-start(bf16[2,4,4,48,128]{4,3,2,1,0:T(8,128)(2,1)S(1)} %dynamic-slice_bitcast_fusion), channel_id=1, source_target_pairs={{0,24},{8,16},{16,8},{24,0},{1,25},{9,17},{17,9},{25,1},{2,26},{10... | collective-permute-start | bytes 1179656 | tf_op jit(solution)/shard_map/ppermute | solution.py:164
  85.7 7.8 %collective-permute-start.3 = (bf16[4,4,48,128]{3,2,1,0:T(8,128)(2,1)S(1)}, bf16[4,4,48,128]{3,2,1,0:T(8,128)(2,1)S(1)}, u32[]{:S(2)}, u32[]{:S(2)}) collective-permute-start(bf16[4,4,48,128]{3,2,1,0:T(8,128)(2,1)S(1)} %dynamic-slice_bitcast_fusion.7), channel_id=1, source_target_pairs={{0,3},{1,2},{2,1},{3,0},{4,7},{5,6},{6,5},{7,4},{8,11},{9,10},{10,... | collective-permute-start | bytes 589832 | tf_op jit(solution)/shard_map/ppermute | solution.py:164
  88.4 6.3 %collective-permute-start.5 = (bf16[4,4,48,128]{3,2,1,0:T(8,128)(2,1)S(1)}, bf16[4,4,48,128]{3,2,1,0:T(8,128)(2,1)S(1)}, u32[]{:S(2)}, u32[]{:S(2)}) collective-permute-start(bf16[4,4,48,128]{3,2,1,0:T(8,128)(2,1)S(1)} %dynamic-slice_bitcast_fusion.6), channel_id=1, source_target_pairs={{0,1},{1,0},{2,3},{3,2},{4,5},{5,4},{6,7},{7,6},{8,9},{9,8},{10,11... | collective-permute-start | bytes 589832 | tf_op jit(solution)/shard_map/ppermute | solution.py:164
  94.8 10.9 %collective-permute-start.6 = (bf16[2,2,4,48,128]{4,3,1,2,0:T(8,128)(2,1)S(1)}, bf16[2,2,4,48,128]{4,3,1,2,0:T(8,128)(2,1)S(1)}, u32[]{:S(2)}, u32[]{:S(2)}) collective-permute-start(bf16[2,2,4,48,128]{4,3,1,2,0:T(8,128)(2,1)S(1)} %fusion.17), channel_id=1, source_target_pairs={{0,8},{8,0},{16,24},{24,16},{1,9},{9,1},{17,25},{25,17},{2,10},{10... | collective-permute-start | bytes 589832 | tf_op jit(solution)/shard_map/ppermute | solution.py:164
  95.5 6.1 %collective-permute-start.11 = (bf16[4,4,48,128]{3,2,1,0:T(8,128)(2,1)S(1)}, bf16[4,4,48,128]{3,2,1,0:T(8,128)(2,1)S(1)}, u32[]{:S(2)}, u32[]{:S(2)}) collective-permute-start(bf16[4,4,48,128]{3,2,1,0:T(8,128)(2,1)S(1)} %dynamic-slice_bitcast_fusion.5), channel_id=1, source_target_pairs={{0,24},{8,16},{16,8},{24,0},{1,25},{9,17},{17,9},{25,1},{2,26},{10... | collective-permute-start | bytes 589832 | tf_op jit(solution)/shard_map/ppermute | solution.py:164
  98.2 6.6 %collective-permute-start.13 = (bf16[4,4,48,128]{3,2,1,0:T(8,128)(2,1)S(1)}, bf16[4,4,48,128]{3,2,1,0:T(8,128)(2,1)S(1)}, u32[]{:S(2)}, u32[]{:S(2)}) collective-permute-start(bf16[4,4,48,128]{3,2,1,0:T(8,128)(2,1)S(1)} %dynamic-slice_bitcast_fusion.4), channel_id=1, source_target_pairs={{0,8},{8,0},{16,24},{24,16},{1,9},{9,1},{17,25},{25,17},{2,10},{10... | collective-permute-start | bytes 589832 | tf_op jit(solution)/shard_map/ppermute | solution.py:164
  104.9 5.8 %collective-permute-start.14 = (bf16[2,2,4,48,128]{4,3,1,2,0:T(8,128)(2,1)S(1)}, bf16[2,2,4,48,128]{4,3,1,2,0:T(8,128)(2,1)S(1)}, u32[]{:S(2)}, u32[]{:S(2)}) collective-permute-start(bf16[2,2,4,48,128]{4,3,1,2,0:T(8,128)(2,1)S(1)} %fusion.13), channel_id=1, source_target_pairs={{0,1},{1,0},{2,3},{3,2},{4,5},{5,4},{6,7},{7,6},{8,9},{9,8},{10,11... | collective-permute-start | bytes 589832 | tf_op jit(solution)/shard_map/ppermute | solution.py:164
  105.8 7.1 %collective-permute-start.7 = (bf16[2,4,48,128]{3,2,0,1:T(8,128)(2,1)S(1)}, bf16[2,4,48,128]{3,2,0,1:T(8,128)(2,1)S(1)}, u32[]{:S(2)}, u32[]{:S(2)}) collective-permute-start(bf16[2,4,48,128]{3,2,0,1:T(8,128)(2,1)S(1)} %dynamic-slice_bitcast_fusion.10), channel_id=1, source_target_pairs={{0,24},{8,16},{16,8},{24,0},{1,25},{9,17},{17,9},{25,1},{2,26},{10... | collective-permute-start | bytes 294920 | tf_op jit(solution)/shard_map/ppermute | solution.py:164
  110.8 5.9 %collective-permute-start.15 = (bf16[2,4,48,128]{3,2,0,1:T(8,128)(2,1)S(1)}, bf16[2,4,48,128]{3,2,0,1:T(8,128)(2,1)S(1)}, u32[]{:S(2)}, u32[]{:S(2)}) collective-permute-start(bf16[2,4,48,128]{3,2,0,1:T(8,128)(2,1)S(1)} %dynamic-slice_bitcast_fusion.9), channel_id=1, source_target_pairs={{0,3},{1,2},{2,1},{3,0},{4,7},{5,6},{6,5},{7,4},{8,11},{9,10},{10,... | collective-permute-start | bytes 294920 | tf_op jit(solution)/shard_map/ppermute | solution.py:164
  116.8 4.7 %collective-permute-start.16 = (bf16[2,2,2,48,128]{4,3,2,1,0:T(8,128)(2,1)S(1)}, bf16[2,2,2,48,128]{4,3,2,1,0:T(8,128)(2,1)S(1)}, u32[]{:S(2)}, u32[]{:S(2)}) collective-permute-start(bf16[2,2,2,48,128]{4,3,2,1,0:T(8,128)(2,1)S(1)} %dynamic-slice_bitcast_fusion.8), channel_id=1, source_target_pairs={{0,32},{32,0},{64,96},{96,64},{128,160},{160,128},{192,224},{224,1... | collective-permute-start | bytes 294920 | tf_op jit(solution)/shard_map/ppermute | solution.py:164
  118.8 12.9 %collective-permute-start.22 = (bf16[128,512]{1,0:T(8,128)(2,1)S(1)}, bf16[128,512]{1,0:T(8,128)(2,1)S(1)}, u32[]{:S(2)}, u32[]{:S(2)}) collective-permute-start(bf16[128,512]{1,0:T(8,128)(2,1)S(1)} %copy-done.9), channel_id=1, source_target_pairs={{1,0},{2,1},{3,2},{5,4},{6,5},{7,6},{9,8},{10,9},{11,10},{13,12},{... | collective-permute-start | bytes 393224 | tf_op jit(solution)/shard_map/ppermute | solution.py:191
  121.5 8.0 %collective-permute-start.17 = (bf16[2,2,48,128]{3,2,1,0:T(8,128)(2,1)S(1)}, bf16[2,2,48,128]{3,2,1,0:T(8,128)(2,1)S(1)}, u32[]{:S(2)}, u32[]{:S(2)}) collective-permute-start(bf16[2,2,48,128]{3,2,1,0:T(8,128)(2,1)S(1)} %dynamic-slice_bitcast_fusion.11), channel_id=1, source_target_pairs={{0,224},{32,64},{64,32},{96,128},{128,96},{160,192},{192,160},{224... | collective-permute-start | bytes 147464 | tf_op jit(solution)/shard_map/ppermute | solution.py:164
  129.6 6.0 %collective-permute-start.18 = (bf16[2,2,24,128]{3,2,1,0:T(8,128)(2,1)S(1)}, bf16[2,2,24,128]{3,2,1,0:T(8,128)(2,1)S(1)}, u32[]{:S(2)}, u32[]{:S(2)}) collective-permute-start(bf16[2,2,24,128]{3,2,1,0:T(8,128)(2,1)S(1)} %fusion.29), channel_id=1, source_target_pairs={{0,96},{32,192},{64,160},{96,0},{128,224},{160,64},{192,32},{224,1... | collective-permute-start | bytes 73736 | tf_op jit(solution)/shard_map/ppermute | solution.py:164
  135.6 4.0 %collective-permute-start.21 = (bf16[2,2,24,128]{3,2,1,0:T(8,128)(2,1)S(1)}, bf16[2,2,24,128]{3,2,1,0:T(8,128)(2,1)S(1)}, u32[]{:S(2)}, u32[]{:S(2)}) collective-permute-start(bf16[2,2,24,128]{3,2,1,0:T(8,128)(2,1)S(1)} %fusion.27), channel_id=1, source_target_pairs={{0,3},{1,0},{2,1},{3,2},{4,7},{5,4},{6,5},{7,6},{8,11},{9,8},{10,9... | collective-permute-start | bytes 73736 | tf_op jit(solution)/shard_map/ppermute | solution.py:247
  137.8 5.3 %collective-permute-start.20 = (bf16[2,2,24,128]{3,2,1,0:T(8,128)(2,1)S(1)}, bf16[2,2,24,128]{3,2,1,0:T(8,128)(2,1)S(1)}, u32[]{:S(2)}, u32[]{:S(2)}) collective-permute-start(bf16[2,2,24,128]{3,2,1,0:T(8,128)(2,1)S(1)} %fusion.27), channel_id=1, source_target_pairs={{0,2},{1,3},{2,0},{3,1},{4,6},{5,7},{6,4},{7,5},{8,10},{9,11},{10,... | collective-permute-start | bytes 73736 | tf_op jit(solution)/shard_map/ppermute | solution.py:247
  137.8 5.3 %collective-permute-start.19 = (bf16[2,2,24,128]{3,2,1,0:T(8,128)(2,1)S(1)}, bf16[2,2,24,128]{3,2,1,0:T(8,128)(2,1)S(1)}, u32[]{:S(2)}, u32[]{:S(2)}) collective-permute-start(bf16[2,2,24,128]{3,2,1,0:T(8,128)(2,1)S(1)} %fusion.27), channel_id=1, source_target_pairs={{0,1},{1,2},{2,3},{3,0},{4,5},{5,6},{6,7},{7,4},{8,9},{9,10},{10,1... | collective-permute-start | bytes 73736 | tf_op jit(solution)/shard_map/ppermute | solution.py:247
  (11 other events, 117.3 us)
where the time goes:
time: 147 us
  waiting for transfers between devices  48.9 us (33%)
  starting transfers between devices  38 us (26%)
  Pallas kernels  29.1 us (20%)
  between operations  16.3 us (11%)
  other arithmetic  8.71 us (6%)
  local copies, waits for them, and re-layouts  5.89 us (4%)
    pallas_call x4, Pallas kernels, kernel_call(): pl.pallas_call(kernel, out_shape=[jax.ShapeDtypeStruct(s, t) for s, t in...  29.1 us
    ppermute x15, starting transfers between devices, halve(): got = lax.ppermute(sent, axis, list(enumerate(pairs)))  28.9 us
    ppermute x15, waiting for transfers between devices, halve(): got = lax.ppermute(sent, axis, list(enumerate(pairs)))  27.9 us
    ppermute x3, waiting for transfers between devices, along(): lax.ppermute(value, 'x', [(s, s + steps) for s in range(initial, last)])  17.5 us
    ppermute x3, starting transfers between devices, along(): lax.ppermute(value, 'x', [(s, s + steps) for s in range(initial, last)])  5.99 us
    ppermute x3, waiting for transfers between devices, on_device(): lax.ppermute(s, 'x', [(i, (i + k) % X) for i in range(X)])  3.56 us
    ppermute x3, starting transfers between devices, on_device(): lax.ppermute(s, 'x', [(i, (i + k) % X) for i in range(X)])  3.13 us
  transfers between devices with their start and end apart: 23, of which 14 were waited for; matrix products, arithmetic and copies ran while one was open for 5% of the time, Pallas kernels for 9%

commit v1 on v0

v1 whole, which is shorter than its diff:
```python
import functools

import jax
import jax.numpy as jnp
from jax import lax
from jax.experimental import pallas as pl
from jax.experimental.pallas import tpu as pltpu
from jax.sharding import Mesh, PartitionSpec as P

F32, BF16 = jnp.float32, jnp.bfloat16
Z, Y, CORES, X = 8, 4, 2, 4
D0, D1 = 128, 256
ROWS, CH = 512, 512
HALO = D0 + D1
TILE = 256
MIB = 1024 * 1024

FIRST, SECOND = (1, 0, 3, 2), (3, 2, 1, 0)
BIT_A, BIT_B = (0, 1, 1, 0), (0, 0, 1, 1)
Z_PAIRS = ((1, 0, 3, 2, 5, 4, 7, 6), (7, 2, 1, 4, 3, 6, 5, 0), (3, 6, 5, 0, 7, 2, 1, 4))
Z_ORDER = (0, 3, 7, 4, 1, 6, 2, 5)
Z_ORDERS = (Z_ORDER, tuple((i + 1) % Z for i in Z_ORDER))
Z_PAIRS_NEXT = tuple(tuple((pairs[(i - 1) % Z] + 1) % Z for i in range(Z)) for pairs in Z_PAIRS)
Z_SECOND, Z_THIRD = (sum(((Z_ORDER.index(i) >> k) & 1) << i for i in range(Z)) for k in (1, 0))


def ring_place(i, half):
    a, b = BIT_A[i], BIT_B[i]
    return 2 * a + b if half == 0 else 2 * b + a


def dot(a, b):
    return jnp.dot(a, b, preferred_element_type=F32)


def dot_cols(a, b):
    return lax.dot_general(a, b, (((1,), (1,)), ((), ())), preferred_element_type=F32)


def dot_rows(a, b):
    return lax.dot_general(a, b, (((0,), (0,)), ((), ())), preferred_element_type=F32)


def gates(pre):
    return jnp.tanh(pre[:, :CH]), 0.5 * jnp.tanh(0.5 * pre[:, CH:]) + 0.5


def forward_local_kernel(local, cw, ow, stream, gated0, slope_f, slope_g, skip):
    for r, size in ((D0, D0), (2 * D0, TILE)):
        at = slice(r - D0, r - D0 + size)
        now = local[r : r + size, :]
        pre = dot(local[at, :], cw[0, :CH, :]) + dot(now, cw[0, CH:, :])
        f, g = gates(pre)
        gated = (f * g).astype(BF16)
        stream[at, :] = (now.astype(F32) + dot(gated, ow[0, :, :CH])).astype(BF16)
        gated0[at, :] = gated
        slope_f[at, :] = (1.0 - f * f) * g
        slope_g[at, :] = f * g * (1.0 - g)
        skip[at, :] = dot(gated, ow[0, :, CH:])


def forward_kernel(
    halo, local, cw, ow, rc, sc, stream_high, skip_high,
    early, flow, pre1, stream1, gated0, gated1, slope_f, slope_g, skip,
    ext, skip_low,
):
    ext[:HALO, :] = halo[...]
    ext[HALO:, :] = local[:D0, :]
    for r, size in ((0, TILE), (D1, D0)):
        now = ext[D0 + r : D0 + r + size, :]
        pre = dot(ext[r : r + size, :], cw[0, :CH, :]) + dot(now, cw[0, CH:, :])
        f, g = gates(pre)
        gated = (f * g).astype(BF16)
        stream1[r : r + size, :] = (now.astype(F32) + dot(gated, ow[0, :, :CH])).astype(BF16)
        if r == D1:
            gated0[...] = gated
            slope_f[...] = (1.0 - f * f) * g
            slope_g[...] = f * g * (1.0 - g)
            skip_low[...] = dot(gated, ow[0, :, CH:])
    stream1[HALO:, :] = stream_high[...]
    for r in range(0, ROWS, TILE):
        at = slice(r, r + TILE)
        pre = dot(stream1[at, :], cw[1, :CH, :]) + dot(stream1[r + D1 : r + D1 + TILE, :], cw[1, CH:, :])
        f, g = gates(pre)
        gated = (f * g).astype(BF16)
        gated1[at, :] = gated
        more = dot(gated, ow[1, :, CH:])
        if r == 0:
            skip[:D0, :] = (skip_low[...] + more[:D0, :]).astype(BF16)
            skip[D0:TILE, :] = (skip_high[:D0, :] + more[D0:, :]).astype(BF16)
        else:
            skip[at, :] = (skip_high[D0:, :] + more).astype(BF16)
        gc = dot_cols(rc[at, :], ow[1, :, :CH]) + dot_cols(sc[at, :], ow[1, :, CH:])
        pre1[at, :CH] = (gc * ((1.0 - f * f) * g)).astype(BF16)
        pre1[at, CH:] = (gc * (f * g * (1.0 - g))).astype(BF16)
        pc = pre1[at, :]
        flow[at, :] = rc[at, :].astype(F32) + dot_cols(pc, cw[1, CH:, :])
        ahead = dot_cols(pc, cw[1, :CH, :])
        if r < D1:
            early[at, :] = ahead.astype(BF16)
        else:
            flow[:TILE, :] += ahead


def backward_low_kernel(flow1, low_f, low_g, high_f, high_g, sc, ow, cw, proj, pre0, flow, early):
    fl = flow1[:TILE, :]
    flow_b = fl.astype(BF16)
    proj[...] = flow_b
    gc = dot_cols(flow_b, ow[0, :, :CH]) + dot_cols(sc[:TILE, :], ow[0, :, CH:])
    pre0[:D0, :CH] = (gc[:D0] * low_f[...]).astype(BF16)
    pre0[:D0, CH:] = (gc[:D0] * low_g[...]).astype(BF16)
    pre0[D0:, :CH] = (gc[D0:] * high_f[:D0, :]).astype(BF16)
    pre0[D0:, CH:] = (gc[D0:] * high_g[:D0, :]).astype(BF16)
    pc = pre0[...]
    flow[...] = fl + dot_cols(pc, cw[0, CH:, :])
    ahead = dot_cols(pc, cw[0, :CH, :])
    early[...] = ahead[:D0, :].astype(BF16)
    flow[:D0, :] += ahead[D0:, :]


def backward_high_kernel(flow1, returned, high_f, high_g, sc, ow, cw, flow_low, proj, pre0, resid, tail):
    fl = flow1[TILE:, :] + returned[...].astype(F32)
    flow_b = fl.astype(BF16)
    proj[...] = flow_b
    gc = dot_cols(flow_b, ow[0, :, :CH]) + dot_cols(sc[TILE:, :], ow[0, :, CH:])
    pre0[:, :CH] = (gc * high_f[D0:, :]).astype(BF16)
    pre0[:, CH:] = (gc * high_g[D0:, :]).astype(BF16)
    pc = pre0[...]
    fl = fl + dot_cols(pc, cw[0, CH:, :])
    ahead = dot_cols(pc, cw[0, :CH, :])
    resid[:D0, :] = flow_low[:D0, :].astype(BF16)
    resid[D0:TILE, :] = (flow_low[D0:, :] + ahead[:D0, :]).astype(BF16)
    resid[TILE:, :] = (fl[:D0, :] + ahead[D0:, :]).astype(BF16)
    tail[...] = fl[D0:, :]


def place(layer, half, y, z):
    order = Z_ORDERS[half] if layer == 1 else Z_ORDER
    unit, t = divmod(order.index(z), 2)
    if layer == 1:
        return (unit, ring_place(y, 0)), t
    return (ring_place(y, half), unit), t


def gradient_body(core, layer, stream, gated, pre, left, right, mine, other):
    delay = D1 if layer == 1 else D0
    odd = jnp.full((16, CH // 2), core[0], jnp.int32) == 1
    odd_8 = jnp.full((8, CH // 2), core[0], jnp.int32) == 1
    for n in range(4):
        half = n // 2
        cols = slice((n % 2) * 256, (n % 2) * 256 + 256)
        cot = pre[:, n * 256 : (n + 1) * 256]
        for m in range(4):
            start = 0 if m < 2 else delay
            lhs = stream[start : start + ROWS, (m % 2) * 256 : (m % 2) * 256 + 256]
            g = dot_rows(lhs, cot)
            for dz in range(2):
                for y in range(Y):
                    row = dz * 128 + y * 32
                    where, t = place(layer, half, y, m * 2 + dz)
                    at = (half, *where, slice(t * 16, t * 16 + 16), cols)
                    even, uneven = g[row : row + 16], g[row + 16 : row + 32]
                    mine[at] = jnp.where(odd, uneven, even).astype(BF16)
                    other[at] = jnp.where(odd, even, uneven).astype(BF16)
        side = left if n < 2 else right
        g = dot_rows(gated[...], side[:, cols])
        order = Z_ORDERS[half] if layer == 1 else Z_ORDER
        for unit in range(4):
            for y in range(Y):
                where, _ = place(layer, half, y, order[2 * unit])
                at = (half, *where, slice(32, 48), cols)
                mine_parts, other_parts = [], []
                for t in range(2):
                    row = order[unit * 2 + t] * 64 + y * 16
                    even, uneven = g[row : row + 8], g[row + 8 : row + 16]
                    mine_parts.append(jnp.where(odd_8, uneven, even))
                    other_parts.append(jnp.where(odd_8, even, uneven))
                mine[at] = jnp.concatenate(mine_parts, axis=0).astype(BF16)
                other[at] = jnp.concatenate(other_parts, axis=0).astype(BF16)


def gradient_1_kernel(core, stream, gated, pre, left, right, mine, other):
    gradient_body(core, 1, stream, gated, pre, left, right, mine, other)


def gradient_0_kernel(
    core, halo, local, gated_low, gated_high, pre_low, pre_high, left_low, left_high, right,
    mine, other,
    stream, gated, pre, left,
):
    stream[:D0, :] = halo[D1:, :]
    stream[D0:, :] = local[...]
    gated[:D0, :] = gated_low[...]
    gated[D0:, :] = gated_high[...]
    pre[:TILE, :] = pre_low[...]
    pre[TILE:, :] = pre_high[...]
    left[:TILE, :] = left_low[...]
    left[TILE:, :] = left_high[...]
    gradient_body(core, 0, stream, gated, pre, left, right, mine, other)


def kernel_call(kernel, shapes, args, flops, moved, limit, scratch=(), smem=0):
    vmem = pl.BlockSpec(memory_space=pltpu.VMEM)
    return pl.pallas_call(
        kernel,
        out_shape=[jax.ShapeDtypeStruct(s, t) for s, t in shapes],
        in_specs=[pl.BlockSpec(memory_space=pltpu.SMEM)] * smem + [vmem] * (len(args) - smem),
        out_specs=[vmem] * len(shapes),
        scratch_shapes=scratch,
        compiler_params=pltpu.CompilerParams(vmem_limit_bytes=limit * MIB),
        cost_estimate=pl.CostEstimate(flops=flops, bytes_accessed=moved, transcendentals=0),
    )(*args)


def halve(parts, axis, pairs, bit):
    kept = lax.dynamic_index_in_dim(parts, bit, 0, False, allow_negative_indices=False)
    sent = lax.dynamic_index_in_dim(parts, 1 - bit, 0, False, allow_negative_indices=False)
    got = lax.ppermute(sent, axis, list(enumerate(pairs)))
    return (kept.astype(F32) + got.astype(F32)).astype(BF16)


def core_sum(mine, other):
    got = lax.ppermute(other, "c", [(0, 1), (1, 0)])
    return (mine.astype(F32) + got.astype(F32)).astype(BF16)


def split(s):
    return s.reshape((2, 2) + s.shape[1:])


def split_last(s):
    lead = s.shape[:-2]
    conv, out = s[..., :32, :].reshape(*lead, 2, 16, CH), s[..., 32:, :].reshape(*lead, 2, 8, CH)
    return jnp.moveaxis(jnp.concatenate([conv, out], axis=-2), -3, 0)


def together(a, b):
    return lax.optimization_barrier((a, b))


def from_x(s):
    return [lax.ppermute(s, "x", [(i, (i + k) % X) for i in range(X)]) for k in (2, 1, 3)]


def along(value, steps):
    initial, last = (max(0, -steps), min(X, X - steps))
    return lax.ppermute(value, "x", [(s, s + steps) for s in range(initial, last)])


def assemble_kernel(own, opposite, one, two, conv, out):
    for layer in range(2):
        for half in range(2):
            i = 2 * layer + half
            at = slice(half * CH, half * CH + CH)
            piece = (own[i].astype(F32) + opposite[i].astype(F32)) + (one[i].astype(F32) + two[i].astype(F32))
            conv[layer, :, at] = piece[:16]
            out[layer, :, at] = piece[16:]


def ring_bits(i):
    b = i >> 1
    return (i + b) & 1, b


def on_device(resid_in, conv_weight, out_weight, resid_cot, skip_cot):
    x0, rc, sc = resid_in[0], resid_cot[0], skip_cot[0]
    core = lax.axis_index("c")[None]
    yi, zi = lax.axis_index("y"), lax.axis_index("z")
    ya, yb = ring_bits(yi)
    z_bits = [(((i + 1) >> 1) & 1, (Z_SECOND >> i) & 1, (Z_THIRD >> i) & 1) for i in (zi, (zi - 1) & (Z - 1))]
    high = ROWS - D0
    halo = along(x0[ROWS - HALO :], 1)
    stream_high, gated_high, high_f, high_g, skip_high = kernel_call(
        forward_local_kernel,
        [((high, CH), BF16)] * 2 + [((high, CH), F32)] * 3,
        (x0, conv_weight, out_weight),
        12 * 10**8,
        10**7,
        16,
    )
    halo, high_f = lax.optimization_barrier((halo, high_f))
    early1, flow1, pre1, stream1, gated_low, gated1, low_f, low_g, skip = kernel_call(
        forward_kernel,
        [((D1, CH), BF16), ((ROWS, CH), F32), ((ROWS, 2 * CH), BF16), ((ROWS + D1, CH), BF16)]
        + [((D0, CH), BF16), ((ROWS, CH), BF16)]
        + [((D0, CH), F32)] * 2
        + [((ROWS, CH), BF16)],
        (halo, x0, conv_weight, out_weight, rc, sc, stream_high, skip_high),
        4 * 10**9,
        10**7,
        20,
        [pltpu.VMEM((HALO + D0, CH), BF16), pltpu.VMEM((D0, CH), F32)],
    )
    returned1 = along(early1, -1)
    pieces = (4, 4, 48, CH)
    mine1, other1 = kernel_call(
        gradient_1_kernel,
        [((2,) + pieces, BF16)] * 2,
        (core, stream1, gated1, pre1, rc, sc),
        5 * 10**9,
        6 * 10**6,
        16,
        smem=1,
    )
    proj_low, pre_low, flow_low, early0 = kernel_call(
        backward_low_kernel,
        [((TILE, CH), BF16), ((TILE, 2 * CH), BF16), ((TILE, CH), F32), ((D0, CH), BF16)],
        (flow1, low_f, low_g, high_f, high_g, sc, out_weight, conv_weight),
        25 * 10**8,
        6 * 10**6,
        16,
    )
    returned1, mine1, other1, flow_low = lax.optimization_barrier((returned1, mine1, other1, flow_low))
    returned0 = along(early0, -1)
    proj_high, pre_high, resid_most, tail = kernel_call(
        backward_high_kernel,
        [((TILE, CH), BF16), ((TILE, 2 * CH), BF16), ((high, CH), BF16), ((D0, CH), F32)],
        (flow1, returned1, high_f, high_g, sc, out_weight, conv_weight, flow_low),
        25 * 10**8,
        6 * 10**6,
        16,
    )
    sums1 = core_sum(mine1, other1)
    mine0, other0 = kernel_call(
        gradient_0_kernel,
        [((2,) + pieces, BF16)] * 2,
        (core, halo, x0, gated_low, gated_high, pre_low, pre_high, proj_low, proj_high, sc),
        5 * 10**9,
        6 * 10**6,
        16,
        [pltpu.VMEM((ROWS + D0, CH), BF16), pltpu.VMEM((ROWS, CH), BF16)]
        + [pltpu.VMEM((ROWS, 2 * CH), BF16), pltpu.VMEM((ROWS, CH), BF16)],
        smem=1,
    )
    sums0 = core_sum(mine0, other0)
    resid = jnp.concatenate([resid_most, (tail + returned0.astype(F32)).astype(BF16)])

    pairs_1 = (Z_PAIRS, Z_PAIRS_NEXT)
    y_steps = ((FIRST, ya), (SECOND, yb))
    s1 = [halve(split(sums1[half]), "z", pairs_1[half][0], z_bits[half][0]) for half in range(2)]
    s0 = [halve(split(sums0[half]), "y", *y_steps[half]) for half in range(2)]
    s0, s1 = together(s0, s1)
    s0 = [halve(s0[half], "y", *y_steps[1 - half]) for half in range(2)]
    s1 = [halve(s1[half], "z", pairs_1[half][1], z_bits[half][1]) for half in range(2)]
    s0, s1 = together(s0, s1)
    s0 = halve(split(jnp.stack(s0, axis=1)), "z", Z_PAIRS[0], z_bits[0][0])
    s1 = halve(split(jnp.stack(s1, axis=1)), "y", *y_steps[0])
    s0, s1 = together(s0, s1)
    s0 = halve(s0, "z", Z_PAIRS[1], z_bits[0][1])
    s1 = halve(s1, "y", *y_steps[1])
    most, least = together(jnp.concatenate([s0, s1[:1]]), s1[1:])
    most = halve(split_last(most), "z", Z_PAIRS[2], z_bits[0][2])
    least = halve(split_last(least), "z", Z_PAIRS_NEXT[2], z_bits[1][2])
    s = jnp.concatenate([most, least])
    conv_grad, out_grad = kernel_call(
        assemble_kernel,
        [((2, 16, 1024), F32), ((2, 8, 1024), F32)],
        [s] + from_x(s),
        10**6,
        10**6,
        8,
    )
    return conv_grad, out_grad, resid[None], skip[None]


def solution(mesh):
    fine = Mesh(mesh.devices.reshape(Z, Y, CORES, X), ("z", "y", "c", "x"))
    dp = ("z", "y", "c")
    return jax.shard_map(
        on_device,
        mesh=fine,
        in_specs=(P(dp, "x", None), P(), P(), P(dp, "x", None), P(dp, "x", None)),
        out_specs=(P(None, dp, None), P(None, dp, None), P(dp, "x", None), P(dp, "x", None)),
        check_vma=False,
    )
```

time: 147 us -> 105 us (0.71)
  the two profiles are of different devices: /device:TPU:8 before, /device:TPU:38 now
where the time goes in v1:
time: 105 us; the launch traced here: 104 us
  waiting for transfers between devices  39.1 us (37%)
  starting transfers between devices  35.8 us (34%)
  Pallas kernels  15.7 us (15%)
  local copies, waits for them, and re-layouts  7 us (7%)
  other arithmetic  5.84 us (6%)
    ppermute x14, waiting for transfers between devices, halve(): got = lax.ppermute(sent, axis, list(enumerate(pairs)))  29.3 us
    ppermute x14, starting transfers between devices, halve(): got = lax.ppermute(sent, axis, list(enumerate(pairs)))  23.7 us
    pallas_call x7, Pallas kernels, kernel_call(): pl.pallas_call(kernel, out_shape=[jax.ShapeDtypeStruct(s, t) for s, t in...  15.7 us
    ppermute x3, starting transfers between devices, along(): lax.ppermute(value, 'x', [(s, s + steps) for s in range(initial, last)])  8.27 us
    unnamed x26, local copies, waits for them, and re-layouts  5.5 us
    ppermute x3, waiting for transfers between devices, from_x(): lax.ppermute(s, 'x', [(i, (i + k) % X) for i in range(X)])  5 us
    ppermute x3, waiting for transfers between devices, along(): lax.ppermute(value, 'x', [(s, s + steps) for s in range(initial, last)])  4.83 us
    convert_element_type x2, other arithmetic, core_sum(): return (mine.astype(F32) + got.astype(F32)).astype(BF16)  3.92 us
  transfers between devices with their start and end apart: 22, of which 16 were waited for; matrix products, arithmetic and copies ran while one was open for 6% of the time, Pallas kernels for 10%

profile of v1, /device:TPU:38, one launch (start us, length us, event | category | flops | bytes accessed | tf_op | source)
XLA Modules:
  0.0 104.5 jit_solution(1957807324630708047)
XLA Ops:
  3.0 2.2 %copy-done = bf16[2,1024,1024]{2,1,0:T(8,128)(2,1)S(1)} copy-done((bf16[2,1024,1024]{2,1,0:T(8,128)(2,1)S(1)}, bf16[2,1024,1024]{2,1,0:T(8,128)(2,1)}, u32[]{:S(2)}) %copy-start) | copy-done | bytes 4194328
  7.8 1.8 %shard_map.84 = (bf16[384,512]{1,0:T(8,128)(2,1)S(1)}, bf16[384,512]{1,0:T(8,128)(2,1)S(1)}, f32[384,512]{1,0:T(8,128)S(1)}, f32[384,512]{1,0:T(8,128)S(1)}, f32[384,512]{1,0:T(8,128)S(1)}) custom-call(bf16[512,512]{1,0:T(8,128)(2,1)S(1)} %bitcast.110, bf16[2,1024,1024]{2,1,0:T(8,128)(2,1)S(1)} %copy-done, bf16[2,512,1024]{2,1,0:T(8,128)(2,1)S(1)} %copy-done.2), custom_call_target="tpu_custom_call" | custom-call | flops 1200000000 | bytes 10000000 | tf_op jit(solution)/shard_map/pallas_call | solution.py:204
  9.6 4.8 %collective-permute-done.halo = bf16[384,512]{1,0:T(8,128)(2,1)S(1)} collective-permute-done((bf16[384,512]{1,0:T(8,128)(2,1)S(1)}, bf16[384,512]{1,0:T(8,128)(2,1)S(1)}, u32[]{:S(2)}, u32[]{:S(2)}) %collective-permute-start) | collective-permute-done | bytes 393248 | tf_op jit(solution)/shard_map/ppermute | solution.py:247
  14.4 5.0 %shard_map.85 = (bf16[256,512]{1,0:T(8,128)(2,1)S(1)}, f32[512,512]{1,0:T(8,128)S(1)}, bf16[512,1024]{1,0:T(8,128)(2,1)S(1)}, bf16[768,512]{1,0:T(8,128)(2,1)S(1...) custom-call(bf16[384,512]{1,0:T(8,128)(2,1)S(1)} %collective-permute, ...), custom_call_target="tpu_custom_call" | custom-call | flops 4000000000 | bytes 10000000 | tf_op jit(solution)/shard_map/pallas_call | solution.py:204
  19.4 2.7 %collective-permute-start.1 = (bf16[256,512]{1,0:T(8,128)(2,1)S(1)}, bf16[256,512]{1,0:T(8,128)(2,1)S(1)}, u32[]{:S(2)}, u32[]{:S(2)}) collective-permute-start(bf16[256,512]{1,0:T(8,128)(2,1)S(1)} %get-tuple-element.62), channel_id=1, source_target_pairs={{1,0},{2,1},{3,2},{5,4},{6,5},{7,6},{9,8},{10,9},{11,10},{13,12},{... | collective-permute-start | bytes 786440 | tf_op jit(solution)/shard_map/ppermute | solution.py:247
  22.2 3.0 %shard_map.87 = (bf16[2,4,4,48,512]{4,3,2,1,0:T(8,128)(2,1)S(1)}, bf16[2,4,4,48,512]{4,3,2,1,0:T(8,128)(2,1)}) custom-call(s32[1]{0:T(128)} %bitcast.core, bf16[768,512]{1,0:T(8,128)(2,1)S(1)} %get-tuple-element.63.stream, bf16[512,512]{1,0:T(8,128)(2,1)S(1)} %get-tuple-element.64.gated, bf16[512,1024]{1,0:T(8,128)(2,1)S(1)} %get-tuple-element.65.pre, ...), custom_call_target="tpu_custom_call" | custom-call | flops 5000000000 | bytes 6000000 | tf_op jit(solution)/shard_map/pallas_call | solution.py:204
  28.1 3.0 %shard_map.89 = (bf16[2,4,4,48,512]{4,3,2,1,0:T(8,128)(2,1)S(1)}, bf16[2,4,4,48,512]{4,3,2,1,0:T(8,128)(2,1)}) custom-call(s32[1]{0:T(128)} %bitcast.core, bf16[384,512]{1,0:T(8,128)(2,1)S(1)} %copy-done.11, bf16[512,512]{1,0:T(8,128)(2,1)S(1)} %bitcast.112, bf16[128,512]{1,0:T(8,128)(2,1)S(1)} %get-tuple-element.54.gated_low, ...), custom_call_target="tpu_custom_call" | custom-call | flops 5000000000 | bytes 6000000 | tf_op jit(solution)/shard_map/pallas_call | solution.py:204
  31.7 4.2 %collective-permute-start.21 = (bf16[128,512]{1,0:T(8,128)(2,1)}, bf16[128,512]{1,0:T(8,128)(2,1)S(1)}, u32[]{:S(2)}, u32[]{:S(2)}) collective-permute-start(bf16[128,512]{1,0:T(8,128)(2,1)} %copy-done.12), channel_id=1, source_target_pairs={{1,0},{2,1},{3,2},{5,4},{6,5},{7,6},{9,8},{10,9},{11,10},{13,12},{... | collective-permute-start | bytes 393224 | tf_op jit(solution)/shard_map/ppermute | solution.py:247
  35.9 2.0 %add_convert_fusion = bf16[2,4,4,48,512]{4,3,2,1,0:T(8,128)(2,1)S(1)} fusion(bf16[2,4,4,48,512]{4,3,2,1,0:T(8,128)(2,1)} %collective-permute-done.5, bf16[2,4,4,48,512]{4,3,2,1,0:T(8,128)(2,1)S(1)} %get-tuple-element.76), kind=kLoop, calls=%fused_computation | loop fusion | flops 3145728 | bytes 4718592 | tf_op jit(solution)/shard_map/convert_element_type | solution.py:224
  38.1 2.0 %collective-permute-start.7 = (bf16[2,4,48,512]{3,2,1,0:T(8,128)(2,1)S(1)}, bf16[2,4,48,512]{3,2,1,0:T(8,128)(2,1)S(1)}, u32[]{:S(2)}, u32[]{:S(2)}) collective-permute-start(bf16[2,4,48,512]{3,2,1,0:T(8,128)(2,1)S(1)} %dynamic-slice_bitcast_fusion), channel_id=1, source_target_pairs={{0,224},{32,64},{64,32},{96,128},{128,96},{160,192},{192,160},{224... | collective-permute-start | bytes 1179656 | tf_op jit(solution)/shard_map/ppermute | solution.py:218
  40.1 4.1 %collective-permute-start.6 = (bf16[2,4,48,512]{3,2,1,0:T(8,128)(2,1)S(1)}, bf16[2,4,48,512]{3,2,1,0:T(8,128)(2,1)S(1)}, u32[]{:S(2)}, u32[]{:S(2)}) collective-permute-start(bf16[2,4,48,512]{3,2,1,0:T(8,128)(2,1)S(1)} %dynamic-slice_bitcast_fusion.1), channel_id=1, source_target_pairs={{0,32},{32,0},{64,96},{96,64},{128,160},{160,128},{192,224},{224,1... | collective-permute-start | bytes 1179656 | tf_op jit(solution)/shard_map/ppermute | solution.py:218
  44.2 2.0 %add_convert_fusion.1 = bf16[2,4,4,48,512]{4,3,2,1,0:T(8,128)(2,1)S(1)} fusion(bf16[2,4,4,48,512]{4,3,2,1,0:T(8,128)(2,1)} %collective-permute-done.2, bf16[2,4,4,48,512]{4,3,2,1,0:T(8,128)(2,1)S(1)} %get-tuple-element.74), kind=kLoop, calls=%fused_computation.1 | loop fusion | flops 3145728 | bytes 4718592 | tf_op jit(solution)/shard_map/convert_element_type | solution.py:224
  46.4 3.1 %collective-permute-start.4 = (bf16[2,4,48,512]{3,2,1,0:T(8,128)(2,1)S(1)}, bf16[2,4,48,512]{3,2,1,0:T(8,128)(2,1)S(1)}, u32[]{:S(2)}, u32[]{:S(2)}) collective-permute-start(bf16[2,4,48,512]{3,2,1,0:T(8,128)(2,1)S(1)} %dynamic-slice_bitcast_fusion.2), channel_id=1, source_target_pairs={{0,24},{8,16},{16,8},{24,0},{1,25},{9,17},{17,9},{25,1},{2,26},{10... | collective-permute-start | bytes 1179656 | tf_op jit(solution)/shard_map/ppermute | solution.py:218
  49.8 3.1 %collective-permute-done.6 = bf16[2,4,48,512]{3,2,1,0:T(8,128)(2,1)S(1)} collective-permute-done((bf16[2,4,48,512]{3,2,1,0:T(8,128)(2,1)S(1)}, bf16[2,4,48,512]{3,2,1,0:T(8,128)(2,1)S(1)}, u32[]{:S(2)}, u32[]{:S(2)}) %collective-permute-start.6) | collective-permute-done | bytes 393248 | tf_op jit(solution)/shard_map/ppermute | solution.py:218
  53.1 4.8 %collective-permute-done.4 = bf16[2,4,48,512]{3,2,1,0:T(8,128)(2,1)S(1)} collective-permute-done((bf16[2,4,48,512]{3,2,1,0:T(8,128)(2,1)S(1)}, bf16[2,4,48,512]{3,2,1,0:T(8,128)(2,1)S(1)}, u32[]{:S(2)}, u32[]{:S(2)}) %collective-permute-start.4) | collective-permute-done | bytes 393248 | tf_op jit(solution)/shard_map/ppermute | solution.py:218
  62.9 2.5 %collective-permute-done.11 = bf16[4,48,512]{2,1,0:T(8,128)(2,1)S(1)} collective-permute-done((bf16[4,48,512]{2,1,0:T(8,128)(2,1)S(1)}, bf16[4,48,512]{2,1,0:T(8,128)(2,1)S(1)}, u32[]{:S(2)}, u32[]{:S(2)}) %collective-permute-start.11) | collective-permute-done | bytes 196640 | tf_op jit(solution)/shard_map/ppermute | solution.py:218
  70.4 3.9 %collective-permute-done.13 = bf16[2,2,48,512]{3,2,1,0:T(8,128)(2,1)S(1)} collective-permute-done((bf16[2,2,48,512]{3,2,1,0:T(8,128)(2,1)S(1)}, bf16[2,2,48,512]{3,2,1,0:T(8,128)(2,1)S(1)}, u32[]{:S(2)}, u32[]{:S(2)}) %collective-permute-start.13) | collective-permute-done | bytes 196640 | tf_op jit(solution)/shard_map/ppermute | solution.py:218
  75.2 1.6 %collective-permute-start.15 = (bf16[2,48,512]{2,1,0:T(8,128)(2,1)S(1)}, bf16[2,48,512]{2,1,0:T(8,128)(2,1)S(1)}, u32[]{:S(2)}, u32[]{:S(2)}) collective-permute-start(bf16[2,48,512]{2,1,0:T(8,128)(2,1)S(1)} %dynamic-slice_bitcast_fusion.8), channel_id=1, source_target_pairs={{0,24},{8,16},{16,8},{24,0},{1,25},{9,17},{17,9},{25,1},{2,26},{10... | collective-permute-start | bytes 294920 | tf_op jit(solution)/shard_map/ppermute | solution.py:218
  78.1 3.0 %collective-permute-done.15 = bf16[2,48,512]{2,1,0:T(8,128)(2,1)S(1)} collective-permute-done((bf16[2,48,512]{2,1,0:T(8,128)(2,1)S(1)}, bf16[2,48,512]{2,1,0:T(8,128)(2,1)S(1)}, u32[]{:S(2)}, u32[]{:S(2)}) %collective-permute-start.15) | collective-permute-done | bytes 98336 | tf_op jit(solution)/shard_map/ppermute | solution.py:218
  82.1 5.1 %collective-permute-start.17 = (bf16[1,24,512]{2,1,0:T(8,128)(2,1)S(1)}, bf16[1,24,512]{2,1,0:T(8,128)(2,1)S(1)}, u32[]{:S(2)}, u32[]{:S(2)}) collective-permute-start(bf16[1,24,512]{2,1,0:T(8,128)(2,1)S(1)} %fusion.27), channel_id=1, source_target_pairs={{0,160},{32,128},{64,224},{96,192},{128,32},{160,0},{192,96},{224,... | collective-permute-start | bytes 73736 | tf_op jit(solution)/shard_map/ppermute | solution.py:218
  89.0 5.5 %collective-permute-done.16 = bf16[3,24,512]{2,1,0:T(8,128)(2,1)S(1)} collective-permute-done((bf16[3,24,512]{2,1,0:T(8,128)(2,1)S(1)}, bf16[3,24,512]{2,1,0:T(8,128)(2,1)S(1)}, u32[]{:S(2)}, u32[]{:S(2)}) %collective-permute-start.16) | collective-permute-done | bytes 73760 | tf_op jit(solution)/shard_map/ppermute | solution.py:218
  95.6 2.3 %collective-permute-start.19 = (bf16[4,24,512]{2,1,0:T(8,128)(2,1)S(1)}, bf16[4,24,512]{2,1,0:T(8,128)(2,1)S(1)}, u32[]{:S(2)}, u32[]{:S(2)}) collective-permute-start(bf16[4,24,512]{2,1,0:T(8,128)(2,1)S(1)} %pad_maximum_fusion.1.own), channel_id=1, source_target_pairs={{0,1},{1,2},{2,3},{3,0},{4,5},{5,6},{6,7},{7,4},{8,9},{9,10},{10,1... | collective-permute-start | bytes 294920 | tf_op jit(solution)/shard_map/ppermute | solution.py:242
  98.8 2.1 %collective-permute-done.18.opposite = bf16[4,24,512]{2,1,0:T(8,128)(2,1)S(1)} collective-permute-done((bf16[4,24,512]{2,1,0:T(8,128)(2,1)S(1)}, bf16[4,24,512]{2,1,0:T(8,128)(2,1)S(1)}, u32[]{:S(2)}, u32[]{:S(2)}) %collective-permute-start.18) | collective-permute-done | bytes 98336 | tf_op jit(solution)/shard_map/ppermute | solution.py:242
  100.8 2.9 %collective-permute-done.20.two = bf16[4,24,512]{2,1,0:T(8,128)(2,1)S(1)} collective-permute-done((bf16[4,24,512]{2,1,0:T(8,128)(2,1)S(1)}, bf16[4,24,512]{2,1,0:T(8,128)(2,1)S(1)}, u32[]{:S(2)}, u32[]{:S(2)}) %collective-permute-start.20) | collective-permute-done | bytes 98336 | tf_op jit(solution)/shard_map/ppermute | solution.py:242
  (95 shorter events, 26.6 us)
Async XLA Ops:
  1.7 12.7 %collective-permute-start = (bf16[384,512]{1,0:T(8,128)(2,1)S(1)}, bf16[384,512]{1,0:T(8,128)(2,1)S(1)}, u32[]{:S(2)}, u32[]{:S(2)}) collective-permute-start(bf16[384,512]{1,0:T(8,128)(2,1)S(1)} %slice_bitcast_fusion), channel_id=1, source_target_pairs={{0,1},{1,2},{2,3},{4,5},{5,6},{6,7},{8,9},{9,10},{10,11},{12,13},{... | collective-permute-start | bytes 1179656 | tf_op jit(solution)/shard_map/ppermute | solution.py:247
  7.8 6.6 %copy-start.9 = (bf16[1,512,512]{2,1,0:T(8,128)(2,1)S(1)}, bf16[1,512,512]{2,1,0:T(8,128)(2,1)}, u32[]{:S(2)}) copy-start(bf16[1,512,512]{2,1,0:T(8,128)(2,1)} %param.8) | copy-start | bytes 1572868
  19.4 7.6 %collective-permute-start.1 = (bf16[256,512]{1,0:T(8,128)(2,1)S(1)}, bf16[256,512]{1,0:T(8,128)(2,1)S(1)}, u32[]{:S(2)}, u32[]{:S(2)}) collective-permute-start(bf16[256,512]{1,0:T(8,128)(2,1)S(1)} %get-tuple-element.62), channel_id=1, source_target_pairs={{1,0},{2,1},{3,2},{5,4},{6,5},{7,6},{9,8},{10,9},{11,10},{13,12},{... | collective-permute-start | bytes 786440 | tf_op jit(solution)/shard_map/ppermute | solution.py:247
  27.0 8.9 %collective-permute-start.5 = (bf16[2,4,4,48,512]{4,3,2,1,0:T(8,128)(2,1)}, bf16[2,4,4,48,512]{4,3,2,1,0:T(8,128)(2,1)}, u32[]{:S(2)}, u32[]{:S(2)}) collective-permute-start(bf16[2,4,4,48,512]{4,3,2,1,0:T(8,128)(2,1)} %get-tuple-element.77), channel_id=1, source_target_pairs={{0,4},{4,0},{1,5},{5,1},{2,6},{6,2},{3,7},{7,3},{8,12},{12,8},{9,1... | collective-permute-start | bytes 4718600 | tf_op jit(solution)/shard_map/ppermute | solution.py:223
  31.2 13.1 %collective-permute-start.2 = (bf16[2,4,4,48,512]{4,3,2,1,0:T(8,128)(2,1)}, bf16[2,4,4,48,512]{4,3,2,1,0:T(8,128)(2,1)}, u32[]{:S(2)}, u32[]{:S(2)}) collective-permute-start(bf16[2,4,4,48,512]{4,3,2,1,0:T(8,128)(2,1)} %get-tuple-element.75), channel_id=1, source_target_pairs={{0,4},{4,0},{1,5},{5,1},{2,6},{6,2},{3,7},{7,3},{8,12},{12,8},{9,1... | collective-permute-start | bytes 4718600 | tf_op jit(solution)/shard_map/ppermute | solution.py:223
  31.7 37.6 %collective-permute-start.21 = (bf16[128,512]{1,0:T(8,128)(2,1)}, bf16[128,512]{1,0:T(8,128)(2,1)S(1)}, u32[]{:S(2)}, u32[]{:S(2)}) collective-permute-start(bf16[128,512]{1,0:T(8,128)(2,1)} %copy-done.12), channel_id=1, source_target_pairs={{1,0},{2,1},{3,2},{5,4},{6,5},{7,6},{9,8},{10,9},{11,10},{13,12},{... | collective-permute-start | bytes 393224 | tf_op jit(solution)/shard_map/ppermute | solution.py:247
  38.1 11.7 %collective-permute-start.7 = (bf16[2,4,48,512]{3,2,1,0:T(8,128)(2,1)S(1)}, bf16[2,4,48,512]{3,2,1,0:T(8,128)(2,1)S(1)}, u32[]{:S(2)}, u32[]{:S(2)}) collective-permute-start(bf16[2,4,48,512]{3,2,1,0:T(8,128)(2,1)S(1)} %dynamic-slice_bitcast_fusion), channel_id=1, source_target_pairs={{0,224},{32,64},{64,32},{96,128},{128,96},{160,192},{192,160},{224... | collective-permute-start | bytes 1179656 | tf_op jit(solution)/shard_map/ppermute | solution.py:218
  40.1 12.9 %collective-permute-start.6 = (bf16[2,4,48,512]{3,2,1,0:T(8,128)(2,1)S(1)}, bf16[2,4,48,512]{3,2,1,0:T(8,128)(2,1)S(1)}, u32[]{:S(2)}, u32[]{:S(2)}) collective-permute-start(bf16[2,4,48,512]{3,2,1,0:T(8,128)(2,1)S(1)} %dynamic-slice_bitcast_fusion.1), channel_id=1, source_target_pairs={{0,32},{32,0},{64,96},{96,64},{128,160},{160,128},{192,224},{224,1... | collective-permute-start | bytes 1179656 | tf_op jit(solution)/shard_map/ppermute | solution.py:218
  46.4 11.5 %collective-permute-start.4 = (bf16[2,4,48,512]{3,2,1,0:T(8,128)(2,1)S(1)}, bf16[2,4,48,512]{3,2,1,0:T(8,128)(2,1)S(1)}, u32[]{:S(2)}, u32[]{:S(2)}) collective-permute-start(bf16[2,4,48,512]{3,2,1,0:T(8,128)(2,1)S(1)} %dynamic-slice_bitcast_fusion.2), channel_id=1, source_target_pairs={{0,24},{8,16},{16,8},{24,0},{1,25},{9,17},{17,9},{25,1},{2,26},{10... | collective-permute-start | bytes 1179656 | tf_op jit(solution)/shard_map/ppermute | solution.py:218
  49.5 10.0 %collective-permute-start.3 = (bf16[2,4,48,512]{3,2,1,0:T(8,128)(2,1)S(1)}, bf16[2,4,48,512]{3,2,1,0:T(8,128)(2,1)S(1)}, u32[]{:S(2)}, u32[]{:S(2)}) collective-permute-start(bf16[2,4,48,512]{3,2,1,0:T(8,128)(2,1)S(1)} %dynamic-slice_bitcast_fusion.3), channel_id=1, source_target_pairs={{0,8},{8,0},{16,24},{24,16},{1,9},{9,1},{17,25},{25,17},{2,10},{10... | collective-permute-start | bytes 1179656 | tf_op jit(solution)/shard_map/ppermute | solution.py:218
  59.6 5.8 %collective-permute-start.11 = (bf16[4,48,512]{2,1,0:T(8,128)(2,1)S(1)}, bf16[4,48,512]{2,1,0:T(8,128)(2,1)S(1)}, u32[]{:S(2)}, u32[]{:S(2)}) collective-permute-start(bf16[4,48,512]{2,1,0:T(8,128)(2,1)S(1)} %dynamic-slice_bitcast_fusion.4), channel_id=1, source_target_pairs={{0,32},{32,0},{64,96},{96,64},{128,160},{160,128},{192,224},{224,1... | collective-permute-start | bytes 589832 | tf_op jit(solution)/shard_map/ppermute | solution.py:218
  60.1 5.8 %collective-permute-start.10 = (bf16[4,48,512]{2,1,0:T(8,128)(2,1)S(1)}, bf16[4,48,512]{2,1,0:T(8,128)(2,1)S(1)}, u32[]{:S(2)}, u32[]{:S(2)}) collective-permute-start(bf16[4,48,512]{2,1,0:T(8,128)(2,1)S(1)} %dynamic-slice_bitcast_fusion.5), channel_id=1, source_target_pairs={{0,224},{32,64},{64,32},{96,128},{128,96},{160,192},{192,160},{224... | collective-permute-start | bytes 589832 | tf_op jit(solution)/shard_map/ppermute | solution.py:218
  61.2 5.8 %collective-permute-start.9 = (bf16[4,48,512]{2,1,0:T(8,128)(2,1)S(1)}, bf16[4,48,512]{2,1,0:T(8,128)(2,1)S(1)}, u32[]{:S(2)}, u32[]{:S(2)}) collective-permute-start(bf16[4,48,512]{2,1,0:T(8,128)(2,1)S(1)} %dynamic-slice_bitcast_fusion.6), channel_id=1, source_target_pairs={{0,8},{8,0},{16,24},{24,16},{1,9},{9,1},{17,25},{25,17},{2,10},{10... | collective-permute-start | bytes 589832 | tf_op jit(solution)/shard_map/ppermute | solution.py:218
  61.5 7.7 %copy-start.8 = (f32[128,512]{1,0:T(8,128)S(1)}, f32[128,512]{1,0:T(8,128)}, u32[]{:S(2)}) copy-start(f32[128,512]{1,0:T(8,128)} %copy-done.7) | copy-start | bytes 786436
  61.6 7.0 %collective-permute-start.8 = (bf16[4,48,512]{2,1,0:T(8,128)(2,1)S(1)}, bf16[4,48,512]{2,1,0:T(8,128)(2,1)S(1)}, u32[]{:S(2)}, u32[]{:S(2)}) collective-permute-start(bf16[4,48,512]{2,1,0:T(8,128)(2,1)S(1)} %dynamic-slice_bitcast_fusion.7), channel_id=1, source_target_pairs={{0,24},{8,16},{16,8},{24,0},{1,25},{9,17},{17,9},{25,1},{2,26},{10... | collective-permute-start | bytes 589832 | tf_op jit(solution)/shard_map/ppermute | solution.py:218
  68.6 5.8 %collective-permute-start.13 = (bf16[2,2,48,512]{3,2,1,0:T(8,128)(2,1)S(1)}, bf16[2,2,48,512]{3,2,1,0:T(8,128)(2,1)S(1)}, u32[]{:S(2)}, u32[]{:S(2)}) collective-permute-start(bf16[2,2,48,512]{3,2,1,0:T(8,128)(2,1)S(1)} %fusion.11), channel_id=1, source_target_pairs={{0,8},{8,0},{16,24},{24,16},{1,9},{9,1},{17,25},{25,17},{2,10},{10... | collective-permute-start | bytes 589832 | tf_op jit(solution)/shard_map/ppermute | solution.py:218
  69.3 5.8 %collective-permute-start.12 = (bf16[2,2,48,512]{3,2,1,0:T(8,128)(2,1)S(1)}, bf16[2,2,48,512]{3,2,1,0:T(8,128)(2,1)S(1)}, u32[]{:S(2)}, u32[]{:S(2)}) collective-permute-start(bf16[2,2,48,512]{3,2,1,0:T(8,128)(2,1)S(1)} %fusion.15), channel_id=1, source_target_pairs={{0,32},{32,0},{64,96},{96,64},{128,160},{160,128},{192,224},{224,1... | collective-permute-start | bytes 589832 | tf_op jit(solution)/shard_map/ppermute | solution.py:218
  75.2 5.9 %collective-permute-start.15 = (bf16[2,48,512]{2,1,0:T(8,128)(2,1)S(1)}, bf16[2,48,512]{2,1,0:T(8,128)(2,1)S(1)}, u32[]{:S(2)}, u32[]{:S(2)}) collective-permute-start(bf16[2,48,512]{2,1,0:T(8,128)(2,1)S(1)} %dynamic-slice_bitcast_fusion.8), channel_id=1, source_target_pairs={{0,24},{8,16},{16,8},{24,0},{1,25},{9,17},{17,9},{25,1},{2,26},{10... | collective-permute-start | bytes 294920 | tf_op jit(solution)/shard_map/ppermute | solution.py:218
  76.8 5.2 %collective-permute-start.14 = (bf16[2,48,512]{2,1,0:T(8,128)(2,1)S(1)}, bf16[2,48,512]{2,1,0:T(8,128)(2,1)S(1)}, u32[]{:S(2)}, u32[]{:S(2)}) collective-permute-start(bf16[2,48,512]{2,1,0:T(8,128)(2,1)S(1)} %dynamic-slice_bitcast_fusion.9), channel_id=1, source_target_pairs={{0,224},{32,64},{64,32},{96,128},{128,96},{160,192},{192,160},{224... | collective-permute-start | bytes 294920 | tf_op jit(solution)/shard_map/ppermute | solution.py:218
  82.1 6.9 %collective-permute-start.17 = (bf16[1,24,512]{2,1,0:T(8,128)(2,1)S(1)}, bf16[1,24,512]{2,1,0:T(8,128)(2,1)S(1)}, u32[]{:S(2)}, u32[]{:S(2)}) collective-permute-start(bf16[1,24,512]{2,1,0:T(8,128)(2,1)S(1)} %fusion.27), channel_id=1, source_target_pairs={{0,160},{32,128},{64,224},{96,192},{128,32},{160,0},{192,96},{224,... | collective-permute-start | bytes 73736 | tf_op jit(solution)/shard_map/ppermute | solution.py:218
  87.2 7.4 %collective-permute-start.16 = (bf16[3,24,512]{2,1,0:T(8,128)(2,1)S(1)}, bf16[3,24,512]{2,1,0:T(8,128)(2,1)S(1)}, u32[]{:S(2)}, u32[]{:S(2)}) collective-permute-start(bf16[3,24,512]{2,1,0:T(8,128)(2,1)S(1)} %fusion.22), channel_id=1, source_target_pairs={{0,96},{32,192},{64,160},{96,0},{128,224},{160,64},{192,32},{224,1... | collective-permute-start | bytes 221192 | tf_op jit(solution)/shard_map/ppermute | solution.py:218
  94.6 6.2 %collective-permute-start.18 = (bf16[4,24,512]{2,1,0:T(8,128)(2,1)S(1)}, bf16[4,24,512]{2,1,0:T(8,128)(2,1)S(1)}, u32[]{:S(2)}, u32[]{:S(2)}) collective-permute-start(bf16[4,24,512]{2,1,0:T(8,128)(2,1)S(1)} %pad_maximum_fusion.1.own), channel_id=1, source_target_pairs={{0,2},{1,3},{2,0},{3,1},{4,6},{5,7},{6,4},{7,5},{8,10},{9,11},{10,... | collective-permute-start | bytes 294920 | tf_op jit(solution)/shard_map/ppermute | solution.py:242
  95.6 5.3 %collective-permute-start.19 = (bf16[4,24,512]{2,1,0:T(8,128)(2,1)S(1)}, bf16[4,24,512]{2,1,0:T(8,128)(2,1)S(1)}, u32[]{:S(2)}, u32[]{:S(2)}) collective-permute-start(bf16[4,24,512]{2,1,0:T(8,128)(2,1)S(1)} %pad_maximum_fusion.1.own), channel_id=1, source_target_pairs={{0,1},{1,2},{2,3},{3,0},{4,5},{5,6},{6,7},{7,4},{8,9},{9,10},{10,1... | collective-permute-start | bytes 294920 | tf_op jit(solution)/shard_map/ppermute | solution.py:242
  97.9 5.8 %collective-permute-start.20 = (bf16[4,24,512]{2,1,0:T(8,128)(2,1)S(1)}, bf16[4,24,512]{2,1,0:T(8,128)(2,1)S(1)}, u32[]{:S(2)}, u32[]{:S(2)}) collective-permute-start(bf16[4,24,512]{2,1,0:T(8,128)(2,1)S(1)} %pad_maximum_fusion.1.own), channel_id=1, source_target_pairs={{0,3},{1,0},{2,1},{3,2},{4,7},{5,4},{6,5},{7,6},{8,11},{9,8},{10,9... | collective-permute-start | bytes 294920 | tf_op jit(solution)/shard_map/ppermute | solution.py:242
  (11 other events, 37.6 us)

commit v2 on v1

--- a/solution.py
+++ b/solution.py
@@ -59,7 +59,22 @@
         skip[at, :] = dot(gated, ow[0, :, CH:])
 
 
-def forward_kernel(
+def layer_1(r, stream1, cw, ow, rc, sc, gated1, pre1):
+    at = slice(r, r + TILE)
+    pre = dot(stream1[at, :], cw[1, :CH, :]) + dot(stream1[r + D1 : r + D1 + TILE, :], cw[1, CH:, :])
+    f, g = gates(pre)
+    gated = (f * g).astype(BF16)
+    gated1[...] = gated
+    more = dot(gated, ow[1, :, CH:])
+    gc = dot_cols(rc[at, :], ow[1, :, :CH]) + dot_cols(sc[at, :], ow[1, :, CH:])
+    pre1[:, :CH] = (gc * ((1.0 - f * f) * g)).astype(BF16)
+    pre1[:, CH:] = (gc * (f * g * (1.0 - g))).astype(BF16)
+    pc = pre1[...]
+    flow = rc[at, :].astype(F32) + dot_cols(pc, cw[1, CH:, :])
+    return more, flow, dot_cols(pc, cw[1, :CH, :])
+
+
+def forward_low_kernel(
     halo, local, cw, ow, rc, sc, stream_high, skip_high,
     early, flow, pre1, stream1, gated0, gated1, slope_f, slope_g, skip,
     ext, skip_low,
@@ -78,32 +93,29 @@
             slope_g[...] = f * g * (1.0 - g)
             skip_low[...] = dot(gated, ow[0, :, CH:])
     stream1[HALO:, :] = stream_high[...]
-    for r in range(0, ROWS, TILE):
-        at = slice(r, r + TILE)
-        pre = dot(stream1[at, :], cw[1, :CH, :]) + dot(stream1[r + D1 : r + D1 + TILE, :], cw[1, CH:, :])
-        f, g = gates(pre)
-        gated = (f * g).astype(BF16)
-        gated1[at, :] = gated
-        more = dot(gated, ow[1, :, CH:])
-        if r == 0:
-            skip[:D0, :] = (skip_low[...] + more[:D0, :]).astype(BF16)
-            skip[D0:TILE, :] = (skip_high[:D0, :] + more[D0:, :]).astype(BF16)
-        else:
-            skip[at, :] = (skip_high[D0:, :] + more).astype(BF16)
-        gc = dot_cols(rc[at, :], ow[1, :, :CH]) + dot_cols(sc[at, :], ow[1, :, CH:])
-        pre1[at, :CH] = (gc * ((1.0 - f * f) * g)).astype(BF16)
-        pre1[at, CH:] = (gc * (f * g * (1.0 - g))).astype(BF16)
-        pc = pre1[at, :]
-        flow[at, :] = rc[at, :].astype(F32) + dot_cols(pc, cw[1, CH:, :])
-        ahead = dot_cols(pc, cw[1, :CH, :])
-        if r < D1:
-            early[at, :] = ahead.astype(BF16)
-        else:
-            flow[:TILE, :] += ahead
+    more, flow[...], ahead = layer_1(0, stream1, cw, ow, rc, sc, gated1, pre1)
+    early[...] = ahead.astype(BF16)
+    skip[:D0, :] = (skip_low[...] + more[:D0, :]).astype(BF16)
+    skip[D0:, :] = (skip_high[:D0, :] + more[D0:, :]).astype(BF16)
+
+
+def forward_high_kernel(
+    stream1, cw, ow, rc, sc, skip_high, skip_low, gated_low, pre_low, flow_before,
+    flow_low, flow_high, pre1, gated1, skip,
+):
+    high = pl.ds(TILE, TILE)
+    more, flow_high[...], ahead = layer_1(
+        TILE, stream1, cw, ow, rc, sc, gated1.at[high, :], pre1.at[high, :]
+    )
+    flow_low[...] = flow_before[...] + ahead
+    skip[:TILE, :] = skip_low[...]
+    skip[TILE:, :] = (skip_high[D0:, :] + more).astype(BF16)
+    gated1[:TILE, :] = gated_low[...]
+    pre1[:TILE, :] = pre_low[...]
 
 
 def backward_low_kernel(flow1, low_f, low_g, high_f, high_g, sc, ow, cw, proj, pre0, flow, early):
-    fl = flow1[:TILE, :]
+    fl = flow1[...]
     flow_b = fl.astype(BF16)
     proj[...] = flow_b
     gc = dot_cols(flow_b, ow[0, :, :CH]) + dot_cols(sc[:TILE, :], ow[0, :, CH:])
@@ -119,7 +131,7 @@
 
 
 def backward_high_kernel(flow1, returned, high_f, high_g, sc, ow, cw, flow_low, proj, pre0, resid, tail):
-    fl = flow1[TILE:, :] + returned[...].astype(F32)
+    fl = flow1[...] + returned[...].astype(F32)
     flow_b = fl.astype(BF16)
     proj[...] = flow_b
     gc = dot_cols(flow_b, ow[0, :, :CH]) + dot_cols(sc[TILE:, :], ow[0, :, CH:])
@@ -219,9 +231,14 @@
     return (kept.astype(F32) + got.astype(F32)).astype(BF16)
 
 
-def core_sum(mine, other):
-    got = lax.ppermute(other, "c", [(0, 1), (1, 0)])
-    return (mine.astype(F32) + got.astype(F32)).astype(BF16)
+def picked(parts, i):
+    return lax.dynamic_index_in_dim(parts, i, 0, False, allow_negative_indices=False)
+
+
+def halve_of_two(terms, axis, pairs, bit):
+    sent = sum(picked(t, 1 - bit).astype(F32) for t in terms).astype(BF16)
+    got = lax.ppermute(sent, axis, list(enumerate(pairs)))
+    return (sum(picked(t, bit).astype(F32) for t in terms) + got.astype(F32)).astype(BF16)
 
 
 def split(s):
@@ -279,19 +296,27 @@
         16,
     )
     halo, high_f = lax.optimization_barrier((halo, high_f))
-    early1, flow1, pre1, stream1, gated_low, gated1, low_f, low_g, skip = kernel_call(
-        forward_kernel,
-        [((D1, CH), BF16), ((ROWS, CH), F32), ((ROWS, 2 * CH), BF16), ((ROWS + D1, CH), BF16)]
-        + [((D0, CH), BF16), ((ROWS, CH), BF16)]
+    early1, flow_before, pre1_low, stream1, gated_low, gated1_low, low_f, low_g, skip_low = kernel_call(
+        forward_low_kernel,
+        [((D1, CH), BF16), ((TILE, CH), F32), ((TILE, 2 * CH), BF16), ((ROWS + D1, CH), BF16)]
+        + [((D0, CH), BF16), ((TILE, CH), BF16)]
         + [((D0, CH), F32)] * 2
-        + [((ROWS, CH), BF16)],
+        + [((TILE, CH), BF16)],
         (halo, x0, conv_weight, out_weight, rc, sc, stream_high, skip_high),
-        4 * 10**9,
+        2 * 10**9,
         10**7,
-        20,
+        16,
         [pltpu.VMEM((HALO + D0, CH), BF16), pltpu.VMEM((D0, CH), F32)],
     )
     returned1 = along(early1, -1)
+    flow1_low, flow1_high, pre1, gated1, skip = kernel_call(
+        forward_high_kernel,
+        [((TILE, CH), F32)] * 2 + [((ROWS, 2 * CH), BF16), ((ROWS, CH), BF16), ((ROWS, CH), BF16)],
+        (stream1, conv_weight, out_weight, rc, sc, skip_high, skip_low, gated1_low, pre1_low, flow_before),
+        5 * 10**9,
+        10**7,
+        16,
+    )
     pieces = (4, 4, 48, CH)
     mine1, other1 = kernel_call(
         gradient_1_kernel,
@@ -305,7 +330,7 @@
     proj_low, pre_low, flow_low, early0 = kernel_call(
         backward_low_kernel,
         [((TILE, CH), BF16), ((TILE, 2 * CH), BF16), ((TILE, CH), F32), ((D0, CH), BF16)],
-        (flow1, low_f, low_g, high_f, high_g, sc, out_weight, conv_weight),
+        (flow1_low, low_f, low_g, high_f, high_g, sc, out_weight, conv_weight),
         25 * 10**8,
         6 * 10**6,
         16,
@@ -315,12 +340,12 @@
     proj_high, pre_high, resid_most, tail = kernel_call(
         backward_high_kernel,
         [((TILE, CH), BF16), ((TILE, 2 * CH), BF16), ((high, CH), BF16), ((D0, CH), F32)],
-        (flow1, returned1, high_f, high_g, sc, out_weight, conv_weight, flow_low),
+        (flow1_high, returned1, high_f, high_g, sc, out_weight, conv_weight, flow_low),
         25 * 10**8,
         6 * 10**6,
         16,
     )
-    sums1 = core_sum(mine1, other1)
+    got1 = lax.ppermute(other1, "c", [(0, 1), (1, 0)])
     mine0, other0 = kernel_call(
         gradient_0_kernel,
         [((2,) + pieces, BF16)] * 2,
@@ -332,13 +357,16 @@
         + [pltpu.VMEM((ROWS, 2 * CH), BF16), pltpu.VMEM((ROWS, CH), BF16)],
         smem=1,
     )
-    sums0 = core_sum(mine0, other0)
+    got0 = lax.ppermute(other0, "c", [(0, 1), (1, 0)])
     resid = jnp.concatenate([resid_most, (tail + returned0.astype(F32)).astype(BF16)])
 
     pairs_1 = (Z_PAIRS, Z_PAIRS_NEXT)
     y_steps = ((FIRST, ya), (SECOND, yb))
-    s1 = [halve(split(sums1[half]), "z", pairs_1[half][0], z_bits[half][0]) for half in range(2)]
-    s0 = [halve(split(sums0[half]), "y", *y_steps[half]) for half in range(2)]
+    s1 = [
+        halve_of_two((split(mine1[half]), split(got1[half])), "z", pairs_1[half][0], z_bits[half][0])
+        for half in range(2)
+    ]
+    s0 = [halve_of_two((split(mine0[half]), split(got0[half])), "y", *y_steps[half]) for half in range(2)]
     s0, s1 = together(s0, s1)
     s0 = [halve(s0[half], "y", *y_steps[1 - half]) for half in range(2)]
     s1 = [halve(s1[half], "z", pairs_1[half][1], z_bits[half][1]) for half in range(2)]

time: 105 us -> 103 us (0.981)
  other arithmetic: 5.84 us -> 2.5 us
  local copies, waits for them, and re-layouts: 7 us -> 9.85 us
  starting transfers between devices: 35.8 us -> 33.5 us
  Pallas kernels: 15.7 us -> 16.8 us
    ppermute x14 -> x10, starting transfers between devices: 23.7 us -> 14 us  [halve(): got = lax.ppermute(sent, axis, list(enumerate(pairs)))]
    ppermute x2 -> x6, starting transfers between devices: 0.51 us -> 9.97 us  [the longest x4 9.46 us: halve_of_two(): got = lax.ppermute(sent, axis, list(enumerate(pairs)))]
    ppermute x2 -> x6, waiting for transfers between devices: 0.01 us -> 9.32 us  [the longest x4 9.32 us: halve_of_two(): got = lax.ppermute(sent, axis, list(enumerate(pairs)))]
    ppermute x14 -> x10, waiting for transfers between devices: 29.3 us -> 20.1 us  [halve(): got = lax.ppermute(sent, axis, list(enumerate(pairs)))]
    slice x2 -> x4, local copies, waits for them, and re-layouts: 0.23 us -> 3.21 us  [the longest x1 1.47 us: on_device(): got1[half]]
    convert_element_type x2 -> x8, other arithmetic: 3.92 us -> 1.1 us  [the longest x4 0.65 us: halve_of_two(): (sum((picked(t, bit).astype(F32) for t in terms)) + got.astype(F32)).asty...]
    ppermute x3, starting transfers between devices: 8.27 us -> 6.45 us  [along(): lax.ppermute(value, 'x', [(s, s + steps) for s in range(initial, last)])]
    pallas_call x7 -> x8, Pallas kernels: 15.7 us -> 16.8 us  [kernel_call(): pl.pallas_call(kernel, out_shape=[jax.ShapeDtypeStruct(s, t) for s, t in...]
  transfers between devices with their start and end apart: 22 -> 22, of which waited for: 16 -> 16; matrix products, arithmetic and copies ran while one was open for 6% -> 5% of each run, Pallas kernels for 10% -> 12%
where the time goes in v2:
time: 103 us
  waiting for transfers between devices  39.2 us (38%)
  starting transfers between devices  33.5 us (33%)
  Pallas kernels  16.8 us (16%)
  local copies, waits for them, and re-layouts  9.85 us (10%)
  other arithmetic  2.5 us (2%)
    ppermute x10, waiting for transfers between devices, halve(): got = lax.ppermute(sent, axis, list(enumerate(pairs)))  20.1 us
    pallas_call x8, Pallas kernels, kernel_call(): pl.pallas_call(kernel, out_shape=[jax.ShapeDtypeStruct(s, t) for s, t in...  16.8 us
    ppermute x10, starting transfers between devices, halve(): got = lax.ppermute(sent, axis, list(enumerate(pairs)))  14 us
    ppermute x4, starting transfers between devices, halve_of_two(): got = lax.ppermute(sent, axis, list(enumerate(pairs)))  9.46 us
    ppermute x4, waiting for transfers between devices, halve_of_two(): got = lax.ppermute(sent, axis, list(enumerate(pairs)))  9.32 us
    ppermute x3, starting transfers between devices, along(): lax.ppermute(value, 'x', [(s, s + steps) for s in range(initial, last)])  6.45 us
    unnamed x26, local copies, waits for them, and re-layouts  5.5 us
    ppermute x3, waiting for transfers between devices, from_x(): lax.ppermute(s, 'x', [(i, (i + k) % X) for i in range(X)])  4.99 us
  transfers between devices with their start and end apart: 22, of which 16 were waited for; matrix products, arithmetic and copies ran while one was open for 5% of the time, Pallas kernels for 12%

profile of v2, /device:TPU:38, one launch (start us, length us, event | category | flops | bytes accessed | tf_op | source)
XLA Modules:
  0.0 102.9 jit_solution(3537323261587688921)
XLA Ops:
  3.0 2.2 %copy-done = bf16[2,1024,1024]{2,1,0:T(8,128)(2,1)S(1)} copy-done((bf16[2,1024,1024]{2,1,0:T(8,128)(2,1)S(1)}, bf16[2,1024,1024]{2,1,0:T(8,128)(2,1)}, u32[]{:S(2)}) %copy-start) | copy-done | bytes 4194328
  5.2 1.6 %copy-done.2 = bf16[2,512,1024]{2,1,0:T(8,128)(2,1)S(1)} copy-done((bf16[2,512,1024]{2,1,0:T(8,128)(2,1)S(1)}, bf16[2,512,1024]{2,1,0:T(8,128)(2,1)}, u32[]{:S(2)}) %copy-start.2) | copy-done | bytes 2097176
  7.8 1.8 %shard_map.84 = (bf16[384,512]{1,0:T(8,128)(2,1)S(1)}, bf16[384,512]{1,0:T(8,128)(2,1)S(1)}, f32[384,512]{1,0:T(8,128)S(1)}, f32[384,512]{1,0:T(8,128)S(1)}, f32[384,512]{1,0:T(8,128)S(1)}) custom-call(bf16[512,512]{1,0:T(8,128)(2,1)S(1)} %bitcast.119, bf16[2,1024,1024]{2,1,0:T(8,128)(2,1)S(1)} %copy-done, bf16[2,512,1024]{2,1,0:T(8,128)(2,1)S(1)} %copy-done.2), custom_call_target="tpu_custom_call" | custom-call | flops 1200000000 | bytes 10000000 | tf_op jit(solution)/shard_map/pallas_call | solution.py:216
  9.6 4.8 %collective-permute-done.halo = bf16[384,512]{1,0:T(8,128)(2,1)S(1)} collective-permute-done((bf16[384,512]{1,0:T(8,128)(2,1)S(1)}, bf16[384,512]{1,0:T(8,128)(2,1)S(1)}, u32[]{:S(2)}, u32[]{:S(2)}) %collective-permute-start) | collective-permute-done | bytes 393248 | tf_op jit(solution)/shard_map/ppermute | solution.py:264
  14.4 3.3 %shard_map.85 = (bf16[256,512]{1,0:T(8,128)(2,1)S(1)}, f32[256,512]{1,0:T(8,128)S(1)}, bf16[256,1024]{1,0:T(8,128)(2,1)S(1)}, bf16[768,512]{1,0:T(8,128)(2,1)S(1...) custom-call(bf16[384,512]{1,0:T(8,128)(2,1)S(1)} %collective-permute, ...), custom_call_target="tpu_custom_call" | custom-call | flops 2000000000 | bytes 10000000 | tf_op jit(solution)/shard_map/pallas_call | solution.py:216
  17.7 2.8 %collective-permute-start.1 = (bf16[256,512]{1,0:T(8,128)(2,1)S(1)}, bf16[256,512]{1,0:T(8,128)(2,1)S(1)}, u32[]{:S(2)}, u32[]{:S(2)}) collective-permute-start(bf16[256,512]{1,0:T(8,128)(2,1)S(1)} %get-tuple-element.73), channel_id=1, source_target_pairs={{1,0},{2,1},{3,2},{5,4},{6,5},{7,6},{9,8},{10,9},{11,10},{13,12},{... | collective-permute-start | bytes 786440 | tf_op jit(solution)/shard_map/ppermute | solution.py:264
  20.5 2.7 %shard_map.86 = (f32[256,512]{1,0:T(8,128)S(1)}, f32[256,512]{1,0:T(8,128)S(1)}, bf16[512,1024]{1,0:T(8,128)(2,1)S(1)}, bf16[512,512]{1,0:T(8,128)(2,1)S(1)}, bf16[512,512]{1,0:T(8,128)(2,1)}) custom-call(bf16[768,512]{1,0:T(8,128)(2,1)S(1)} %get-tuple-element.61.stream1.stream, bf16[2,1024,1024]{2,1,0:T(8,128)(2,1)S(1)} %copy-done.1, ...), custom_call_target="tpu_custom_call" | custom-call | flops 5000000000 | bytes 10000000 | tf_op jit(solution)/shard_map/pallas_call | solution.py:216
  23.2 3.1 %shard_map.88 = (bf16[2,4,4,48,512]{4,3,2,1,0:T(8,128)(2,1)S(1)}, bf16[2,4,4,48,512]{4,3,2,1,0:T(8,128)(2,1)}) custom-call(s32[1]{0:T(128)} %bitcast.core, bf16[768,512]{1,0:T(8,128)(2,1)S(1)} %get-tuple-element.61.stream1.stream, bf16[512,512]{1,0:T(8,128)(2,1)S(1)} %get-tuple-element.74.gated, bf16[512,1024]{1,0:T(8,128)(2,1)S(1)} %get-tuple-element.75.pre, ...), custom_call_target="tpu_custom_call" | custom-call | flops 5000000000 | bytes 6000000 | tf_op jit(solution)/shard_map/pallas_call | solution.py:216
  29.2 3.0 %shard_map.90 = (bf16[2,4,4,48,512]{4,3,2,1,0:T(8,128)(2,1)S(1)}, bf16[2,4,4,48,512]{4,3,2,1,0:T(8,128)(2,1)}) custom-call(s32[1]{0:T(128)} %bitcast.core, bf16[384,512]{1,0:T(8,128)(2,1)S(1)} %collective-permute-done.halo, bf16[512,512]{1,0:T(8,128)(2,1)S(1)} %bitcast.121, bf16[128,512]{1,0:T(8,128)(2,1)S(1)} %get-tuple-element.59.gated_low, ...), custom_call_target="tpu_custom_call" | custom-call | flops 5000000000 | bytes 6000000 | tf_op jit(solution)/shard_map/pallas_call | solution.py:216
  32.7 2.4 %collective-permute-start.21 = (bf16[128,512]{1,0:T(8,128)(2,1)}, bf16[128,512]{1,0:T(8,128)(2,1)S(1)}, u32[]{:S(2)}, u32[]{:S(2)}) collective-permute-start(bf16[128,512]{1,0:T(8,128)(2,1)} %copy-done.12), channel_id=1, source_target_pairs={{1,0},{2,1},{3,2},{5,4},{6,5},{7,6},{9,8},{10,9},{11,10},{13,12},{... | collective-permute-start | bytes 393224 | tf_op jit(solution)/shard_map/ppermute | solution.py:264
  37.0 2.0 %collective-permute-start.7 = (bf16[2,4,48,512]{3,2,1,0:T(8,128)(2,1)S(1)}, bf16[2,4,48,512]{3,2,1,0:T(8,128)(2,1)S(1)}, u32[]{:S(2)}, u32[]{:S(2)}) collective-permute-start(bf16[2,4,48,512]{3,2,1,0:T(8,128)(2,1)S(1)} %fusion.7), channel_id=1, source_target_pairs={{0,224},{32,64},{64,32},{96,128},{128,96},{160,192},{192,160},{224... | collective-permute-start | bytes 1179656 | tf_op jit(solution)/shard_map/ppermute | solution.py:240
  39.1 4.1 %collective-permute-start.6 = (bf16[2,4,48,512]{3,2,1,0:T(8,128)(2,1)S(1)}, bf16[2,4,48,512]{3,2,1,0:T(8,128)(2,1)S(1)}, u32[]{:S(2)}, u32[]{:S(2)}) collective-permute-start(bf16[2,4,48,512]{3,2,1,0:T(8,128)(2,1)S(1)} %fusion.6), channel_id=1, source_target_pairs={{0,32},{32,0},{64,96},{96,64},{128,160},{160,128},{192,224},{224,1... | collective-permute-start | bytes 1179656 | tf_op jit(solution)/shard_map/ppermute | solution.py:240
  44.9 3.1 %collective-permute-start.4 = (bf16[2,4,48,512]{3,2,1,0:T(8,128)(2,1)S(1)}, bf16[2,4,48,512]{3,2,1,0:T(8,128)(2,1)S(1)}, u32[]{:S(2)}, u32[]{:S(2)}) collective-permute-start(bf16[2,4,48,512]{3,2,1,0:T(8,128)(2,1)S(1)} %fusion.5), channel_id=1, source_target_pairs={{0,24},{8,16},{16,8},{24,0},{1,25},{9,17},{17,9},{25,1},{2,26},{10... | collective-permute-start | bytes 1179656 | tf_op jit(solution)/shard_map/ppermute | solution.py:240
  48.5 3.6 %collective-permute-done.6 = bf16[2,4,48,512]{3,2,1,0:T(8,128)(2,1)S(1)} collective-permute-done((bf16[2,4,48,512]{3,2,1,0:T(8,128)(2,1)S(1)}, bf16[2,4,48,512]{3,2,1,0:T(8,128)(2,1)S(1)}, u32[]{:S(2)}, u32[]{:S(2)}) %collective-permute-start.6) | collective-permute-done | bytes 393248 | tf_op jit(solution)/shard_map/ppermute | solution.py:240
  52.2 4.2 %collective-permute-done.4 = bf16[2,4,48,512]{3,2,1,0:T(8,128)(2,1)S(1)} collective-permute-done((bf16[2,4,48,512]{3,2,1,0:T(8,128)(2,1)S(1)}, bf16[2,4,48,512]{3,2,1,0:T(8,128)(2,1)S(1)}, u32[]{:S(2)}, u32[]{:S(2)}) %collective-permute-start.4) | collective-permute-done | bytes 393248 | tf_op jit(solution)/shard_map/ppermute | solution.py:240
  61.5 2.5 %collective-permute-done.11 = bf16[4,48,512]{2,1,0:T(8,128)(2,1)S(1)} collective-permute-done((bf16[4,48,512]{2,1,0:T(8,128)(2,1)S(1)}, bf16[4,48,512]{2,1,0:T(8,128)(2,1)S(1)}, u32[]{:S(2)}, u32[]{:S(2)}) %collective-permute-start.11) | collective-permute-done | bytes 196640 | tf_op jit(solution)/shard_map/ppermute | solution.py:230
  69.1 4.0 %collective-permute-done.13 = bf16[2,2,48,512]{3,2,1,0:T(8,128)(2,1)S(1)} collective-permute-done((bf16[2,2,48,512]{3,2,1,0:T(8,128)(2,1)S(1)}, bf16[2,2,48,512]{3,2,1,0:T(8,128)(2,1)S(1)}, u32[]{:S(2)}, u32[]{:S(2)}) %collective-permute-start.13) | collective-permute-done | bytes 196640 | tf_op jit(solution)/shard_map/ppermute | solution.py:230
  73.8 1.6 %collective-permute-start.15 = (bf16[2,48,512]{2,1,0:T(8,128)(2,1)S(1)}, bf16[2,48,512]{2,1,0:T(8,128)(2,1)S(1)}, u32[]{:S(2)}, u32[]{:S(2)}) collective-permute-start(bf16[2,48,512]{2,1,0:T(8,128)(2,1)S(1)} %dynamic-slice_bitcast_fusion.4), channel_id=1, source_target_pairs={{0,24},{8,16},{16,8},{24,0},{1,25},{9,17},{17,9},{25,1},{2,26},{10... | collective-permute-start | bytes 294920 | tf_op jit(solution)/shard_map/ppermute | solution.py:230
  76.7 3.0 %collective-permute-done.15 = bf16[2,48,512]{2,1,0:T(8,128)(2,1)S(1)} collective-permute-done((bf16[2,48,512]{2,1,0:T(8,128)(2,1)S(1)}, bf16[2,48,512]{2,1,0:T(8,128)(2,1)S(1)}, u32[]{:S(2)}, u32[]{:S(2)}) %collective-permute-start.15) | collective-permute-done | bytes 98336 | tf_op jit(solution)/shard_map/ppermute | solution.py:230
  80.7 5.1 %collective-permute-start.17 = (bf16[1,24,512]{2,1,0:T(8,128)(2,1)S(1)}, bf16[1,24,512]{2,1,0:T(8,128)(2,1)S(1)}, u32[]{:S(2)}, u32[]{:S(2)}) collective-permute-start(bf16[1,24,512]{2,1,0:T(8,128)(2,1)S(1)} %fusion.31), channel_id=1, source_target_pairs={{0,160},{32,128},{64,224},{96,192},{128,32},{160,0},{192,96},{224,... | collective-permute-start | bytes 73736 | tf_op jit(solution)/shard_map/ppermute | solution.py:230
  87.7 5.5 %collective-permute-done.16 = bf16[3,24,512]{2,1,0:T(8,128)(2,1)S(1)} collective-permute-done((bf16[3,24,512]{2,1,0:T(8,128)(2,1)S(1)}, bf16[3,24,512]{2,1,0:T(8,128)(2,1)S(1)}, u32[]{:S(2)}, u32[]{:S(2)}) %collective-permute-start.16) | collective-permute-done | bytes 73760 | tf_op jit(solution)/shard_map/ppermute | solution.py:230
  93.7 2.6 %collective-permute-start.19 = (bf16[4,24,512]{2,1,0:T(8,128)(2,1)S(1)}, bf16[4,24,512]{2,1,0:T(8,128)(2,1)S(1)}, u32[]{:S(2)}, u32[]{:S(2)}) collective-permute-start(bf16[4,24,512]{2,1,0:T(8,128)(2,1)S(1)} %pad_maximum_fusion.1.own), channel_id=1, source_target_pairs={{0,1},{1,2},{2,3},{3,0},{4,5},{5,6},{6,7},{7,4},{8,9},{9,10},{10,1... | collective-permute-start | bytes 294920 | tf_op jit(solution)/shard_map/ppermute | solution.py:259
  97.1 2.3 %collective-permute-done.18.opposite = bf16[4,24,512]{2,1,0:T(8,128)(2,1)S(1)} collective-permute-done((bf16[4,24,512]{2,1,0:T(8,128)(2,1)S(1)}, bf16[4,24,512]{2,1,0:T(8,128)(2,1)S(1)}, u32[]{:S(2)}, u32[]{:S(2)}) %collective-permute-start.18) | collective-permute-done | bytes 98336 | tf_op jit(solution)/shard_map/ppermute | solution.py:259
  99.5 2.7 %collective-permute-done.20.two = bf16[4,24,512]{2,1,0:T(8,128)(2,1)S(1)} collective-permute-done((bf16[4,24,512]{2,1,0:T(8,128)(2,1)S(1)}, bf16[4,24,512]{2,1,0:T(8,128)(2,1)S(1)}, u32[]{:S(2)}, u32[]{:S(2)}) %collective-permute-start.20) | collective-permute-done | bytes 98336 | tf_op jit(solution)/shard_map/ppermute | solution.py:259
  (96 shorter events, 27.8 us)
Async XLA Ops:
  1.7 12.7 %collective-permute-start = (bf16[384,512]{1,0:T(8,128)(2,1)S(1)}, bf16[384,512]{1,0:T(8,128)(2,1)S(1)}, u32[]{:S(2)}, u32[]{:S(2)}) collective-permute-start(bf16[384,512]{1,0:T(8,128)(2,1)S(1)} %slice_bitcast_fusion), channel_id=1, source_target_pairs={{0,1},{1,2},{2,3},{4,5},{5,6},{6,7},{8,9},{9,10},{10,11},{12,13},{... | collective-permute-start | bytes 1179656 | tf_op jit(solution)/shard_map/ppermute | solution.py:264
  17.7 10.3 %collective-permute-start.1 = (bf16[256,512]{1,0:T(8,128)(2,1)S(1)}, bf16[256,512]{1,0:T(8,128)(2,1)S(1)}, u32[]{:S(2)}, u32[]{:S(2)}) collective-permute-start(bf16[256,512]{1,0:T(8,128)(2,1)S(1)} %get-tuple-element.73), channel_id=1, source_target_pairs={{1,0},{2,1},{3,2},{5,4},{6,5},{7,6},{9,8},{10,9},{11,10},{13,12},{... | collective-permute-start | bytes 786440 | tf_op jit(solution)/shard_map/ppermute | solution.py:264
  28.0 7.4 %collective-permute-start.5 = (bf16[2,4,4,48,512]{4,3,2,1,0:T(8,128)(2,1)}, bf16[2,4,4,48,512]{4,3,2,1,0:T(8,128)(2,1)}, u32[]{:S(2)}, u32[]{:S(2)}) collective-permute-start(bf16[2,4,4,48,512]{4,3,2,1,0:T(8,128)(2,1)} %get-tuple-element.87), channel_id=1, source_target_pairs={{0,4},{4,0},{1,5},{5,1},{2,6},{6,2},{3,7},{7,3},{8,12},{12,8},{9,1... | collective-permute-start | bytes 4718600 | tf_op jit(solution)/shard_map/ppermute | solution.py:348
  32.2 11.1 %collective-permute-start.2 = (bf16[2,4,4,48,512]{4,3,2,1,0:T(8,128)(2,1)}, bf16[2,4,4,48,512]{4,3,2,1,0:T(8,128)(2,1)}, u32[]{:S(2)}, u32[]{:S(2)}) collective-permute-start(bf16[2,4,4,48,512]{4,3,2,1,0:T(8,128)(2,1)} %get-tuple-element.85), channel_id=1, source_target_pairs={{0,4},{4,0},{1,5},{5,1},{2,6},{6,2},{3,7},{7,3},{8,12},{12,8},{9,1... | collective-permute-start | bytes 4718600 | tf_op jit(solution)/shard_map/ppermute | solution.py:360
  32.7 35.2 %collective-permute-start.21 = (bf16[128,512]{1,0:T(8,128)(2,1)}, bf16[128,512]{1,0:T(8,128)(2,1)S(1)}, u32[]{:S(2)}, u32[]{:S(2)}) collective-permute-start(bf16[128,512]{1,0:T(8,128)(2,1)} %copy-done.12), channel_id=1, source_target_pairs={{1,0},{2,1},{3,2},{5,4},{6,5},{7,6},{9,8},{10,9},{11,10},{13,12},{... | collective-permute-start | bytes 393224 | tf_op jit(solution)/shard_map/ppermute | solution.py:264
  37.0 11.3 %collective-permute-start.7 = (bf16[2,4,48,512]{3,2,1,0:T(8,128)(2,1)S(1)}, bf16[2,4,48,512]{3,2,1,0:T(8,128)(2,1)S(1)}, u32[]{:S(2)}, u32[]{:S(2)}) collective-permute-start(bf16[2,4,48,512]{3,2,1,0:T(8,128)(2,1)S(1)} %fusion.7), channel_id=1, source_target_pairs={{0,224},{32,64},{64,32},{96,128},{128,96},{160,192},{192,160},{224... | collective-permute-start | bytes 1179656 | tf_op jit(solution)/shard_map/ppermute | solution.py:240
  39.1 12.9 %collective-permute-start.6 = (bf16[2,4,48,512]{3,2,1,0:T(8,128)(2,1)S(1)}, bf16[2,4,48,512]{3,2,1,0:T(8,128)(2,1)S(1)}, u32[]{:S(2)}, u32[]{:S(2)}) collective-permute-start(bf16[2,4,48,512]{3,2,1,0:T(8,128)(2,1)S(1)} %fusion.6), channel_id=1, source_target_pairs={{0,32},{32,0},{64,96},{96,64},{128,160},{160,128},{192,224},{224,1... | collective-permute-start | bytes 1179656 | tf_op jit(solution)/shard_map/ppermute | solution.py:240
  44.9 11.6 %collective-permute-start.4 = (bf16[2,4,48,512]{3,2,1,0:T(8,128)(2,1)S(1)}, bf16[2,4,48,512]{3,2,1,0:T(8,128)(2,1)S(1)}, u32[]{:S(2)}, u32[]{:S(2)}) collective-permute-start(bf16[2,4,48,512]{3,2,1,0:T(8,128)(2,1)S(1)} %fusion.5), channel_id=1, source_target_pairs={{0,24},{8,16},{16,8},{24,0},{1,25},{9,17},{17,9},{25,1},{2,26},{10... | collective-permute-start | bytes 1179656 | tf_op jit(solution)/shard_map/ppermute | solution.py:240
  48.1 10.0 %collective-permute-start.3 = (bf16[2,4,48,512]{3,2,1,0:T(8,128)(2,1)S(1)}, bf16[2,4,48,512]{3,2,1,0:T(8,128)(2,1)S(1)}, u32[]{:S(2)}, u32[]{:S(2)}) collective-permute-start(bf16[2,4,48,512]{3,2,1,0:T(8,128)(2,1)S(1)} %fusion.4), channel_id=1, source_target_pairs={{0,8},{8,0},{16,24},{24,16},{1,9},{9,1},{17,25},{25,17},{2,10},{10... | collective-permute-start | bytes 1179656 | tf_op jit(solution)/shard_map/ppermute | solution.py:240
  58.3 5.8 %collective-permute-start.11 = (bf16[4,48,512]{2,1,0:T(8,128)(2,1)S(1)}, bf16[4,48,512]{2,1,0:T(8,128)(2,1)S(1)}, u32[]{:S(2)}, u32[]{:S(2)}) collective-permute-start(bf16[4,48,512]{2,1,0:T(8,128)(2,1)S(1)} %dynamic-slice_bitcast_fusion), channel_id=1, source_target_pairs={{0,32},{32,0},{64,96},{96,64},{128,160},{160,128},{192,224},{224,1... | collective-permute-start | bytes 589832 | tf_op jit(solution)/shard_map/ppermute | solution.py:230
  58.7 5.8 %collective-permute-start.10 = (bf16[4,48,512]{2,1,0:T(8,128)(2,1)S(1)}, bf16[4,48,512]{2,1,0:T(8,128)(2,1)S(1)}, u32[]{:S(2)}, u32[]{:S(2)}) collective-permute-start(bf16[4,48,512]{2,1,0:T(8,128)(2,1)S(1)} %dynamic-slice_bitcast_fusion.1), channel_id=1, source_target_pairs={{0,224},{32,64},{64,32},{96,128},{128,96},{160,192},{192,160},{224... | collective-permute-start | bytes 589832 | tf_op jit(solution)/shard_map/ppermute | solution.py:230
  59.8 5.8 %collective-permute-start.9 = (bf16[4,48,512]{2,1,0:T(8,128)(2,1)S(1)}, bf16[4,48,512]{2,1,0:T(8,128)(2,1)S(1)}, u32[]{:S(2)}, u32[]{:S(2)}) collective-permute-start(bf16[4,48,512]{2,1,0:T(8,128)(2,1)S(1)} %dynamic-slice_bitcast_fusion.2), channel_id=1, source_target_pairs={{0,8},{8,0},{16,24},{24,16},{1,9},{9,1},{17,25},{25,17},{2,10},{10... | collective-permute-start | bytes 589832 | tf_op jit(solution)/shard_map/ppermute | solution.py:230
  60.2 7.7 %copy-start.11 = (f32[128,512]{1,0:T(8,128)S(1)}, f32[128,512]{1,0:T(8,128)}, u32[]{:S(2)}) copy-start(f32[128,512]{1,0:T(8,128)} %copy-done.10) | copy-start | bytes 786436
  60.2 7.0 %collective-permute-start.8 = (bf16[4,48,512]{2,1,0:T(8,128)(2,1)S(1)}, bf16[4,48,512]{2,1,0:T(8,128)(2,1)S(1)}, u32[]{:S(2)}, u32[]{:S(2)}) collective-permute-start(bf16[4,48,512]{2,1,0:T(8,128)(2,1)S(1)} %dynamic-slice_bitcast_fusion.3), channel_id=1, source_target_pairs={{0,24},{8,16},{16,8},{24,0},{1,25},{9,17},{17,9},{25,1},{2,26},{10... | collective-permute-start | bytes 589832 | tf_op jit(solution)/shard_map/ppermute | solution.py:230
  67.3 5.8 %collective-permute-start.13 = (bf16[2,2,48,512]{3,2,1,0:T(8,128)(2,1)S(1)}, bf16[2,2,48,512]{3,2,1,0:T(8,128)(2,1)S(1)}, u32[]{:S(2)}, u32[]{:S(2)}) collective-permute-start(bf16[2,2,48,512]{3,2,1,0:T(8,128)(2,1)S(1)} %fusion.15), channel_id=1, source_target_pairs={{0,8},{8,0},{16,24},{24,16},{1,9},{9,1},{17,25},{25,17},{2,10},{10... | collective-permute-start | bytes 589832 | tf_op jit(solution)/shard_map/ppermute | solution.py:230
  68.0 5.8 %collective-permute-start.12 = (bf16[2,2,48,512]{3,2,1,0:T(8,128)(2,1)S(1)}, bf16[2,2,48,512]{3,2,1,0:T(8,128)(2,1)S(1)}, u32[]{:S(2)}, u32[]{:S(2)}) collective-permute-start(bf16[2,2,48,512]{3,2,1,0:T(8,128)(2,1)S(1)} %fusion.19), channel_id=1, source_target_pairs={{0,32},{32,0},{64,96},{96,64},{128,160},{160,128},{192,224},{224,1... | collective-permute-start | bytes 589832 | tf_op jit(solution)/shard_map/ppermute | solution.py:230
  73.8 22.5 %copy-start.9 = (bf16[384,512]{1,0:T(8,128)(2,1)S(1)}, bf16[384,512]{1,0:T(8,128)(2,1)}, u32[]{:S(2)}) copy-start(bf16[384,512]{1,0:T(8,128)(2,1)} %copy-done.8) | copy-start | bytes 1179652
  73.8 5.9 %collective-permute-start.15 = (bf16[2,48,512]{2,1,0:T(8,128)(2,1)S(1)}, bf16[2,48,512]{2,1,0:T(8,128)(2,1)S(1)}, u32[]{:S(2)}, u32[]{:S(2)}) collective-permute-start(bf16[2,48,512]{2,1,0:T(8,128)(2,1)S(1)} %dynamic-slice_bitcast_fusion.4), channel_id=1, source_target_pairs={{0,24},{8,16},{16,8},{24,0},{1,25},{9,17},{17,9},{25,1},{2,26},{10... | collective-permute-start | bytes 294920 | tf_op jit(solution)/shard_map/ppermute | solution.py:230
  75.4 5.2 %collective-permute-start.14 = (bf16[2,48,512]{2,1,0:T(8,128)(2,1)S(1)}, bf16[2,48,512]{2,1,0:T(8,128)(2,1)S(1)}, u32[]{:S(2)}, u32[]{:S(2)}) collective-permute-start(bf16[2,48,512]{2,1,0:T(8,128)(2,1)S(1)} %dynamic-slice_bitcast_fusion.5), channel_id=1, source_target_pairs={{0,224},{32,64},{64,32},{96,128},{128,96},{160,192},{192,160},{224... | collective-permute-start | bytes 294920 | tf_op jit(solution)/shard_map/ppermute | solution.py:230
  80.7 6.9 %collective-permute-start.17 = (bf16[1,24,512]{2,1,0:T(8,128)(2,1)S(1)}, bf16[1,24,512]{2,1,0:T(8,128)(2,1)S(1)}, u32[]{:S(2)}, u32[]{:S(2)}) collective-permute-start(bf16[1,24,512]{2,1,0:T(8,128)(2,1)S(1)} %fusion.31), channel_id=1, source_target_pairs={{0,160},{32,128},{64,224},{96,192},{128,32},{160,0},{192,96},{224,... | collective-permute-start | bytes 73736 | tf_op jit(solution)/shard_map/ppermute | solution.py:230
  85.9 7.4 %collective-permute-start.16 = (bf16[3,24,512]{2,1,0:T(8,128)(2,1)S(1)}, bf16[3,24,512]{2,1,0:T(8,128)(2,1)S(1)}, u32[]{:S(2)}, u32[]{:S(2)}) collective-permute-start(bf16[3,24,512]{2,1,0:T(8,128)(2,1)S(1)} %fusion.26), channel_id=1, source_target_pairs={{0,96},{32,192},{64,160},{96,0},{128,224},{160,64},{192,32},{224,1... | collective-permute-start | bytes 221192 | tf_op jit(solution)/shard_map/ppermute | solution.py:230
  93.3 6.2 %collective-permute-start.18 = (bf16[4,24,512]{2,1,0:T(8,128)(2,1)S(1)}, bf16[4,24,512]{2,1,0:T(8,128)(2,1)S(1)}, u32[]{:S(2)}, u32[]{:S(2)}) collective-permute-start(bf16[4,24,512]{2,1,0:T(8,128)(2,1)S(1)} %pad_maximum_fusion.1.own), channel_id=1, source_target_pairs={{0,2},{1,3},{2,0},{3,1},{4,6},{5,7},{6,4},{7,5},{8,10},{9,11},{10,... | collective-permute-start | bytes 294920 | tf_op jit(solution)/shard_map/ppermute | solution.py:259
  93.7 5.8 %collective-permute-start.19 = (bf16[4,24,512]{2,1,0:T(8,128)(2,1)S(1)}, bf16[4,24,512]{2,1,0:T(8,128)(2,1)S(1)}, u32[]{:S(2)}, u32[]{:S(2)}) collective-permute-start(bf16[4,24,512]{2,1,0:T(8,128)(2,1)S(1)} %pad_maximum_fusion.1.own), channel_id=1, source_target_pairs={{0,1},{1,2},{2,3},{3,0},{4,5},{5,6},{6,7},{7,4},{8,9},{9,10},{10,1... | collective-permute-start | bytes 294920 | tf_op jit(solution)/shard_map/ppermute | solution.py:259
  96.3 5.8 %collective-permute-start.20 = (bf16[4,24,512]{2,1,0:T(8,128)(2,1)S(1)}, bf16[4,24,512]{2,1,0:T(8,128)(2,1)S(1)}, u32[]{:S(2)}, u32[]{:S(2)}) collective-permute-start(bf16[4,24,512]{2,1,0:T(8,128)(2,1)S(1)} %pad_maximum_fusion.1.own), channel_id=1, source_target_pairs={{0,3},{1,0},{2,1},{3,2},{4,7},{5,4},{6,5},{7,6},{8,11},{9,8},{10,9... | collective-permute-start | bytes 294920 | tf_op jit(solution)/shard_map/ppermute | solution.py:259
  (11 other events, 38.1 us)

commit v3 on v2

--- a/solution.py
+++ b/solution.py
@@ -65,19 +65,16 @@
     f, g = gates(pre)
     gated = (f * g).astype(BF16)
     gated1[...] = gated
-    more = dot(gated, ow[1, :, CH:])
     gc = dot_cols(rc[at, :], ow[1, :, :CH]) + dot_cols(sc[at, :], ow[1, :, CH:])
     pre1[:, :CH] = (gc * ((1.0 - f * f) * g)).astype(BF16)
     pre1[:, CH:] = (gc * (f * g * (1.0 - g))).astype(BF16)
-    pc = pre1[...]
-    flow = rc[at, :].astype(F32) + dot_cols(pc, cw[1, CH:, :])
-    return more, flow, dot_cols(pc, cw[1, :CH, :])
+    return dot_cols(pre1[...], cw[1, :CH, :])
 
 
 def forward_low_kernel(
-    halo, local, cw, ow, rc, sc, stream_high, skip_high,
-    early, flow, pre1, stream1, gated0, gated1, slope_f, slope_g, skip,
-    ext, skip_low,
+    halo, local, cw, ow, rc, sc, stream_high,
+    early, pre1, stream1, gated0, gated1, slope_f, slope_g,
+    ext,
 ):
     ext[:HALO, :] = halo[...]
     ext[HALO:, :] = local[:D0, :]
@@ -91,27 +88,23 @@
             gated0[...] = gated
             slope_f[...] = (1.0 - f * f) * g
             slope_g[...] = f * g * (1.0 - g)
-            skip_low[...] = dot(gated, ow[0, :, CH:])
     stream1[HALO:, :] = stream_high[...]
-    more, flow[...], ahead = layer_1(0, stream1, cw, ow, rc, sc, gated1, pre1)
-    early[...] = ahead.astype(BF16)
-    skip[:D0, :] = (skip_low[...] + more[:D0, :]).astype(BF16)
-    skip[D0:, :] = (skip_high[:D0, :] + more[D0:, :]).astype(BF16)
+    early[...] = layer_1(0, stream1, cw, ow, rc, sc, gated1, pre1).astype(BF16)
 
 
 def forward_high_kernel(
-    stream1, cw, ow, rc, sc, skip_high, skip_low, gated_low, pre_low, flow_before,
+    stream1, cw, ow, rc, sc, skip_high, gated0_low, gated_low, pre_low,
     flow_low, flow_high, pre1, gated1, skip,
 ):
     high = pl.ds(TILE, TILE)
-    more, flow_high[...], ahead = layer_1(
-        TILE, stream1, cw, ow, rc, sc, gated1.at[high, :], pre1.at[high, :]
-    )
-    flow_low[...] = flow_before[...] + ahead
-    skip[:TILE, :] = skip_low[...]
-    skip[TILE:, :] = (skip_high[D0:, :] + more).astype(BF16)
+    ahead = layer_1(TILE, stream1, cw, ow, rc, sc, gated1.at[high, :], pre1.at[high, :])
     gated1[:TILE, :] = gated_low[...]
     pre1[:TILE, :] = pre_low[...]
+    flow_high[...] = rc[TILE:, :].astype(F32) + dot_cols(pre1[TILE:, :], cw[1, CH:, :])
+    flow_low[...] = rc[:TILE, :].astype(F32) + dot_cols(pre_low[...], cw[1, CH:, :]) + ahead
+    more = dot(gated1[...], ow[1, :, CH:])
+    skip[:D0, :] = (dot(gated0_low[...], ow[0, :, CH:]) + more[:D0, :]).astype(BF16)
+    skip[D0:, :] = (skip_high[...] + more[D0:, :]).astype(BF16)
 
 
 def backward_low_kernel(flow1, low_f, low_g, high_f, high_g, sc, ow, cw, proj, pre0, flow, early):
@@ -154,8 +147,9 @@
     return (ring_place(y, half), unit), t
 
 
-def gradient_body(core, layer, stream, gated, pre, left, right, mine, other):
+def gradient_body(core, layer, stream, gated, pre, left, right, mine, sent, other, sems):
     delay = D1 if layer == 1 else D0
+    copies = [pltpu.make_async_copy(other.at[half], sent.at[half], sems.at[half]) for half in range(2)]
     odd = jnp.full((16, CH // 2), core[0], jnp.int32) == 1
     odd_8 = jnp.full((8, CH // 2), core[0], jnp.int32) == 1
     for n in range(4):
@@ -189,16 +183,20 @@
                     other_parts.append(jnp.where(odd_8, even, uneven))
                 mine[at] = jnp.concatenate(mine_parts, axis=0).astype(BF16)
                 other[at] = jnp.concatenate(other_parts, axis=0).astype(BF16)
-
-
-def gradient_1_kernel(core, stream, gated, pre, left, right, mine, other):
-    gradient_body(core, 1, stream, gated, pre, left, right, mine, other)
+        if n % 2 == 1:
+            copies[half].start()
+    for copy in copies:
+        copy.wait()
+
+
+def gradient_1_kernel(core, *refs):
+    gradient_body(core, 1, *refs)
 
 
 def gradient_0_kernel(
     core, halo, local, gated_low, gated_high, pre_low, pre_high, left_low, left_high, right,
-    mine, other,
-    stream, gated, pre, left,
+    mine, sent,
+    stream, gated, pre, left, other, sems,
 ):
     stream[:D0, :] = halo[D1:, :]
     stream[D0:, :] = local[...]
@@ -208,16 +206,16 @@
     pre[TILE:, :] = pre_high[...]
     left[:TILE, :] = left_low[...]
     left[TILE:, :] = left_high[...]
-    gradient_body(core, 0, stream, gated, pre, left, right, mine, other)
-
-
-def kernel_call(kernel, shapes, args, flops, moved, limit, scratch=(), smem=0):
+    gradient_body(core, 0, stream, gated, pre, left, right, mine, sent, other, sems)
+
+
+def kernel_call(kernel, shapes, args, flops, moved, limit, scratch=(), smem=0, sent=0):
     vmem = pl.BlockSpec(memory_space=pltpu.VMEM)
     return pl.pallas_call(
         kernel,
         out_shape=[jax.ShapeDtypeStruct(s, t) for s, t in shapes],
         in_specs=[pl.BlockSpec(memory_space=pltpu.SMEM)] * smem + [vmem] * (len(args) - smem),
-        out_specs=[vmem] * len(shapes),
+        out_specs=[vmem] * (len(shapes) - sent) + [pl.BlockSpec(memory_space=pl.ANY)] * sent,
         scratch_shapes=scratch,
         compiler_params=pltpu.CompilerParams(vmem_limit_bytes=limit * MIB),
         cost_estimate=pl.CostEstimate(flops=flops, bytes_accessed=moved, transcendentals=0),
@@ -296,28 +294,28 @@
         16,
     )
     halo, high_f = lax.optimization_barrier((halo, high_f))
-    early1, flow_before, pre1_low, stream1, gated_low, gated1_low, low_f, low_g, skip_low = kernel_call(
+    early1, pre1_low, stream1, gated_low, gated1_low, low_f, low_g = kernel_call(
         forward_low_kernel,
-        [((D1, CH), BF16), ((TILE, CH), F32), ((TILE, 2 * CH), BF16), ((ROWS + D1, CH), BF16)]
+        [((D1, CH), BF16), ((TILE, 2 * CH), BF16), ((ROWS + D1, CH), BF16)]
         + [((D0, CH), BF16), ((TILE, CH), BF16)]
-        + [((D0, CH), F32)] * 2
-        + [((TILE, CH), BF16)],
-        (halo, x0, conv_weight, out_weight, rc, sc, stream_high, skip_high),
+        + [((D0, CH), F32)] * 2,
+        (halo, x0, conv_weight, out_weight, rc, sc, stream_high),
         2 * 10**9,
         10**7,
         16,
-        [pltpu.VMEM((HALO + D0, CH), BF16), pltpu.VMEM((D0, CH), F32)],
+        [pltpu.VMEM((HALO + D0, CH), BF16)],
     )
     returned1 = along(early1, -1)
     flow1_low, flow1_high, pre1, gated1, skip = kernel_call(
         forward_high_kernel,
         [((TILE, CH), F32)] * 2 + [((ROWS, 2 * CH), BF16), ((ROWS, CH), BF16), ((ROWS, CH), BF16)],
-        (stream1, conv_weight, out_weight, rc, sc, skip_high, skip_low, gated1_low, pre1_low, flow_before),
+        (stream1, conv_weight, out_weight, rc, sc, skip_high, gated_low, gated1_low, pre1_low),
         5 * 10**9,
         10**7,
         16,
     )
     pieces = (4, 4, 48, CH)
+    own_copy = [pltpu.VMEM((2,) + pieces, BF16), pltpu.SemaphoreType.DMA((2,))]
     mine1, other1 = kernel_call(
         gradient_1_kernel,
         [((2,) + pieces, BF16)] * 2,
@@ -325,7 +323,9 @@
         5 * 10**9,
         6 * 10**6,
         16,
+        own_copy,
         smem=1,
+        sent=1,
     )
     proj_low, pre_low, flow_low, early0 = kernel_call(
         backward_low_kernel,
@@ -335,7 +335,7 @@
         6 * 10**6,
         16,
     )
-    returned1, mine1, other1, flow_low = lax.optimization_barrier((returned1, mine1, other1, flow_low))
+    returned1, mine1, flow_low = lax.optimization_barrier((returned1, mine1, flow_low))
     returned0 = along(early0, -1)
     proj_high, pre_high, resid_most, tail = kernel_call(
         backward_high_kernel,
@@ -354,8 +354,10 @@
         6 * 10**6,
         16,
         [pltpu.VMEM((ROWS + D0, CH), BF16), pltpu.VMEM((ROWS, CH), BF16)]
-        + [pltpu.VMEM((ROWS, 2 * CH), BF16), pltpu.VMEM((ROWS, CH), BF16)],
+        + [pltpu.VMEM((ROWS, 2 * CH), BF16), pltpu.VMEM((ROWS, CH), BF16)]
+        + own_copy,
         smem=1,
+        sent=1,
     )
     got0 = lax.ppermute(other0, "c", [(0, 1), (1, 0)])
     resid = jnp.concatenate([resid_most, (tail + returned0.astype(F32)).astype(BF16)])

time: 103 us -> 103 us (level)
  transfers between devices with their start and end apart: 22 -> 22, of which waited for: 16 -> 16; matrix products, arithmetic and copies ran while one was open for 5% -> 6% of each run, Pallas kernels for 12% -> 12%
where the time goes in v3:
time: 103 us
  waiting for transfers between devices  39.2 us (38%)
  starting transfers between devices  33.9 us (33%)
  Pallas kernels  16 us (16%)
  local copies, waits for them, and re-layouts  9.85 us (10%)
  other arithmetic  2.5 us (2%)
  between operations  1.04 us (1%)
    ppermute x10, waiting for transfers between devices, halve(): got = lax.ppermute(sent, axis, list(enumerate(pairs)))  20.1 us
    pallas_call x8, Pallas kernels, kernel_call(): pl.pallas_call(kernel, out_shape=[jax.ShapeDtypeStruct(s, t) for s, t in...  16 us
    ppermute x10, starting transfers between devices, halve(): got = lax.ppermute(sent, axis, list(enumerate(pairs)))  14.1 us
    ppermute x4, starting transfers between devices, halve_of_two(): got = lax.ppermute(sent, axis, list(enumerate(pairs)))  9.47 us
    ppermute x4, waiting for transfers between devices, halve_of_two(): got = lax.ppermute(sent, axis, list(enumerate(pairs)))  9.32 us
    ppermute x3, starting transfers between devices, along(): lax.ppermute(value, 'x', [(s, s + steps) for s in range(initial, last)])  6.47 us
    unnamed x26, local copies, waits for them, and re-layouts  5.5 us
    ppermute x3, waiting for transfers between devices, from_x(): lax.ppermute(s, 'x', [(i, (i + k) % X) for i in range(X)])  4.99 us
  transfers between devices with their start and end apart: 22, of which 16 were waited for; matrix products, arithmetic and copies ran while one was open for 6% of the time, Pallas kernels for 12%

profile of v3, /device:TPU:38, one launch (start us, length us, event | category | flops | bytes accessed | tf_op | source)
XLA Modules:
  0.0 102.5 jit_solution(11300054104543181804)
XLA Ops:
  3.0 2.2 %copy-done = bf16[2,1024,1024]{2,1,0:T(8,128)(2,1)S(1)} copy-done((bf16[2,1024,1024]{2,1,0:T(8,128)(2,1)S(1)}, bf16[2,1024,1024]{2,1,0:T(8,128)(2,1)}, u32[]{:S(2)}) %copy-start) | copy-done | bytes 4194328
  5.2 1.6 %copy-done.2 = bf16[2,512,1024]{2,1,0:T(8,128)(2,1)S(1)} copy-done((bf16[2,512,1024]{2,1,0:T(8,128)(2,1)S(1)}, bf16[2,512,1024]{2,1,0:T(8,128)(2,1)}, u32[]{:S(2)}) %copy-start.2) | copy-done | bytes 2097176
  7.8 1.8 %shard_map.84 = (bf16[384,512]{1,0:T(8,128)(2,1)S(1)}, bf16[384,512]{1,0:T(8,128)(2,1)S(1)}, f32[384,512]{1,0:T(8,128)S(1)}, f32[384,512]{1,0:T(8,128)S(1)}, f32[384,512]{1,0:T(8,128)S(1)}) custom-call(bf16[512,512]{1,0:T(8,128)(2,1)S(1)} %bitcast.119, bf16[2,1024,1024]{2,1,0:T(8,128)(2,1)S(1)} %copy-done, bf16[2,512,1024]{2,1,0:T(8,128)(2,1)S(1)} %copy-done.2), custom_call_target="tpu_custom_call" | custom-call | flops 1200000000 | bytes 10000000 | tf_op jit(solution)/shard_map/pallas_call | solution.py:214
  9.6 4.8 %collective-permute-done.halo = bf16[384,512]{1,0:T(8,128)(2,1)S(1)} collective-permute-done((bf16[384,512]{1,0:T(8,128)(2,1)S(1)}, bf16[384,512]{1,0:T(8,128)(2,1)S(1)}, u32[]{:S(2)}, u32[]{:S(2)}) %collective-permute-start) | collective-permute-done | bytes 393248 | tf_op jit(solution)/shard_map/ppermute | solution.py:262
  14.4 2.7 %shard_map.85 = (bf16[256,512]{1,0:T(8,128)(2,1)S(1)}, bf16[256,1024]{1,0:T(8,128)(2,1)S(1)}, bf16[768,512]{1,0:T(8,128)(2,1)S(1)}, bf16[128,512]{1,0:T(8,128)(2...) custom-call(bf16[384,512]{1,0:T(8,128)(2,1)S(1)} %collective-permute-done.halo, ...), custom_call_target="tpu_custom_call" | custom-call | flops 2000000000 | bytes 10000000 | tf_op jit(solution)/shard_map/pallas_call | solution.py:214
  17.2 2.8 %collective-permute-start.1 = (bf16[256,512]{1,0:T(8,128)(2,1)S(1)}, bf16[256,512]{1,0:T(8,128)(2,1)S(1)}, u32[]{:S(2)}, u32[]{:S(2)}) collective-permute-start(bf16[256,512]{1,0:T(8,128)(2,1)S(1)} %get-tuple-element.68), channel_id=1, source_target_pairs={{1,0},{2,1},{3,2},{5,4},{6,5},{7,6},{9,8},{10,9},{11,10},{13,12},{... | collective-permute-start | bytes 786440 | tf_op jit(solution)/shard_map/ppermute | solution.py:262
  20.0 3.1 %shard_map.86 = (f32[256,512]{1,0:T(8,128)S(1)}, f32[256,512]{1,0:T(8,128)S(1)}, bf16[512,1024]{1,0:T(8,128)(2,1)S(1)}, bf16[512,512]{1,0:T(8,128)(2,1)S(1)}, bf16[512,512]{1,0:T(8,128)(2,1)}) custom-call(bf16[768,512]{1,0:T(8,128)(2,1)S(1)} %get-tuple-element.57.stream1.refs_0_, bf16[2,1024,1024]{2,1,0:T(8,128)(2,1)S(1)} %copy-done.1, ...), custom_call_target="tpu_custom_call" | custom-call | flops 5000000000 | bytes 10000000 | tf_op jit(solution)/shard_map/pallas_call | solution.py:214
  23.0 2.8 %shard_map.88 = (bf16[2,4,4,48,512]{4,3,2,1,0:T(8,128)(2,1)S(1)}, bf16[2,4,4,48,512]{4,3,2,1,0:T(8,128)(2,1)}) custom-call(s32[1]{0:T(128)} %bitcast.core, bf16[768,512]{1,0:T(8,128)(2,1)S(1)} %get-tuple-element.57.stream1.refs_0_, bf16[512,512]{1,0:T(8,128)(2,1)S(1)} %get-tuple-element.69.refs_1_, bf16[512,1024]{1,0:T(8,128)(2,1)S(1)} %get-tuple-element.70.refs_2_, ...), custom_call_target="tpu_custom_call" | custom-call | flops 5000000000 | bytes 6000000 | tf_op jit(solution)/shard_map/pallas_call | solution.py:214
  29.0 2.8 %shard_map.90 = (bf16[2,4,4,48,512]{4,3,2,1,0:T(8,128)(2,1)S(1)}, bf16[2,4,4,48,512]{4,3,2,1,0:T(8,128)(2,1)}) custom-call(s32[1]{0:T(128)} %bitcast.core, bf16[384,512]{1,0:T(8,128)(2,1)S(1)} %collective-permute-done.halo, bf16[512,512]{1,0:T(8,128)(2,1)S(1)} %bitcast.121, bf16[128,512]{1,0:T(8,128)(2,1)S(1)} %get-tuple-element.55.gated0_low.gated_low, ...), custom_call_target="tpu_custom_call" | custom-call | flops 5000000000 | bytes 6000000 | tf_op jit(solution)/shard_map/pallas_call | solution.py:214
  32.4 2.4 %collective-permute-start.21 = (bf16[128,512]{1,0:T(8,128)(2,1)}, bf16[128,512]{1,0:T(8,128)(2,1)S(1)}, u32[]{:S(2)}, u32[]{:S(2)}) collective-permute-start(bf16[128,512]{1,0:T(8,128)(2,1)} %copy-done.12), channel_id=1, source_target_pairs={{1,0},{2,1},{3,2},{5,4},{6,5},{7,6},{9,8},{10,9},{11,10},{13,12},{... | collective-permute-start | bytes 393224 | tf_op jit(solution)/shard_map/ppermute | solution.py:262
  36.7 2.0 %collective-permute-start.7 = (bf16[2,4,48,512]{3,2,1,0:T(8,128)(2,1)S(1)}, bf16[2,4,48,512]{3,2,1,0:T(8,128)(2,1)S(1)}, u32[]{:S(2)}, u32[]{:S(2)}) collective-permute-start(bf16[2,4,48,512]{3,2,1,0:T(8,128)(2,1)S(1)} %fusion.7), channel_id=1, source_target_pairs={{0,224},{32,64},{64,32},{96,128},{128,96},{160,192},{192,160},{224... | collective-permute-start | bytes 1179656 | tf_op jit(solution)/shard_map/ppermute | solution.py:238
  38.8 4.1 %collective-permute-start.6 = (bf16[2,4,48,512]{3,2,1,0:T(8,128)(2,1)S(1)}, bf16[2,4,48,512]{3,2,1,0:T(8,128)(2,1)S(1)}, u32[]{:S(2)}, u32[]{:S(2)}) collective-permute-start(bf16[2,4,48,512]{3,2,1,0:T(8,128)(2,1)S(1)} %fusion.6), channel_id=1, source_target_pairs={{0,32},{32,0},{64,96},{96,64},{128,160},{160,128},{192,224},{224,1... | collective-permute-start | bytes 1179656 | tf_op jit(solution)/shard_map/ppermute | solution.py:238
  44.5 3.1 %collective-permute-start.4 = (bf16[2,4,48,512]{3,2,1,0:T(8,128)(2,1)S(1)}, bf16[2,4,48,512]{3,2,1,0:T(8,128)(2,1)S(1)}, u32[]{:S(2)}, u32[]{:S(2)}) collective-permute-start(bf16[2,4,48,512]{3,2,1,0:T(8,128)(2,1)S(1)} %fusion.5), channel_id=1, source_target_pairs={{0,24},{8,16},{16,8},{24,0},{1,25},{9,17},{17,9},{25,1},{2,26},{10... | collective-permute-start | bytes 1179656 | tf_op jit(solution)/shard_map/ppermute | solution.py:238
  48.2 3.6 %collective-permute-done.6 = bf16[2,4,48,512]{3,2,1,0:T(8,128)(2,1)S(1)} collective-permute-done((bf16[2,4,48,512]{3,2,1,0:T(8,128)(2,1)S(1)}, bf16[2,4,48,512]{3,2,1,0:T(8,128)(2,1)S(1)}, u32[]{:S(2)}, u32[]{:S(2)}) %collective-permute-start.6) | collective-permute-done | bytes 393248 | tf_op jit(solution)/shard_map/ppermute | solution.py:238
  51.9 4.3 %collective-permute-done.4 = bf16[2,4,48,512]{3,2,1,0:T(8,128)(2,1)S(1)} collective-permute-done((bf16[2,4,48,512]{3,2,1,0:T(8,128)(2,1)S(1)}, bf16[2,4,48,512]{3,2,1,0:T(8,128)(2,1)S(1)}, u32[]{:S(2)}, u32[]{:S(2)}) %collective-permute-start.4) | collective-permute-done | bytes 393248 | tf_op jit(solution)/shard_map/ppermute | solution.py:238
  61.2 2.5 %collective-permute-done.11 = bf16[4,48,512]{2,1,0:T(8,128)(2,1)S(1)} collective-permute-done((bf16[4,48,512]{2,1,0:T(8,128)(2,1)S(1)}, bf16[4,48,512]{2,1,0:T(8,128)(2,1)S(1)}, u32[]{:S(2)}, u32[]{:S(2)}) %collective-permute-start.11) | collective-permute-done | bytes 196640 | tf_op jit(solution)/shard_map/ppermute | solution.py:228
  68.8 4.0 %collective-permute-done.13 = bf16[2,2,48,512]{3,2,1,0:T(8,128)(2,1)S(1)} collective-permute-done((bf16[2,2,48,512]{3,2,1,0:T(8,128)(2,1)S(1)}, bf16[2,2,48,512]{3,2,1,0:T(8,128)(2,1)S(1)}, u32[]{:S(2)}, u32[]{:S(2)}) %collective-permute-start.13) | collective-permute-done | bytes 196640 | tf_op jit(solution)/shard_map/ppermute | solution.py:228
  73.5 1.8 %collective-permute-start.15 = (bf16[2,48,512]{2,1,0:T(8,128)(2,1)S(1)}, bf16[2,48,512]{2,1,0:T(8,128)(2,1)S(1)}, u32[]{:S(2)}, u32[]{:S(2)}) collective-permute-start(bf16[2,48,512]{2,1,0:T(8,128)(2,1)S(1)} %dynamic-slice_bitcast_fusion.4), channel_id=1, source_target_pairs={{0,24},{8,16},{16,8},{24,0},{1,25},{9,17},{17,9},{25,1},{2,26},{10... | collective-permute-start | bytes 294920 | tf_op jit(solution)/shard_map/ppermute | solution.py:228
  76.4 3.2 %collective-permute-done.15 = bf16[2,48,512]{2,1,0:T(8,128)(2,1)S(1)} collective-permute-done((bf16[2,48,512]{2,1,0:T(8,128)(2,1)S(1)}, bf16[2,48,512]{2,1,0:T(8,128)(2,1)S(1)}, u32[]{:S(2)}, u32[]{:S(2)}) %collective-permute-start.15) | collective-permute-done | bytes 98336 | tf_op jit(solution)/shard_map/ppermute | solution.py:228
  80.4 5.1 %collective-permute-start.17 = (bf16[1,24,512]{2,1,0:T(8,128)(2,1)S(1)}, bf16[1,24,512]{2,1,0:T(8,128)(2,1)S(1)}, u32[]{:S(2)}, u32[]{:S(2)}) collective-permute-start(bf16[1,24,512]{2,1,0:T(8,128)(2,1)S(1)} %fusion.31), channel_id=1, source_target_pairs={{0,160},{32,128},{64,224},{96,192},{128,32},{160,0},{192,96},{224,... | collective-permute-start | bytes 73736 | tf_op jit(solution)/shard_map/ppermute | solution.py:228
  87.4 5.5 %collective-permute-done.16 = bf16[3,24,512]{2,1,0:T(8,128)(2,1)S(1)} collective-permute-done((bf16[3,24,512]{2,1,0:T(8,128)(2,1)S(1)}, bf16[3,24,512]{2,1,0:T(8,128)(2,1)S(1)}, u32[]{:S(2)}, u32[]{:S(2)}) %collective-permute-start.16) | collective-permute-done | bytes 73760 | tf_op jit(solution)/shard_map/ppermute | solution.py:228
  93.4 2.6 %collective-permute-start.19 = (bf16[4,24,512]{2,1,0:T(8,128)(2,1)S(1)}, bf16[4,24,512]{2,1,0:T(8,128)(2,1)S(1)}, u32[]{:S(2)}, u32[]{:S(2)}) collective-permute-start(bf16[4,24,512]{2,1,0:T(8,128)(2,1)S(1)} %pad_maximum_fusion.1.own), channel_id=1, source_target_pairs={{0,1},{1,2},{2,3},{3,0},{4,5},{5,6},{6,7},{7,4},{8,9},{9,10},{10,1... | collective-permute-start | bytes 294920 | tf_op jit(solution)/shard_map/ppermute | solution.py:257
  96.8 2.3 %collective-permute-done.18.opposite = bf16[4,24,512]{2,1,0:T(8,128)(2,1)S(1)} collective-permute-done((bf16[4,24,512]{2,1,0:T(8,128)(2,1)S(1)}, bf16[4,24,512]{2,1,0:T(8,128)(2,1)S(1)}, u32[]{:S(2)}, u32[]{:S(2)}) %collective-permute-start.18) | collective-permute-done | bytes 98336 | tf_op jit(solution)/shard_map/ppermute | solution.py:257
  99.2 2.7 %collective-permute-done.20.two = bf16[4,24,512]{2,1,0:T(8,128)(2,1)S(1)} collective-permute-done((bf16[4,24,512]{2,1,0:T(8,128)(2,1)S(1)}, bf16[4,24,512]{2,1,0:T(8,128)(2,1)S(1)}, u32[]{:S(2)}, u32[]{:S(2)}) %collective-permute-start.20) | collective-permute-done | bytes 98336 | tf_op jit(solution)/shard_map/ppermute | solution.py:257
  (96 shorter events, 27.7 us)
Async XLA Ops:
  1.7 12.7 %collective-permute-start = (bf16[384,512]{1,0:T(8,128)(2,1)S(1)}, bf16[384,512]{1,0:T(8,128)(2,1)S(1)}, u32[]{:S(2)}, u32[]{:S(2)}) collective-permute-start(bf16[384,512]{1,0:T(8,128)(2,1)S(1)} %slice_bitcast_fusion), channel_id=1, source_target_pairs={{0,1},{1,2},{2,3},{4,5},{5,6},{6,7},{8,9},{9,10},{10,11},{12,13},{... | collective-permute-start | bytes 1179656 | tf_op jit(solution)/shard_map/ppermute | solution.py:262
  17.2 10.7 %collective-permute-start.1 = (bf16[256,512]{1,0:T(8,128)(2,1)S(1)}, bf16[256,512]{1,0:T(8,128)(2,1)S(1)}, u32[]{:S(2)}, u32[]{:S(2)}) collective-permute-start(bf16[256,512]{1,0:T(8,128)(2,1)S(1)} %get-tuple-element.68), channel_id=1, source_target_pairs={{1,0},{2,1},{3,2},{5,4},{6,5},{7,6},{9,8},{10,9},{11,10},{13,12},{... | collective-permute-start | bytes 786440 | tf_op jit(solution)/shard_map/ppermute | solution.py:262
  25.8 9.3 %collective-permute-start.5 = (bf16[2,4,4,48,512]{4,3,2,1,0:T(8,128)(2,1)}, bf16[2,4,4,48,512]{4,3,2,1,0:T(8,128)(2,1)}, u32[]{:S(2)}, u32[]{:S(2)}) collective-permute-start(bf16[2,4,4,48,512]{4,3,2,1,0:T(8,128)(2,1)} %get-tuple-element.81), channel_id=1, source_target_pairs={{0,4},{4,0},{1,5},{5,1},{2,6},{6,2},{3,7},{7,3},{8,12},{12,8},{9,1... | collective-permute-start | bytes 4718600 | tf_op jit(solution)/shard_map/ppermute | solution.py:348
  31.8 11.1 %collective-permute-start.2 = (bf16[2,4,4,48,512]{4,3,2,1,0:T(8,128)(2,1)}, bf16[2,4,4,48,512]{4,3,2,1,0:T(8,128)(2,1)}, u32[]{:S(2)}, u32[]{:S(2)}) collective-permute-start(bf16[2,4,4,48,512]{4,3,2,1,0:T(8,128)(2,1)} %get-tuple-element.79), channel_id=1, source_target_pairs={{0,4},{4,0},{1,5},{5,1},{2,6},{6,2},{3,7},{7,3},{8,12},{12,8},{9,1... | collective-permute-start | bytes 4718600 | tf_op jit(solution)/shard_map/ppermute | solution.py:362
  32.4 35.2 %collective-permute-start.21 = (bf16[128,512]{1,0:T(8,128)(2,1)}, bf16[128,512]{1,0:T(8,128)(2,1)S(1)}, u32[]{:S(2)}, u32[]{:S(2)}) collective-permute-start(bf16[128,512]{1,0:T(8,128)(2,1)} %copy-done.12), channel_id=1, source_target_pairs={{1,0},{2,1},{3,2},{5,4},{6,5},{7,6},{9,8},{10,9},{11,10},{13,12},{... | collective-permute-start | bytes 393224 | tf_op jit(solution)/shard_map/ppermute | solution.py:262
  36.7 11.3 %collective-permute-start.7 = (bf16[2,4,48,512]{3,2,1,0:T(8,128)(2,1)S(1)}, bf16[2,4,48,512]{3,2,1,0:T(8,128)(2,1)S(1)}, u32[]{:S(2)}, u32[]{:S(2)}) collective-permute-start(bf16[2,4,48,512]{3,2,1,0:T(8,128)(2,1)S(1)} %fusion.7), channel_id=1, source_target_pairs={{0,224},{32,64},{64,32},{96,128},{128,96},{160,192},{192,160},{224... | collective-permute-start | bytes 1179656 | tf_op jit(solution)/shard_map/ppermute | solution.py:238
  38.8 12.9 %collective-permute-start.6 = (bf16[2,4,48,512]{3,2,1,0:T(8,128)(2,1)S(1)}, bf16[2,4,48,512]{3,2,1,0:T(8,128)(2,1)S(1)}, u32[]{:S(2)}, u32[]{:S(2)}) collective-permute-start(bf16[2,4,48,512]{3,2,1,0:T(8,128)(2,1)S(1)} %fusion.6), channel_id=1, source_target_pairs={{0,32},{32,0},{64,96},{96,64},{128,160},{160,128},{192,224},{224,1... | collective-permute-start | bytes 1179656 | tf_op jit(solution)/shard_map/ppermute | solution.py:238
  44.5 11.6 %collective-permute-start.4 = (bf16[2,4,48,512]{3,2,1,0:T(8,128)(2,1)S(1)}, bf16[2,4,48,512]{3,2,1,0:T(8,128)(2,1)S(1)}, u32[]{:S(2)}, u32[]{:S(2)}) collective-permute-start(bf16[2,4,48,512]{3,2,1,0:T(8,128)(2,1)S(1)} %fusion.5), channel_id=1, source_target_pairs={{0,24},{8,16},{16,8},{24,0},{1,25},{9,17},{17,9},{25,1},{2,26},{10... | collective-permute-start | bytes 1179656 | tf_op jit(solution)/shard_map/ppermute | solution.py:238
  47.8 10.0 %collective-permute-start.3 = (bf16[2,4,48,512]{3,2,1,0:T(8,128)(2,1)S(1)}, bf16[2,4,48,512]{3,2,1,0:T(8,128)(2,1)S(1)}, u32[]{:S(2)}, u32[]{:S(2)}) collective-permute-start(bf16[2,4,48,512]{3,2,1,0:T(8,128)(2,1)S(1)} %fusion.4), channel_id=1, source_target_pairs={{0,8},{8,0},{16,24},{24,16},{1,9},{9,1},{17,25},{25,17},{2,10},{10... | collective-permute-start | bytes 1179656 | tf_op jit(solution)/shard_map/ppermute | solution.py:238
  58.0 5.8 %collective-permute-start.11 = (bf16[4,48,512]{2,1,0:T(8,128)(2,1)S(1)}, bf16[4,48,512]{2,1,0:T(8,128)(2,1)S(1)}, u32[]{:S(2)}, u32[]{:S(2)}) collective-permute-start(bf16[4,48,512]{2,1,0:T(8,128)(2,1)S(1)} %dynamic-slice_bitcast_fusion), channel_id=1, source_target_pairs={{0,32},{32,0},{64,96},{96,64},{128,160},{160,128},{192,224},{224,1... | collective-permute-start | bytes 589832 | tf_op jit(solution)/shard_map/ppermute | solution.py:228
  58.4 5.8 %collective-permute-start.10 = (bf16[4,48,512]{2,1,0:T(8,128)(2,1)S(1)}, bf16[4,48,512]{2,1,0:T(8,128)(2,1)S(1)}, u32[]{:S(2)}, u32[]{:S(2)}) collective-permute-start(bf16[4,48,512]{2,1,0:T(8,128)(2,1)S(1)} %dynamic-slice_bitcast_fusion.1), channel_id=1, source_target_pairs={{0,224},{32,64},{64,32},{96,128},{128,96},{160,192},{192,160},{224... | collective-permute-start | bytes 589832 | tf_op jit(solution)/shard_map/ppermute | solution.py:228
  59.5 5.8 %collective-permute-start.9 = (bf16[4,48,512]{2,1,0:T(8,128)(2,1)S(1)}, bf16[4,48,512]{2,1,0:T(8,128)(2,1)S(1)}, u32[]{:S(2)}, u32[]{:S(2)}) collective-permute-start(bf16[4,48,512]{2,1,0:T(8,128)(2,1)S(1)} %dynamic-slice_bitcast_fusion.2), channel_id=1, source_target_pairs={{0,8},{8,0},{16,24},{24,16},{1,9},{9,1},{17,25},{25,17},{2,10},{10... | collective-permute-start | bytes 589832 | tf_op jit(solution)/shard_map/ppermute | solution.py:228
  59.9 7.7 %copy-start.11 = (f32[128,512]{1,0:T(8,128)S(1)}, f32[128,512]{1,0:T(8,128)}, u32[]{:S(2)}) copy-start(f32[128,512]{1,0:T(8,128)} %copy-done.10) | copy-start | bytes 786436
  59.9 7.0 %collective-permute-start.8 = (bf16[4,48,512]{2,1,0:T(8,128)(2,1)S(1)}, bf16[4,48,512]{2,1,0:T(8,128)(2,1)S(1)}, u32[]{:S(2)}, u32[]{:S(2)}) collective-permute-start(bf16[4,48,512]{2,1,0:T(8,128)(2,1)S(1)} %dynamic-slice_bitcast_fusion.3), channel_id=1, source_target_pairs={{0,24},{8,16},{16,8},{24,0},{1,25},{9,17},{17,9},{25,1},{2,26},{10... | collective-permute-start | bytes 589832 | tf_op jit(solution)/shard_map/ppermute | solution.py:228
  67.0 5.8 %collective-permute-start.13 = (bf16[2,2,48,512]{3,2,1,0:T(8,128)(2,1)S(1)}, bf16[2,2,48,512]{3,2,1,0:T(8,128)(2,1)S(1)}, u32[]{:S(2)}, u32[]{:S(2)}) collective-permute-start(bf16[2,2,48,512]{3,2,1,0:T(8,128)(2,1)S(1)} %fusion.15), channel_id=1, source_target_pairs={{0,8},{8,0},{16,24},{24,16},{1,9},{9,1},{17,25},{25,17},{2,10},{10... | collective-permute-start | bytes 589832 | tf_op jit(solution)/shard_map/ppermute | solution.py:228
  67.7 5.8 %collective-permute-start.12 = (bf16[2,2,48,512]{3,2,1,0:T(8,128)(2,1)S(1)}, bf16[2,2,48,512]{3,2,1,0:T(8,128)(2,1)S(1)}, u32[]{:S(2)}, u32[]{:S(2)}) collective-permute-start(bf16[2,2,48,512]{3,2,1,0:T(8,128)(2,1)S(1)} %fusion.19), channel_id=1, source_target_pairs={{0,32},{32,0},{64,96},{96,64},{128,160},{160,128},{192,224},{224,1... | collective-permute-start | bytes 589832 | tf_op jit(solution)/shard_map/ppermute | solution.py:228
  73.5 22.5 %copy-start.9 = (bf16[384,512]{1,0:T(8,128)(2,1)S(1)}, bf16[384,512]{1,0:T(8,128)(2,1)}, u32[]{:S(2)}) copy-start(bf16[384,512]{1,0:T(8,128)(2,1)} %copy-done.8) | copy-start | bytes 1179652
  73.5 6.1 %collective-permute-start.15 = (bf16[2,48,512]{2,1,0:T(8,128)(2,1)S(1)}, bf16[2,48,512]{2,1,0:T(8,128)(2,1)S(1)}, u32[]{:S(2)}, u32[]{:S(2)}) collective-permute-start(bf16[2,48,512]{2,1,0:T(8,128)(2,1)S(1)} %dynamic-slice_bitcast_fusion.4), channel_id=1, source_target_pairs={{0,24},{8,16},{16,8},{24,0},{1,25},{9,17},{17,9},{25,1},{2,26},{10... | collective-permute-start | bytes 294920 | tf_op jit(solution)/shard_map/ppermute | solution.py:228
  75.3 5.0 %collective-permute-start.14 = (bf16[2,48,512]{2,1,0:T(8,128)(2,1)S(1)}, bf16[2,48,512]{2,1,0:T(8,128)(2,1)S(1)}, u32[]{:S(2)}, u32[]{:S(2)}) collective-permute-start(bf16[2,48,512]{2,1,0:T(8,128)(2,1)S(1)} %dynamic-slice_bitcast_fusion.5), channel_id=1, source_target_pairs={{0,224},{32,64},{64,32},{96,128},{128,96},{160,192},{192,160},{224... | collective-permute-start | bytes 294920 | tf_op jit(solution)/shard_map/ppermute | solution.py:228
  80.4 6.9 %collective-permute-start.17 = (bf16[1,24,512]{2,1,0:T(8,128)(2,1)S(1)}, bf16[1,24,512]{2,1,0:T(8,128)(2,1)S(1)}, u32[]{:S(2)}, u32[]{:S(2)}) collective-permute-start(bf16[1,24,512]{2,1,0:T(8,128)(2,1)S(1)} %fusion.31), channel_id=1, source_target_pairs={{0,160},{32,128},{64,224},{96,192},{128,32},{160,0},{192,96},{224,... | collective-permute-start | bytes 73736 | tf_op jit(solution)/shard_map/ppermute | solution.py:228
  85.5 7.4 %collective-permute-start.16 = (bf16[3,24,512]{2,1,0:T(8,128)(2,1)S(1)}, bf16[3,24,512]{2,1,0:T(8,128)(2,1)S(1)}, u32[]{:S(2)}, u32[]{:S(2)}) collective-permute-start(bf16[3,24,512]{2,1,0:T(8,128)(2,1)S(1)} %fusion.26), channel_id=1, source_target_pairs={{0,96},{32,192},{64,160},{96,0},{128,224},{160,64},{192,32},{224,1... | collective-permute-start | bytes 221192 | tf_op jit(solution)/shard_map/ppermute | solution.py:228
  93.0 6.2 %collective-permute-start.18 = (bf16[4,24,512]{2,1,0:T(8,128)(2,1)S(1)}, bf16[4,24,512]{2,1,0:T(8,128)(2,1)S(1)}, u32[]{:S(2)}, u32[]{:S(2)}) collective-permute-start(bf16[4,24,512]{2,1,0:T(8,128)(2,1)S(1)} %pad_maximum_fusion.1.own), channel_id=1, source_target_pairs={{0,2},{1,3},{2,0},{3,1},{4,6},{5,7},{6,4},{7,5},{8,10},{9,11},{10,... | collective-permute-start | bytes 294920 | tf_op jit(solution)/shard_map/ppermute | solution.py:257
  93.4 5.8 %collective-permute-start.19 = (bf16[4,24,512]{2,1,0:T(8,128)(2,1)S(1)}, bf16[4,24,512]{2,1,0:T(8,128)(2,1)S(1)}, u32[]{:S(2)}, u32[]{:S(2)}) collective-permute-start(bf16[4,24,512]{2,1,0:T(8,128)(2,1)S(1)} %pad_maximum_fusion.1.own), channel_id=1, source_target_pairs={{0,1},{1,2},{2,3},{3,0},{4,5},{5,6},{6,7},{7,4},{8,9},{9,10},{10,1... | collective-permute-start | bytes 294920 | tf_op jit(solution)/shard_map/ppermute | solution.py:257
  96.0 5.8 %collective-permute-start.20 = (bf16[4,24,512]{2,1,0:T(8,128)(2,1)S(1)}, bf16[4,24,512]{2,1,0:T(8,128)(2,1)S(1)}, u32[]{:S(2)}, u32[]{:S(2)}) collective-permute-start(bf16[4,24,512]{2,1,0:T(8,128)(2,1)S(1)} %pad_maximum_fusion.1.own), channel_id=1, source_target_pairs={{0,3},{1,0},{2,1},{3,2},{4,7},{5,4},{6,5},{7,6},{8,11},{9,8},{10,9... | collective-permute-start | bytes 294920 | tf_op jit(solution)/shard_map/ppermute | solution.py:257
  (11 other events, 36.6 us)

commit v4 on v3

--- a/solution.py
+++ b/solution.py
@@ -336,7 +336,6 @@
         16,
     )
     returned1, mine1, flow_low = lax.optimization_barrier((returned1, mine1, flow_low))
-    returned0 = along(early0, -1)
     proj_high, pre_high, resid_most, tail = kernel_call(
         backward_high_kernel,
         [((TILE, CH), BF16), ((TILE, 2 * CH), BF16), ((high, CH), BF16), ((D0, CH), F32)],
@@ -360,7 +359,6 @@
         sent=1,
     )
     got0 = lax.ppermute(other0, "c", [(0, 1), (1, 0)])
-    resid = jnp.concatenate([resid_most, (tail + returned0.astype(F32)).astype(BF16)])
 
     pairs_1 = (Z_PAIRS, Z_PAIRS_NEXT)
     y_steps = ((FIRST, ya), (SECOND, yb))
@@ -370,6 +368,9 @@
     ]
     s0 = [halve_of_two((split(mine0[half]), split(got0[half])), "y", *y_steps[half]) for half in range(2)]
     s0, s1 = together(s0, s1)
+    early0, s0 = together(early0, s0)
+    returned0 = along(early0, -1)
+    resid = jnp.concatenate([resid_most, (tail + returned0.astype(F32)).astype(BF16)])
     s0 = [halve(s0[half], "y", *y_steps[1 - half]) for half in range(2)]
     s1 = [halve(s1[half], "z", pairs_1[half][1], z_bits[half][1]) for half in range(2)]
     s0, s1 = together(s0, s1)

time: 103 us -> 102 us (level)
  waiting for transfers between devices: 39.2 us -> 37.7 us
  starting transfers between devices: 33.9 us -> 35.2 us
    ppermute x10, waiting for transfers between devices: 20.1 us -> 18.3 us  [halve(): got = lax.ppermute(sent, axis, list(enumerate(pairs)))]
    ppermute x10, starting transfers between devices: 14.1 us -> 15.7 us  [halve(): got = lax.ppermute(sent, axis, list(enumerate(pairs)))]
    unnamed x26 -> x28, local copies, waits for them, and re-layouts: 5.5 us -> 4.87 us
  transfers between devices with their start and end apart: 22 -> 22, of which waited for: 16 -> 17; matrix products, arithmetic and copies ran while one was open for 6% -> 5% of each run, Pallas kernels for 12% -> 13%
where the time goes in v4:
time: 102 us
  waiting for transfers between devices  37.7 us (37%)
  starting transfers between devices  35.2 us (35%)
  Pallas kernels  16.2 us (16%)
  local copies, waits for them, and re-layouts  9.16 us (9%)
  other arithmetic  2.53 us (2%)
  between operations  1.08 us (1%)
    ppermute x10, waiting for transfers between devices, halve(): got = lax.ppermute(sent, axis, list(enumerate(pairs)))  18.3 us
    pallas_call x8, Pallas kernels, kernel_call(): pl.pallas_call(kernel, out_shape=[jax.ShapeDtypeStruct(s, t) for s, t in...  16.2 us
    ppermute x10, starting transfers between devices, halve(): got = lax.ppermute(sent, axis, list(enumerate(pairs)))  15.7 us
    ppermute x4, waiting for transfers between devices, halve_of_two(): got = lax.ppermute(sent, axis, list(enumerate(pairs)))  9.59 us
    ppermute x4, starting transfers between devices, halve_of_two(): got = lax.ppermute(sent, axis, list(enumerate(pairs)))  9.44 us
    ppermute x3, starting transfers between devices, along(): lax.ppermute(value, 'x', [(s, s + steps) for s in range(initial, last)])  6.5 us
    ppermute x3, waiting for transfers between devices, from_x(): lax.ppermute(s, 'x', [(i, (i + k) % X) for i in range(X)])  4.99 us
    unnamed x28, local copies, waits for them, and re-layouts  4.87 us
  transfers between devices with their start and end apart: 22, of which 17 were waited for; matrix products, arithmetic and copies ran while one was open for 5% of the time, Pallas kernels for 13%

profile of v4, /device:TPU:38, one launch (start us, length us, event | category | flops | bytes accessed | tf_op | source)
XLA Modules:
  0.0 102.0 jit_solution(16684105134315595529)
XLA Ops:
  3.0 2.2 %copy-done = bf16[2,1024,1024]{2,1,0:T(8,128)(2,1)S(1)} copy-done((bf16[2,1024,1024]{2,1,0:T(8,128)(2,1)S(1)}, bf16[2,1024,1024]{2,1,0:T(8,128)(2,1)}, u32[]{:S(2)}) %copy-start) | copy-done | bytes 4194328
  9.6 4.8 %collective-permute-done.halo = bf16[384,512]{1,0:T(8,128)(2,1)S(1)} collective-permute-done((bf16[384,512]{1,0:T(8,128)(2,1)S(1)}, bf16[384,512]{1,0:T(8,128)(2,1)S(1)}, u32[]{:S(2)}, u32[]{:S(2)}) %collective-permute-start) | collective-permute-done | bytes 393248 | tf_op jit(solution)/shard_map/ppermute | solution.py:262
  14.4 2.7 %shard_map.85 = (bf16[256,512]{1,0:T(8,128)(2,1)S(1)}, bf16[256,1024]{1,0:T(8,128)(2,1)S(1)}, bf16[768,512]{1,0:T(8,128)(2,1)S(1)}, bf16[128,512]{1,0:T(8,128)(2...) custom-call(bf16[384,512]{1,0:T(8,128)(2,1)S(1)} %collective-permute-done.halo, ...), custom_call_target="tpu_custom_call" | custom-call | flops 2000000000 | bytes 10000000 | tf_op jit(solution)/shard_map/pallas_call | solution.py:214
  17.2 2.8 %collective-permute-start.1 = (bf16[256,512]{1,0:T(8,128)(2,1)S(1)}, bf16[256,512]{1,0:T(8,128)(2,1)S(1)}, u32[]{:S(2)}, u32[]{:S(2)}) collective-permute-start(bf16[256,512]{1,0:T(8,128)(2,1)S(1)} %get-tuple-element.72), channel_id=1, source_target_pairs={{1,0},{2,1},{3,2},{5,4},{6,5},{7,6},{9,8},{10,9},{11,10},{13,12},{... | collective-permute-start | bytes 786440 | tf_op jit(solution)/shard_map/ppermute | solution.py:262
  20.0 3.1 %shard_map.86 = (f32[256,512]{1,0:T(8,128)S(1)}, f32[256,512]{1,0:T(8,128)S(1)}, bf16[512,1024]{1,0:T(8,128)(2,1)S(1)}, bf16[512,512]{1,0:T(8,128)(2,1)S(1)}, bf16[512,512]{1,0:T(8,128)(2,1)}) custom-call(bf16[768,512]{1,0:T(8,128)(2,1)S(1)} %get-tuple-element.58.stream1.refs_0_, bf16[2,1024,1024]{2,1,0:T(8,128)(2,1)S(1)} %copy-done.1, ...), custom_call_target="tpu_custom_call" | custom-call | flops 5000000000 | bytes 10000000 | tf_op jit(solution)/shard_map/pallas_call | solution.py:214
  23.1 2.8 %shard_map.88 = (bf16[2,4,4,48,512]{4,3,2,1,0:T(8,128)(2,1)S(1)}, bf16[2,4,4,48,512]{4,3,2,1,0:T(8,128)(2,1)}) custom-call(s32[1]{0:T(128)} %bitcast.4.core, bf16[768,512]{1,0:T(8,128)(2,1)S(1)} %get-tuple-element.58.stream1.refs_0_, bf16[512,512]{1,0:T(8,128)(2,1)S(1)} %get-tuple-element.73.refs_1_, bf16[512,1024]{1,0:T(8,128)(2,1)S(1)} %get-tuple-element.74.refs_2_, ...), custom_call_target="tpu_custom_call" | custom-call | flops 5000000000 | bytes 6000000 | tf_op jit(solution)/shard_map/pallas_call | solution.py:214
  28.5 2.8 %shard_map.90 = (bf16[2,4,4,48,512]{4,3,2,1,0:T(8,128)(2,1)S(1)}, bf16[2,4,4,48,512]{4,3,2,1,0:T(8,128)(2,1)}) custom-call(s32[1]{0:T(128)} %bitcast.4.core, bf16[384,512]{1,0:T(8,128)(2,1)S(1)} %collective-permute-done.halo, bf16[512,512]{1,0:T(8,128)(2,1)S(1)} %bitcast.121, bf16[128,512]{1,0:T(8,128)(2,1)S(1)} %get-tuple-element.60.gated0_low.gated_low, ...), custom_call_target="tpu_custom_call" | custom-call | flops 5000000000 | bytes 6000000 | tf_op jit(solution)/shard_map/pallas_call | solution.py:214
  33.8 2.0 %collective-permute-start.7 = (bf16[2,4,48,512]{3,2,1,0:T(8,128)(2,1)S(1)}, bf16[2,4,48,512]{3,2,1,0:T(8,128)(2,1)S(1)}, u32[]{:S(2)}, u32[]{:S(2)}) collective-permute-start(bf16[2,4,48,512]{3,2,1,0:T(8,128)(2,1)S(1)} %fusion.7), channel_id=1, source_target_pairs={{0,224},{32,64},{64,32},{96,128},{128,96},{160,192},{192,160},{224... | collective-permute-start | bytes 1179656 | tf_op jit(solution)/shard_map/ppermute | solution.py:238
  35.9 4.1 %collective-permute-start.6 = (bf16[2,4,48,512]{3,2,1,0:T(8,128)(2,1)S(1)}, bf16[2,4,48,512]{3,2,1,0:T(8,128)(2,1)S(1)}, u32[]{:S(2)}, u32[]{:S(2)}) collective-permute-start(bf16[2,4,48,512]{3,2,1,0:T(8,128)(2,1)S(1)} %fusion.6), channel_id=1, source_target_pairs={{0,32},{32,0},{64,96},{96,64},{128,160},{160,128},{192,224},{224,1... | collective-permute-start | bytes 1179656 | tf_op jit(solution)/shard_map/ppermute | solution.py:238
  41.6 3.1 %collective-permute-start.4 = (bf16[2,4,48,512]{3,2,1,0:T(8,128)(2,1)S(1)}, bf16[2,4,48,512]{3,2,1,0:T(8,128)(2,1)S(1)}, u32[]{:S(2)}, u32[]{:S(2)}) collective-permute-start(bf16[2,4,48,512]{3,2,1,0:T(8,128)(2,1)S(1)} %fusion.5), channel_id=1, source_target_pairs={{0,24},{8,16},{16,8},{24,0},{1,25},{9,17},{17,9},{25,1},{2,26},{10... | collective-permute-start | bytes 1179656 | tf_op jit(solution)/shard_map/ppermute | solution.py:238
  45.3 3.8 %collective-permute-done.6 = bf16[2,4,48,512]{3,2,1,0:T(8,128)(2,1)S(1)} collective-permute-done((bf16[2,4,48,512]{3,2,1,0:T(8,128)(2,1)S(1)}, bf16[2,4,48,512]{3,2,1,0:T(8,128)(2,1)S(1)}, u32[]{:S(2)}, u32[]{:S(2)}) %collective-permute-start.6) | collective-permute-done | bytes 393248 | tf_op jit(solution)/shard_map/ppermute | solution.py:238
  49.2 4.2 %collective-permute-done.4 = bf16[2,4,48,512]{3,2,1,0:T(8,128)(2,1)S(1)} collective-permute-done((bf16[2,4,48,512]{3,2,1,0:T(8,128)(2,1)S(1)}, bf16[2,4,48,512]{3,2,1,0:T(8,128)(2,1)S(1)}, u32[]{:S(2)}, u32[]{:S(2)}) %collective-permute-start.4) | collective-permute-done | bytes 393248 | tf_op jit(solution)/shard_map/ppermute | solution.py:238
  55.3 2.4 %collective-permute-start.21 = (bf16[128,512]{1,0:T(8,128)(2,1)S(1)}, bf16[128,512]{1,0:T(8,128)(2,1)S(1)}, u32[]{:S(2)}, u32[]{:S(2)}) collective-permute-start(bf16[128,512]{1,0:T(8,128)(2,1)S(1)} %copy-done.13), channel_id=1, source_target_pairs={{1,0},{2,1},{3,2},{5,4},{6,5},{7,6},{9,8},{10,9},{11,10},{13,12},{... | collective-permute-start | bytes 393224 | tf_op jit(solution)/shard_map/ppermute | solution.py:262
  61.0 2.5 %collective-permute-done.11 = bf16[4,48,512]{2,1,0:T(8,128)(2,1)S(1)} collective-permute-done((bf16[4,48,512]{2,1,0:T(8,128)(2,1)S(1)}, bf16[4,48,512]{2,1,0:T(8,128)(2,1)S(1)}, u32[]{:S(2)}, u32[]{:S(2)}) %collective-permute-start.11) | collective-permute-done | bytes 196640 | tf_op jit(solution)/shard_map/ppermute | solution.py:228
  67.5 1.9 %collective-permute-start.12 = (bf16[2,2,48,512]{3,2,1,0:T(8,128)(2,1)S(1)}, bf16[2,2,48,512]{3,2,1,0:T(8,128)(2,1)S(1)}, u32[]{:S(2)}, u32[]{:S(2)}) collective-permute-start(bf16[2,2,48,512]{3,2,1,0:T(8,128)(2,1)S(1)} %fusion.19), channel_id=1, source_target_pairs={{0,32},{32,0},{64,96},{96,64},{128,160},{160,128},{192,224},{224,1... | collective-permute-start | bytes 589832 | tf_op jit(solution)/shard_map/ppermute | solution.py:228
  69.4 3.1 %collective-permute-done.13 = bf16[2,2,48,512]{3,2,1,0:T(8,128)(2,1)S(1)} collective-permute-done((bf16[2,2,48,512]{3,2,1,0:T(8,128)(2,1)S(1)}, bf16[2,2,48,512]{3,2,1,0:T(8,128)(2,1)S(1)}, u32[]{:S(2)}, u32[]{:S(2)}) %collective-permute-start.13) | collective-permute-done | bytes 196640 | tf_op jit(solution)/shard_map/ppermute | solution.py:228
  73.3 1.8 %collective-permute-start.15 = (bf16[2,48,512]{2,1,0:T(8,128)(2,1)S(1)}, bf16[2,48,512]{2,1,0:T(8,128)(2,1)S(1)}, u32[]{:S(2)}, u32[]{:S(2)}) collective-permute-start(bf16[2,48,512]{2,1,0:T(8,128)(2,1)S(1)} %dynamic-slice_bitcast_fusion.4), channel_id=1, source_target_pairs={{0,24},{8,16},{16,8},{24,0},{1,25},{9,17},{17,9},{25,1},{2,26},{10... | collective-permute-start | bytes 294920 | tf_op jit(solution)/shard_map/ppermute | solution.py:228
  76.2 3.2 %collective-permute-done.15 = bf16[2,48,512]{2,1,0:T(8,128)(2,1)S(1)} collective-permute-done((bf16[2,48,512]{2,1,0:T(8,128)(2,1)S(1)}, bf16[2,48,512]{2,1,0:T(8,128)(2,1)S(1)}, u32[]{:S(2)}, u32[]{:S(2)}) %collective-permute-start.15) | collective-permute-done | bytes 98336 | tf_op jit(solution)/shard_map/ppermute | solution.py:228
  80.0 5.3 %collective-permute-start.17 = (bf16[1,24,512]{2,1,0:T(8,128)(2,1)S(1)}, bf16[1,24,512]{2,1,0:T(8,128)(2,1)S(1)}, u32[]{:S(2)}, u32[]{:S(2)}) collective-permute-start(bf16[1,24,512]{2,1,0:T(8,128)(2,1)S(1)} %fusion.31), channel_id=1, source_target_pairs={{0,160},{32,128},{64,224},{96,192},{128,32},{160,0},{192,96},{224,... | collective-permute-start | bytes 73736 | tf_op jit(solution)/shard_map/ppermute | solution.py:228
  85.3 1.8 %collective-permute-start.16 = (bf16[3,24,512]{2,1,0:T(8,128)(2,1)S(1)}, bf16[3,24,512]{2,1,0:T(8,128)(2,1)S(1)}, u32[]{:S(2)}, u32[]{:S(2)}) collective-permute-start(bf16[3,24,512]{2,1,0:T(8,128)(2,1)S(1)} %fusion.26), channel_id=1, source_target_pairs={{0,96},{32,192},{64,160},{96,0},{128,224},{160,64},{192,32},{224,1... | collective-permute-start | bytes 221192 | tf_op jit(solution)/shard_map/ppermute | solution.py:228
  87.4 5.2 %collective-permute-done.16 = bf16[3,24,512]{2,1,0:T(8,128)(2,1)S(1)} collective-permute-done((bf16[3,24,512]{2,1,0:T(8,128)(2,1)S(1)}, bf16[3,24,512]{2,1,0:T(8,128)(2,1)S(1)}, u32[]{:S(2)}, u32[]{:S(2)}) %collective-permute-start.16) | collective-permute-done | bytes 73760 | tf_op jit(solution)/shard_map/ppermute | solution.py:228
  92.8 2.6 %collective-permute-start.19 = (bf16[4,24,512]{2,1,0:T(8,128)(2,1)S(1)}, bf16[4,24,512]{2,1,0:T(8,128)(2,1)S(1)}, u32[]{:S(2)}, u32[]{:S(2)}) collective-permute-start(bf16[4,24,512]{2,1,0:T(8,128)(2,1)S(1)} %pad_maximum_fusion.1.own), channel_id=1, source_target_pairs={{0,1},{1,2},{2,3},{3,0},{4,5},{5,6},{6,7},{7,4},{8,9},{9,10},{10,1... | collective-permute-start | bytes 294920 | tf_op jit(solution)/shard_map/ppermute | solution.py:257
  96.3 2.6 %collective-permute-done.18.opposite = bf16[4,24,512]{2,1,0:T(8,128)(2,1)S(1)} collective-permute-done((bf16[4,24,512]{2,1,0:T(8,128)(2,1)S(1)}, bf16[4,24,512]{2,1,0:T(8,128)(2,1)S(1)}, u32[]{:S(2)}, u32[]{:S(2)}) %collective-permute-start.18) | collective-permute-done | bytes 98336 | tf_op jit(solution)/shard_map/ppermute | solution.py:257
  98.9 2.3 %collective-permute-done.20.two = bf16[4,24,512]{2,1,0:T(8,128)(2,1)S(1)} collective-permute-done((bf16[4,24,512]{2,1,0:T(8,128)(2,1)S(1)}, bf16[4,24,512]{2,1,0:T(8,128)(2,1)S(1)}, u32[]{:S(2)}, u32[]{:S(2)}) %collective-permute-start.20) | collective-permute-done | bytes 98336 | tf_op jit(solution)/shard_map/ppermute | solution.py:257
  (98 shorter events, 27.3 us)
Async XLA Ops:
  1.7 12.7 %collective-permute-start = (bf16[384,512]{1,0:T(8,128)(2,1)S(1)}, bf16[384,512]{1,0:T(8,128)(2,1)S(1)}, u32[]{:S(2)}, u32[]{:S(2)}) collective-permute-start(bf16[384,512]{1,0:T(8,128)(2,1)S(1)} %slice_bitcast_fusion), channel_id=1, source_target_pairs={{0,1},{1,2},{2,3},{4,5},{5,6},{6,7},{8,9},{9,10},{10,11},{12,13},{... | collective-permute-start | bytes 1179656 | tf_op jit(solution)/shard_map/ppermute | solution.py:262
  17.2 10.2 %collective-permute-start.1 = (bf16[256,512]{1,0:T(8,128)(2,1)S(1)}, bf16[256,512]{1,0:T(8,128)(2,1)S(1)}, u32[]{:S(2)}, u32[]{:S(2)}) collective-permute-start(bf16[256,512]{1,0:T(8,128)(2,1)S(1)} %get-tuple-element.72), channel_id=1, source_target_pairs={{1,0},{2,1},{3,2},{5,4},{6,5},{7,6},{9,8},{10,9},{11,10},{13,12},{... | collective-permute-start | bytes 786440 | tf_op jit(solution)/shard_map/ppermute | solution.py:262
  25.9 6.2 %collective-permute-start.5 = (bf16[2,4,4,48,512]{4,3,2,1,0:T(8,128)(2,1)}, bf16[2,4,4,48,512]{4,3,2,1,0:T(8,128)(2,1)}, u32[]{:S(2)}, u32[]{:S(2)}) collective-permute-start(bf16[2,4,4,48,512]{4,3,2,1,0:T(8,128)(2,1)} %get-tuple-element.85), channel_id=1, source_target_pairs={{0,4},{4,0},{1,5},{5,1},{2,6},{6,2},{3,7},{7,3},{8,12},{12,8},{9,1... | collective-permute-start | bytes 4718600 | tf_op jit(solution)/shard_map/ppermute | solution.py:347
  31.4 8.6 %collective-permute-start.2 = (bf16[2,4,4,48,512]{4,3,2,1,0:T(8,128)(2,1)}, bf16[2,4,4,48,512]{4,3,2,1,0:T(8,128)(2,1)}, u32[]{:S(2)}, u32[]{:S(2)}) collective-permute-start(bf16[2,4,4,48,512]{4,3,2,1,0:T(8,128)(2,1)} %get-tuple-element.83), channel_id=1, source_target_pairs={{0,4},{4,0},{1,5},{5,1},{2,6},{6,2},{3,7},{7,3},{8,12},{12,8},{9,1... | collective-permute-start | bytes 4718600 | tf_op jit(solution)/shard_map/ppermute | solution.py:361
  33.8 11.3 %collective-permute-start.7 = (bf16[2,4,48,512]{3,2,1,0:T(8,128)(2,1)S(1)}, bf16[2,4,48,512]{3,2,1,0:T(8,128)(2,1)S(1)}, u32[]{:S(2)}, u32[]{:S(2)}) collective-permute-start(bf16[2,4,48,512]{3,2,1,0:T(8,128)(2,1)S(1)} %fusion.7), channel_id=1, source_target_pairs={{0,224},{32,64},{64,32},{96,128},{128,96},{160,192},{192,160},{224... | collective-permute-start | bytes 1179656 | tf_op jit(solution)/shard_map/ppermute | solution.py:238
  35.9 13.2 %collective-permute-start.6 = (bf16[2,4,48,512]{3,2,1,0:T(8,128)(2,1)S(1)}, bf16[2,4,48,512]{3,2,1,0:T(8,128)(2,1)S(1)}, u32[]{:S(2)}, u32[]{:S(2)}) collective-permute-start(bf16[2,4,48,512]{3,2,1,0:T(8,128)(2,1)S(1)} %fusion.6), channel_id=1, source_target_pairs={{0,32},{32,0},{64,96},{96,64},{128,160},{160,128},{192,224},{224,1... | collective-permute-start | bytes 1179656 | tf_op jit(solution)/shard_map/ppermute | solution.py:238
  41.6 11.9 %collective-permute-start.4 = (bf16[2,4,48,512]{3,2,1,0:T(8,128)(2,1)S(1)}, bf16[2,4,48,512]{3,2,1,0:T(8,128)(2,1)S(1)}, u32[]{:S(2)}, u32[]{:S(2)}) collective-permute-start(bf16[2,4,48,512]{3,2,1,0:T(8,128)(2,1)S(1)} %fusion.5), channel_id=1, source_target_pairs={{0,24},{8,16},{16,8},{24,0},{1,25},{9,17},{17,9},{25,1},{2,26},{10... | collective-permute-start | bytes 1179656 | tf_op jit(solution)/shard_map/ppermute | solution.py:238
  44.8 10.3 %collective-permute-start.3 = (bf16[2,4,48,512]{3,2,1,0:T(8,128)(2,1)S(1)}, bf16[2,4,48,512]{3,2,1,0:T(8,128)(2,1)S(1)}, u32[]{:S(2)}, u32[]{:S(2)}) collective-permute-start(bf16[2,4,48,512]{3,2,1,0:T(8,128)(2,1)S(1)} %fusion.4), channel_id=1, source_target_pairs={{0,8},{8,0},{16,24},{24,16},{1,9},{9,1},{17,25},{25,17},{2,10},{10... | collective-permute-start | bytes 1179656 | tf_op jit(solution)/shard_map/ppermute | solution.py:238
  55.3 12.1 %collective-permute-start.21 = (bf16[128,512]{1,0:T(8,128)(2,1)S(1)}, bf16[128,512]{1,0:T(8,128)(2,1)S(1)}, u32[]{:S(2)}, u32[]{:S(2)}) collective-permute-start(bf16[128,512]{1,0:T(8,128)(2,1)S(1)} %copy-done.13), channel_id=1, source_target_pairs={{1,0},{2,1},{3,2},{5,4},{6,5},{7,6},{9,8},{10,9},{11,10},{13,12},{... | collective-permute-start | bytes 393224 | tf_op jit(solution)/shard_map/ppermute | solution.py:262
  57.8 5.8 %collective-permute-start.11 = (bf16[4,48,512]{2,1,0:T(8,128)(2,1)S(1)}, bf16[4,48,512]{2,1,0:T(8,128)(2,1)S(1)}, u32[]{:S(2)}, u32[]{:S(2)}) collective-permute-start(bf16[4,48,512]{2,1,0:T(8,128)(2,1)S(1)} %dynamic-slice_bitcast_fusion), channel_id=1, source_target_pairs={{0,32},{32,0},{64,96},{96,64},{128,160},{160,128},{192,224},{224,1... | collective-permute-start | bytes 589832 | tf_op jit(solution)/shard_map/ppermute | solution.py:228
  58.2 5.8 %collective-permute-start.10 = (bf16[4,48,512]{2,1,0:T(8,128)(2,1)S(1)}, bf16[4,48,512]{2,1,0:T(8,128)(2,1)S(1)}, u32[]{:S(2)}, u32[]{:S(2)}) collective-permute-start(bf16[4,48,512]{2,1,0:T(8,128)(2,1)S(1)} %dynamic-slice_bitcast_fusion.1), channel_id=1, source_target_pairs={{0,224},{32,64},{64,32},{96,128},{128,96},{160,192},{192,160},{224... | collective-permute-start | bytes 589832 | tf_op jit(solution)/shard_map/ppermute | solution.py:228
  59.3 5.8 %collective-permute-start.9 = (bf16[4,48,512]{2,1,0:T(8,128)(2,1)S(1)}, bf16[4,48,512]{2,1,0:T(8,128)(2,1)S(1)}, u32[]{:S(2)}, u32[]{:S(2)}) collective-permute-start(bf16[4,48,512]{2,1,0:T(8,128)(2,1)S(1)} %dynamic-slice_bitcast_fusion.2), channel_id=1, source_target_pairs={{0,8},{8,0},{16,24},{24,16},{1,9},{9,1},{17,25},{25,17},{2,10},{10... | collective-permute-start | bytes 589832 | tf_op jit(solution)/shard_map/ppermute | solution.py:228
  59.7 7.7 %copy-start.11 = (f32[128,512]{1,0:T(8,128)S(1)}, f32[128,512]{1,0:T(8,128)}, u32[]{:S(2)}) copy-start(f32[128,512]{1,0:T(8,128)} %copy-done.10) | copy-start | bytes 786436
  59.7 7.0 %collective-permute-start.8 = (bf16[4,48,512]{2,1,0:T(8,128)(2,1)S(1)}, bf16[4,48,512]{2,1,0:T(8,128)(2,1)S(1)}, u32[]{:S(2)}, u32[]{:S(2)}) collective-permute-start(bf16[4,48,512]{2,1,0:T(8,128)(2,1)S(1)} %dynamic-slice_bitcast_fusion.3), channel_id=1, source_target_pairs={{0,24},{8,16},{16,8},{24,0},{1,25},{9,17},{17,9},{25,1},{2,26},{10... | collective-permute-start | bytes 589832 | tf_op jit(solution)/shard_map/ppermute | solution.py:228
  66.8 5.8 %collective-permute-start.13 = (bf16[2,2,48,512]{3,2,1,0:T(8,128)(2,1)S(1)}, bf16[2,2,48,512]{3,2,1,0:T(8,128)(2,1)S(1)}, u32[]{:S(2)}, u32[]{:S(2)}) collective-permute-start(bf16[2,2,48,512]{3,2,1,0:T(8,128)(2,1)S(1)} %fusion.15), channel_id=1, source_target_pairs={{0,8},{8,0},{16,24},{24,16},{1,9},{9,1},{17,25},{25,17},{2,10},{10... | collective-permute-start | bytes 589832 | tf_op jit(solution)/shard_map/ppermute | solution.py:228
  67.5 5.8 %collective-permute-start.12 = (bf16[2,2,48,512]{3,2,1,0:T(8,128)(2,1)S(1)}, bf16[2,2,48,512]{3,2,1,0:T(8,128)(2,1)S(1)}, u32[]{:S(2)}, u32[]{:S(2)}) collective-permute-start(bf16[2,2,48,512]{3,2,1,0:T(8,128)(2,1)S(1)} %fusion.19), channel_id=1, source_target_pairs={{0,32},{32,0},{64,96},{96,64},{128,160},{160,128},{192,224},{224,1... | collective-permute-start | bytes 589832 | tf_op jit(solution)/shard_map/ppermute | solution.py:228
  73.3 22.1 %copy-start.9 = (bf16[384,512]{1,0:T(8,128)(2,1)S(1)}, bf16[384,512]{1,0:T(8,128)(2,1)}, u32[]{:S(2)}) copy-start(bf16[384,512]{1,0:T(8,128)(2,1)} %copy-done.8) | copy-start | bytes 1179652
  73.3 6.1 %collective-permute-start.15 = (bf16[2,48,512]{2,1,0:T(8,128)(2,1)S(1)}, bf16[2,48,512]{2,1,0:T(8,128)(2,1)S(1)}, u32[]{:S(2)}, u32[]{:S(2)}) collective-permute-start(bf16[2,48,512]{2,1,0:T(8,128)(2,1)S(1)} %dynamic-slice_bitcast_fusion.4), channel_id=1, source_target_pairs={{0,24},{8,16},{16,8},{24,0},{1,25},{9,17},{17,9},{25,1},{2,26},{10... | collective-permute-start | bytes 294920 | tf_op jit(solution)/shard_map/ppermute | solution.py:228
  75.1 4.7 %collective-permute-start.14 = (bf16[2,48,512]{2,1,0:T(8,128)(2,1)S(1)}, bf16[2,48,512]{2,1,0:T(8,128)(2,1)S(1)}, u32[]{:S(2)}, u32[]{:S(2)}) collective-permute-start(bf16[2,48,512]{2,1,0:T(8,128)(2,1)S(1)} %dynamic-slice_bitcast_fusion.5), channel_id=1, source_target_pairs={{0,224},{32,64},{64,32},{96,128},{128,96},{160,192},{192,160},{224... | collective-permute-start | bytes 294920 | tf_op jit(solution)/shard_map/ppermute | solution.py:228
  80.0 7.5 %collective-permute-start.17 = (bf16[1,24,512]{2,1,0:T(8,128)(2,1)S(1)}, bf16[1,24,512]{2,1,0:T(8,128)(2,1)S(1)}, u32[]{:S(2)}, u32[]{:S(2)}) collective-permute-start(bf16[1,24,512]{2,1,0:T(8,128)(2,1)S(1)} %fusion.31), channel_id=1, source_target_pairs={{0,160},{32,128},{64,224},{96,192},{128,32},{160,0},{192,96},{224,... | collective-permute-start | bytes 73736 | tf_op jit(solution)/shard_map/ppermute | solution.py:228
  85.3 7.4 %collective-permute-start.16 = (bf16[3,24,512]{2,1,0:T(8,128)(2,1)S(1)}, bf16[3,24,512]{2,1,0:T(8,128)(2,1)S(1)}, u32[]{:S(2)}, u32[]{:S(2)}) collective-permute-start(bf16[3,24,512]{2,1,0:T(8,128)(2,1)S(1)} %fusion.26), channel_id=1, source_target_pairs={{0,96},{32,192},{64,160},{96,0},{128,224},{160,64},{192,32},{224,1... | collective-permute-start | bytes 221192 | tf_op jit(solution)/shard_map/ppermute | solution.py:228
  92.7 6.2 %collective-permute-start.18 = (bf16[4,24,512]{2,1,0:T(8,128)(2,1)S(1)}, bf16[4,24,512]{2,1,0:T(8,128)(2,1)S(1)}, u32[]{:S(2)}, u32[]{:S(2)}) collective-permute-start(bf16[4,24,512]{2,1,0:T(8,128)(2,1)S(1)} %pad_maximum_fusion.1.own), channel_id=1, source_target_pairs={{0,2},{1,3},{2,0},{3,1},{4,6},{5,7},{6,4},{7,5},{8,10},{9,11},{10,... | collective-permute-start | bytes 294920 | tf_op jit(solution)/shard_map/ppermute | solution.py:257
  92.8 6.1 %collective-permute-start.19 = (bf16[4,24,512]{2,1,0:T(8,128)(2,1)S(1)}, bf16[4,24,512]{2,1,0:T(8,128)(2,1)S(1)}, u32[]{:S(2)}, u32[]{:S(2)}) collective-permute-start(bf16[4,24,512]{2,1,0:T(8,128)(2,1)S(1)} %pad_maximum_fusion.1.own), channel_id=1, source_target_pairs={{0,1},{1,2},{2,3},{3,0},{4,5},{5,6},{6,7},{7,4},{8,9},{9,10},{10,1... | collective-permute-start | bytes 294920 | tf_op jit(solution)/shard_map/ppermute | solution.py:257
  95.4 5.8 %collective-permute-start.20 = (bf16[4,24,512]{2,1,0:T(8,128)(2,1)S(1)}, bf16[4,24,512]{2,1,0:T(8,128)(2,1)S(1)}, u32[]{:S(2)}, u32[]{:S(2)}) collective-permute-start(bf16[4,24,512]{2,1,0:T(8,128)(2,1)S(1)} %pad_maximum_fusion.1.own), channel_id=1, source_target_pairs={{0,3},{1,0},{2,1},{3,2},{4,7},{5,4},{6,5},{7,6},{8,11},{9,8},{10,9... | collective-permute-start | bytes 294920 | tf_op jit(solution)/shard_map/ppermute | solution.py:257
  (12 other events, 43.2 us)
